TPU v7x, 512 devices: a whole 4x8x8 slice. The times are simulated.
512 devices in a mesh: grp: 8 (over z_lo, x), ep: 64 (over z_hi, y, core).
Axes of the slice: x: 4, y: 8, z: 8 (z_hi: 4, z_lo: 2; z = z_hi * 2 + z_lo), core: 2. Of those that a mesh axis runs over, the one named last changes fastest.
Arguments:
- latent_cache: bfloat16 [8, 64, 4, 64, 576], P('grp', 'ep'), may hold values from -6 to 6
- page_table: int32 [8, 64, 2, 2], P('grp', 'ep'), may hold values from 0 to 3, as said below
- lengths: int32 [8, 64, 2], P('grp', 'ep'), may hold values from 1 to 128, as said below
- move_to: int32 [8, 64, 2], P('grp', 'ep'), may hold values from 0 to 2, as said below
- query: bfloat16 [8, 64, 2, 64, 576], P('grp', 'ep'), may hold values from -110 to 110
- hidden: bfloat16 [8, 64, 2, 3584], P('grp', 'ep'), may hold values from -6 to 6
- norm_gain: float32 [3584], replicated, may hold values from 0.1 to 1.9
- expert_ids: int32 [8, 64, 4, 6], P('grp', 'ep'), may hold values from 0 to 7, all different within a row; in each aligned block of 4 rows (0 to 3, 4 to 7, ..., all dimensions but the last counted through in order) at most 4 rows name the same one
- expert_gates: float32 [8, 64, 4, 6], P('grp', 'ep'), may hold values from 0.05 to 1
- gate_weight: bfloat16 [64, 3584, 128], P('ep'), may hold values from -0.09375 to 0.09375
- up_weight: bfloat16 [64, 3584, 128], P('ep'), may hold values from -0.09375 to 0.09375
- down_weight: bfloat16 [64, 128, 3584], P('ep'), may hold values from -0.1875 to 0.1875
Outputs:
- attn_out: bfloat16 [8, 64, 4, 64, 512], P('grp', 'ep')
- moe_out: bfloat16 [8, 64, 4, 3584], P('grp', 'ep')
Inputs may be any that keep to these rules, and one draw needn't show every extreme that they name: `page_table`: each device's table holds each of its 4 pages once. `lengths`: some request has exactly 128 tokens. `move_to`: on one device each of the values 1 and 2 is named by at most one request. `expert_ids`: among the rows of one device no expert is named by more than 4 rows.
All inputs are finite; a program needn't handle non-finite values.
Results may differ from a plain program's by a relative error of at most 0.014.
Values may be sent and summed in bfloat16 or wider, within the bound.
No kernel may reach another device: no remote copies, remote signals or barrier semaphores. Data moves between devices by JAX's collectives and lax.ppermute only.
A program may use at most 64 MiB of HBM per device.

v0:
```python
import jax
import jax.numpy as jnp
from jax import lax
from jax.sharding import PartitionSpec as P

VDIM = 512
QK_DIM = 192
SLICES = 8


def passed_along(shard, axis, by):
    length = lax.axis_size(axis)
    return lax.ppermute(shard, axis, [(i, (i + by) % length) for i in range(length)])


def select_rows(picker, values):
    taken = lax.dot_general(
        picker, values, (((1,), (0,)), ((), ())), preferred_element_type=jnp.float32
    )
    return taken.astype(jnp.bfloat16)


def attend_rows(questions, keys, lens):
    scores = jnp.einsum(
        "rhl,rtl->rht", questions, keys, preferred_element_type=jnp.float32
    ) * QK_DIM ** (-0.5)
    live = jnp.arange(keys.shape[1], dtype=jnp.int32)[None, None, :] < lens[:, None, None]
    scores = jnp.where(live, scores, jnp.float32(-1e30))
    top = jnp.max(scores, axis=2, keepdims=True)
    expo = jnp.exp(scores - top)
    probs = (expo / jnp.sum(expo, axis=2, keepdims=True)).astype(jnp.bfloat16)
    return jnp.einsum("rht,rtv->rhv", probs, keys[:, :, :VDIM], preferred_element_type=jnp.float32)


def body(
    latent_cache,
    page_table,
    lengths,
    move_to,
    query,
    hidden,
    norm_gain,
    expert_ids,
    expert_gates,
    gate_weight,
    up_weight,
    down_weight,
):
    pool = latent_cache[0, 0]
    table = page_table[0, 0]
    requests = table.shape[0]
    keys = pool[table.reshape(-1)].reshape(requests, table.shape[1] * pool.shape[1], pool.shape[2])
    moves = move_to[0, 0]
    own_lens = lengths[0, 0]
    questions = query[0, 0]
    own_rows = hidden[0, 0]
    forward = (moves == 1).astype(jnp.bfloat16)[None, :]
    backward = (moves == 2).astype(jnp.bfloat16)[None, :]
    stays = moves == 0
    lens_wide = own_lens.astype(jnp.bfloat16)[:, None]
    send_next = (
        select_rows(forward, keys),
        select_rows(forward, questions),
        select_rows(forward, own_rows),
        select_rows(forward, lens_wide),
    )
    send_prev = (
        select_rows(backward, keys),
        select_rows(backward, questions),
        select_rows(backward, own_rows),
        select_rows(backward, lens_wide),
    )
    prev_keys, prev_questions, prev_rows, prev_lens = passed_along(
        (send_next[0], send_next[1], send_next[2], send_next[3]), "grp", 1
    )
    next_keys, next_questions, next_rows, next_lens = passed_along(
        (send_prev[0], send_prev[1], send_prev[2], send_prev[3]), "grp", -1
    )
    all_keys = jnp.concatenate([keys, prev_keys, next_keys], axis=0)
    all_questions = jnp.concatenate([questions, prev_questions, next_questions], axis=0)
    all_lens = jnp.concatenate(
        [
            jnp.where(stays, own_lens, 0),
            prev_lens[:, 0].astype(jnp.int32),
            next_lens[:, 0].astype(jnp.int32),
        ],
        axis=0,
    )
    result = attend_rows(all_questions, all_keys, all_lens)
    attn = jnp.where((all_lens > 0)[:, None, None], result, 0.0).astype(jnp.bfloat16)
    served = jnp.concatenate(
        [jnp.where(stays[:, None], own_rows, jnp.zeros_like(own_rows)), prev_rows, next_rows],
        axis=0,
    )
    wide = served.astype(jnp.float32)
    normed = (
        wide * lax.rsqrt(jnp.mean(wide * wide, axis=-1, keepdims=True) + 1e-06) * norm_gain
    ).astype(jnp.bfloat16)
    ids = expert_ids[0, 0]
    gates = expert_gates[0, 0]
    rows_served = ids.shape[0]
    choose_count = ids.shape[1]
    experts_here = lax.axis_size("ep") // SLICES
    capacity = min(rows_served, (rows_served * choose_count + experts_here - 1) // experts_here + 2)
    onehot = (ids[:, :, None] == jnp.arange(experts_here, dtype=jnp.int32)).astype(jnp.float32)
    chosen = jnp.sum(onehot, axis=1)
    slot = jnp.cumsum(chosen, axis=0) - chosen
    place = chosen[:, :, None] * (
        slot[:, :, None] == jnp.arange(capacity, dtype=jnp.float32)
    ).astype(jnp.float32)
    buffers = jnp.einsum(
        "sxc,sd->xcd", place.astype(jnp.bfloat16), normed, preferred_element_type=jnp.float32
    ).astype(jnp.bfloat16)
    outgoing = jnp.repeat(buffers, SLICES, axis=0)
    w_gate = gate_weight[0]
    w_up = up_weight[0]
    w_down = down_weight[0]
    received = lax.all_to_all(outgoing, "ep", split_axis=0, concat_axis=0, tiled=True)
    gate = jnp.einsum("skd,df->skf", received, w_gate, preferred_element_type=jnp.float32)
    upper = jnp.einsum("skd,df->skf", received, w_up, preferred_element_type=jnp.float32)
    act = (jax.nn.silu(gate) * upper).astype(jnp.bfloat16)
    part = jnp.einsum("skf,fd->skd", act, w_down, preferred_element_type=jnp.float32).astype(
        jnp.bfloat16
    )
    returned = lax.all_to_all(part, "ep", split_axis=0, concat_axis=0, tiled=True)
    summed = jnp.sum(
        returned.reshape(experts_here, SLICES, capacity, returned.shape[2]).astype(jnp.float32),
        axis=1,
    )
    mix = jnp.einsum("sk,skx->sx", gates, onehot)
    weights = mix[:, :, None] * place
    moe = jnp.einsum("sxc,xcd->sd", weights, summed).astype(jnp.bfloat16)
    return (attn[None, None], moe[None, None])


def solution(mesh):
    in_specs = (
        P("grp", "ep", None, None, None),
        P("grp", "ep", None, None),
        P("grp", "ep", None),
        P("grp", "ep", None),
        P("grp", "ep", None, None, None),
        P("grp", "ep", None, None),
        P(),
        P("grp", "ep", None, None),
        P("grp", "ep", None, None),
        P("ep", None, None),
        P("ep", None, None),
        P("ep", None, None),
    )
    out_specs = (P("grp", "ep", None, None, None), P("grp", "ep", None, None))
    return jax.shard_map(body, mesh=mesh, in_specs=in_specs, out_specs=out_specs, check_vma=False)
```

profile of v0, /device:TPU:8, one launch (start us, length us, event | category | flops | bytes accessed | tf_op | source)
XLA Modules:
  0.0 156.7 jit_solution(11358406382889091063)
XLA Ops:
  0.6 1.0 convolution_reduce_fusion
  1.6 6.5 %collective-permute-start.7 = (bf16[1,3584]{1,0:T(2,128)(2,1)S(1)}, bf16[1,3584]{1,0:T(2,128)(2,1)S(1)}, u32[]{:S(2)}, u32[]{:S(2)}) collective-permute-start(bf16[1,3584]{1,0:T(2,128)(2,1)S(1)} %convert_element_type.134), channel_id=1, source_target_pairs={{0,448},{64,0},{128,64},{192,128},{256,192},{320,256},{384,320},{4... | collective-permute-start | bytes 21512 | tf_op jit(solution)/shard_map/ppermute | solution.py:13
  8.1 0.9 convolution_reduce_fusion.1
  9.0 1.9 %collective-permute-start.6 = (bf16[1,3584]{1,0:T(2,128)(2,1)S(1)}, bf16[1,3584]{1,0:T(2,128)(2,1)S(1)}, u32[]{:S(2)}, u32[]{:S(2)}) collective-permute-start(bf16[1,3584]{1,0:T(2,128)(2,1)S(1)} %convert_element_type.132), channel_id=1, source_target_pairs={{0,64},{64,128},{128,192},{192,256},{256,320},{320,384},{384,448},... | collective-permute-start | bytes 21512 | tf_op jit(solution)/shard_map/ppermute | solution.py:13
  11.0 0.7 compare_bitcast_fusion
  11.6 0.8 copy.32
  12.4 0.8 broadcast_select_fusion
  13.3 3.4 %collective-permute-done.6 = bf16[1,3584]{1,0:T(2,128)(2,1)S(1)} collective-permute-done((bf16[1,3584]{1,0:T(2,128)(2,1)S(1)}, bf16[1,3584]{1,0:T(2,128)(2,1)S(1)}, u32[]{:S(2)}, u32[]{:S(2)}) %collective-permute-start.6) | collective-permute-done | bytes 7200 | tf_op jit(solution)/shard_map/ppermute | solution.py:13
  16.9 1.0 convolution_convert_fusion.1
  18.6 60.9 %all_to_all.10 = bf16[64,4,3584]{2,1,0:T(4,128)(2,1)S(1)} all-to-all(bf16[64,4,3584]{2,1,0:T(4,128)(2,1)S(1)} %bitcast.119), channel_id=1, replica_groups=mesh['grp'=8,'ep'=64] {'ep'}, dimensions={0} | all-to-all | bytes 3670016 | tf_op jit(solution)/shard_map/all_to_all | solution.py:118
  79.4 0.6 fusion.5
  80.1 3.6 %convolution_convert_fusion = bf16[64,4,3584]{2,0,1:T(8,128)(2,1)} fusion(bf16[64,4,3584]{2,1,0:T(4,128)(2,1)S(1)} %all_to_all.10, bf16[1,128,3584]{2,1,0:T(8,128)(2,1)S(1)} %copy-done, bf16[1,3584,128]{2,1,0:T(8,128)(2,1)} %param.22, f32[64,4,128]{2,0,1:T(8,128)S(1)} %fusion.5), kind=kOutput, calls=%fused_computation.2 | convolution fusion | flops 470876160 | bytes 5636096 | tf_op jit(solution)/shard_map/skf,fd->skd/dot_general | solution.py:122
  83.7 4.2 %copy.36 = bf16[64,4,3584]{2,1,0:T(4,128)(2,1)} copy(bf16[64,4,3584]{2,0,1:T(8,128)(2,1)} %convolution_convert_fusion) | data formatting | bytes 3670016 | tf_op jit(solution)/shard_map/convert_element_type | solution.py:122
  87.9 11.4 %all-to-all-start.1 = ((bf16[64,4,3584]{2,1,0:T(4,128)(2,1)}), bf16[64,4,3584]{2,1,0:T(4,128)(2,1)S(1)}, u32[]{:S(2)}, u32[]{:S(2)}) async-start(bf16[64,4,3584]{2,1,0:T(4,128)(2,1)} %copy.36), calls=%async_computation.1 | async-start | bytes 3670016 | tf_op jit(solution)/shard_map/all_to_all | solution.py:125
  99.9 1.9 %collective-permute-start = (bf16[1,1]{1,0:T(2,128)(2,1)}, bf16[1,1]{1,0:T(2,128)(2,1)}, u32[]{:S(2)}, u32[]{:S(2)}) collective-permute-start(bf16[1,1]{1,0:T(2,128)(2,1)} %bitcast.4), channel_id=1, source_target_pairs={{0,64},{64,128},{128,192},{192,256},{256,320},{320,384},{384,448},... | collective-permute-start | bytes 14 | tf_op jit(solution)/shard_map/ppermute | solution.py:13
  101.8 6.0 %collective-permute-start.1 = (bf16[1,1]{1,0:T(2,128)(2,1)}, bf16[1,1]{1,0:T(2,128)(2,1)}, u32[]{:S(2)}, u32[]{:S(2)}) collective-permute-start(bf16[1,1]{1,0:T(2,128)(2,1)} %bitcast.7), channel_id=1, source_target_pairs={{0,448},{64,0},{128,64},{192,128},{256,192},{320,256},{384,320},{4... | collective-permute-start | bytes 14 | tf_op jit(solution)/shard_map/ppermute | solution.py:13
  108.2 0.6 copy.82
  108.8 1.9 %collective-permute-start.3 = (bf16[1,64,576]{2,1,0:T(8,128)(2,1)}, bf16[1,64,576]{2,1,0:T(8,128)(2,1)}, u32[]{:S(2)}, u32[]{:S(2)}) collective-permute-start(bf16[1,64,576]{2,1,0:T(8,128)(2,1)} %bitcast.117), channel_id=1, source_target_pairs={{0,448},{64,0},{128,64},{192,128},{256,192},{320,256},{384,320},{4... | collective-permute-start | bytes 221192 | tf_op jit(solution)/shard_map/ppermute | solution.py:13
  111.1 0.6 copy.81
  111.7 3.9 %collective-permute-start.2 = (bf16[1,64,576]{2,1,0:T(8,128)(2,1)}, bf16[1,64,576]{2,1,0:T(8,128)(2,1)}, u32[]{:S(2)}, u32[]{:S(2)}) collective-permute-start(bf16[1,64,576]{2,1,0:T(8,128)(2,1)} %bitcast.115), channel_id=1, source_target_pairs={{0,64},{64,128},{128,192},{192,256},{256,320},{320,384},{384,448},... | collective-permute-start | bytes 221192 | tf_op jit(solution)/shard_map/ppermute | solution.py:13
  115.7 0.6 gather_fusion
  116.6 0.8 copy.52
  117.4 4.0 %collective-permute-start.5 = (bf16[1,128,576]{1,2,0:T(8,128)(2,1)}, bf16[1,128,576]{1,2,0:T(8,128)(2,1)}, u32[]{:S(2)}, u32[]{:S(2)}) collective-permute-start(bf16[1,128,576]{1,2,0:T(8,128)(2,1)} %bitcast.111), channel_id=1, source_target_pairs={{0,448},{64,0},{128,64},{192,128},{256,192},{320,256},{384,320},{4... | collective-permute-start | bytes 442376 | tf_op jit(solution)/shard_map/ppermute | solution.py:13
  121.8 0.7 bitcast_select_fusion.2
  122.4 0.8 fusion.62
  123.2 19.2 %collective-permute-done = bf16[1,1]{1,0:T(2,128)(2,1)} collective-permute-done((bf16[1,1]{1,0:T(2,128)(2,1)}, bf16[1,1]{1,0:T(2,128)(2,1)}, u32[]{:S(2)}, u32[]{:S(2)}) %collective-permute-start) | collective-permute-done | bytes 34 | tf_op jit(solution)/shard_map/ppermute | solution.py:13
  142.4 1.9 %collective-permute-start.4 = (bf16[1,128,576]{1,2,0:T(8,128)(2,1)S(1)}, bf16[1,128,576]{1,2,0:T(8,128)(2,1)S(1)}, u32[]{:S(2)}, u32[]{:S(2)}) collective-permute-start(bf16[1,128,576]{1,2,0:T(8,128)(2,1)S(1)} %bitcast.123), channel_id=1, source_target_pairs={{0,64},{64,128},{128,192},{192,256},{256,320},{320,384},{384,448},... | collective-permute-start | bytes 442376 | tf_op jit(solution)/shard_map/ppermute | solution.py:13
  145.8 5.8 %collective-permute-done.4 = bf16[1,128,576]{1,2,0:T(8,128)(2,1)S(1)} collective-permute-done((bf16[1,128,576]{1,2,0:T(8,128)(2,1)S(1)}, bf16[1,128,576]{1,2,0:T(8,128)(2,1)S(1)}, u32[]{:S(2)}, u32[]{:S(2)}) %collective-permute-start.4) | collective-permute-done | bytes 147488 | tf_op jit(solution)/shard_map/ppermute | solution.py:13
  151.6 1.5 fusion.98
  153.1 2.0 %fusion.8 = bf16[1,1,4,64,512]{4,3,2,1,0:T(8,128)(2,1)} fusion(bf16[1,128,576]{1,2,0:T(8,128)(2,1)} %collective-permute-done.5, bf16[1,128,576]{1,2,0:T(8,128)(2,1)S(1)} %collective-permute-done.4, bf16[2,128,576]{1,2,0:T(8,128)(2,1)S(1)} %copy.30, pred[4]{0:T(512)(128)(4,1)S(1)} %get-tuple-element.8, f32[4,64,128]{2,1,0:T(8,128)S(1)} %get-tuple-element.14, ...), kind=kOutput, calls=%fused_computation.14 | convolution fusion | flops 35454976 | bytes 984068 | tf_op jit(solution)/shard_map/rht,rtv->rhv/dot_general | solution.py:32
  155.0 0.8 convert_reduce_fusion
  155.8 0.8 fusion.2
  (40 shorter events, 3.1 us)
Async XLA Ops:
  0.6 79.4 %copy-start = (bf16[1,128,3584]{2,1,0:T(8,128)(2,1)S(1)}, bf16[1,128,3584]{2,1,0:T(8,128)(2,1)}, u32[]{:S(2)}) copy-start(bf16[1,128,3584]{2,1,0:T(8,128)(2,1)} %param.23) | copy-start | bytes 2752516
  1.6 11.7 %collective-permute-start.7 = (bf16[1,3584]{1,0:T(2,128)(2,1)S(1)}, bf16[1,3584]{1,0:T(2,128)(2,1)S(1)}, u32[]{:S(2)}, u32[]{:S(2)}) collective-permute-start(bf16[1,3584]{1,0:T(2,128)(2,1)S(1)} %convert_element_type.134), channel_id=1, source_target_pairs={{0,448},{64,0},{128,64},{192,128},{256,192},{320,256},{384,320},{4... | collective-permute-start | bytes 21512 | tf_op jit(solution)/shard_map/ppermute | solution.py:13
  9.0 7.7 %collective-permute-start.6 = (bf16[1,3584]{1,0:T(2,128)(2,1)S(1)}, bf16[1,3584]{1,0:T(2,128)(2,1)S(1)}, u32[]{:S(2)}, u32[]{:S(2)}) collective-permute-start(bf16[1,3584]{1,0:T(2,128)(2,1)S(1)} %convert_element_type.132), channel_id=1, source_target_pairs={{0,64},{64,128},{128,192},{192,256},{256,320},{320,384},{384,448},... | collective-permute-start | bytes 21512 | tf_op jit(solution)/shard_map/ppermute | solution.py:13
  18.5 60.9 %copy-start.4 = (bf16[1,3584,128]{2,1,0:T(8,128)(2,1)S(1)}, bf16[1,3584,128]{2,1,0:T(8,128)(2,1)}, u32[]{:S(2)}) copy-start(bf16[1,3584,128]{2,1,0:T(8,128)(2,1)} %param.21) | copy-start | bytes 2752516
  87.9 11.4 %copy-start.2 = (s32[1,1,2]{2,1,0:T(1,128)S(1)}, s32[1,1,2]{2,1,0:T(1,128)}, u32[]{:S(2)}) copy-start(s32[1,1,2]{2,1,0:T(1,128)} %param.15) | copy-start | bytes 28
  87.9 11.4 %copy-start.3 = (s32[1,1,2]{2,1,0:T(1,128)S(1)}, s32[1,1,2]{2,1,0:T(1,128)}, u32[]{:S(2)}) copy-start(s32[1,1,2]{2,1,0:T(1,128)} %param.14) | copy-start | bytes 28
  87.9 20.0 %copy-start.5 = (bf16[1,1,2,64,576]{4,3,2,1,0:T(8,128)(2,1)S(1)}, bf16[1,1,2,64,576]{4,3,2,1,0:T(8,128)(2,1)}, u32[]{:S(2)}) copy-start(bf16[1,1,2,64,576]{4,3,2,1,0:T(8,128)(2,1)} %param.16) | copy-start | bytes 442372
  87.9 67.2 %all-to-all-start.1 = ((bf16[64,4,3584]{2,1,0:T(4,128)(2,1)}), bf16[64,4,3584]{2,1,0:T(4,128)(2,1)S(1)}, u32[]{:S(2)}, u32[]{:S(2)}) async-start(bf16[64,4,3584]{2,1,0:T(4,128)(2,1)} %copy.36), calls=%async_computation.1 | async-start | bytes 3670016 | tf_op jit(solution)/shard_map/all_to_all | solution.py:125
  99.2 16.4 %copy-start.6 = (s32[1,1,2,2]{3,2,1,0:T(2,128)S(1)}, s32[1,1,2,2]{3,2,1,0:T(2,128)}, u32[]{:S(2)}) copy-start(s32[1,1,2,2]{3,2,1,0:T(2,128)} %param.13) | copy-start | bytes 52
  99.3 16.5 %copy-start.1 = (bf16[1,1,4,64,576]{4,3,2,1,0:T(8,128)(2,1)S(1)}, bf16[1,1,4,64,576]{4,3,2,1,0:T(8,128)(2,1)}, u32[]{:S(2)}) copy-start(bf16[1,1,4,64,576]{4,3,2,1,0:T(8,128)(2,1)} %param.12) | copy-start | bytes 884740
  99.9 42.6 %collective-permute-start = (bf16[1,1]{1,0:T(2,128)(2,1)}, bf16[1,1]{1,0:T(2,128)(2,1)}, u32[]{:S(2)}, u32[]{:S(2)}) collective-permute-start(bf16[1,1]{1,0:T(2,128)(2,1)} %bitcast.4), channel_id=1, source_target_pairs={{0,64},{64,128},{128,192},{192,256},{256,320},{320,384},{384,448},... | collective-permute-start | bytes 14 | tf_op jit(solution)/shard_map/ppermute | solution.py:13
  101.8 43.2 %collective-permute-start.1 = (bf16[1,1]{1,0:T(2,128)(2,1)}, bf16[1,1]{1,0:T(2,128)(2,1)}, u32[]{:S(2)}, u32[]{:S(2)}) collective-permute-start(bf16[1,1]{1,0:T(2,128)(2,1)} %bitcast.7), channel_id=1, source_target_pairs={{0,448},{64,0},{128,64},{192,128},{256,192},{320,256},{384,320},{4... | collective-permute-start | bytes 14 | tf_op jit(solution)/shard_map/ppermute | solution.py:13
  108.8 36.9 %collective-permute-start.3 = (bf16[1,64,576]{2,1,0:T(8,128)(2,1)}, bf16[1,64,576]{2,1,0:T(8,128)(2,1)}, u32[]{:S(2)}, u32[]{:S(2)}) collective-permute-start(bf16[1,64,576]{2,1,0:T(8,128)(2,1)} %bitcast.117), channel_id=1, source_target_pairs={{0,448},{64,0},{128,64},{192,128},{256,192},{320,256},{384,320},{4... | collective-permute-start | bytes 221192 | tf_op jit(solution)/shard_map/ppermute | solution.py:13
  111.7 34.1 %collective-permute-start.2 = (bf16[1,64,576]{2,1,0:T(8,128)(2,1)}, bf16[1,64,576]{2,1,0:T(8,128)(2,1)}, u32[]{:S(2)}, u32[]{:S(2)}) collective-permute-start(bf16[1,64,576]{2,1,0:T(8,128)(2,1)} %bitcast.115), channel_id=1, source_target_pairs={{0,64},{64,128},{128,192},{192,256},{256,320},{320,384},{384,448},... | collective-permute-start | bytes 221192 | tf_op jit(solution)/shard_map/ppermute | solution.py:13
  117.4 28.4 %collective-permute-start.5 = (bf16[1,128,576]{1,2,0:T(8,128)(2,1)}, bf16[1,128,576]{1,2,0:T(8,128)(2,1)}, u32[]{:S(2)}, u32[]{:S(2)}) collective-permute-start(bf16[1,128,576]{1,2,0:T(8,128)(2,1)} %bitcast.111), channel_id=1, source_target_pairs={{0,448},{64,0},{128,64},{192,128},{256,192},{320,256},{384,320},{4... | collective-permute-start | bytes 442376 | tf_op jit(solution)/shard_map/ppermute | solution.py:13
  142.4 9.1 %collective-permute-start.4 = (bf16[1,128,576]{1,2,0:T(8,128)(2,1)S(1)}, bf16[1,128,576]{1,2,0:T(8,128)(2,1)S(1)}, u32[]{:S(2)}, u32[]{:S(2)}) collective-permute-start(bf16[1,128,576]{1,2,0:T(8,128)(2,1)S(1)} %bitcast.123), channel_id=1, source_target_pairs={{0,64},{64,128},{128,192},{192,256},{256,320},{320,384},{384,448},... | collective-permute-start | bytes 442376 | tf_op jit(solution)/shard_map/ppermute | solution.py:13
where the time goes:
time: 158 us; the launch traced here: 157 us
  blocking collectives  60.9 us (39%)
  starting transfers between devices  39.4 us (25%)
  waiting for transfers between devices  28.4 us (18%)
  matrix products  12.8 us (8%)
  local copies, waits for them, and re-layouts  8.71 us (6%)
  other arithmetic  4.25 us (3%)
  between operations  2.15 us (1%)
    all_to_all x1, blocking collectives, body(): lax.all_to_all(outgoing, 'ep', split_axis=0, concat_axis=0, tiled=True)  60.9 us
    ppermute x8, waiting for transfers between devices, passed_along(): lax.ppermute(shard, axis, [(i, (i + by) % length) for i in range(length)])  28.4 us
    ppermute x8, starting transfers between devices, passed_along(): lax.ppermute(shard, axis, [(i, (i + by) % length) for i in range(length)])  28.1 us
    all_to_all x1, starting transfers between devices, body(): lax.all_to_all(part, 'ep', split_axis=0, concat_axis=0, tiled=True)  11.4 us
    convert_element_type x1, local copies, waits for them, and re-layouts, body(): jnp.einsum('skf,fd->skd', act, w_down, preferred_element_type=jnp.float32)  4.17 us
    dot_general x1, matrix products, body(): jnp.einsum('skf,fd->skd', act, w_down, preferred_element_type=jnp.float32)  3.6 us
  transfers between devices with their start and end apart: 9, of which 3 were waited for; matrix products, arithmetic and copies ran while one was open for 8% of the time, Pallas kernels for 0%

commit v1 on v0

v1 whole, which is shorter than its diff:
```python
import jax
import jax.numpy as jnp
from jax import lax
from jax.sharding import PartitionSpec as P

VDIM = 512
QK_DIM = 192
SLICES = 8


def passed_along(shard, axis, by):
    length = lax.axis_size(axis)
    return lax.ppermute(shard, axis, [(i, (i + by) % length) for i in range(length)])


def attend_rows(questions, keys, lens):
    scores = jnp.einsum(
        "rhl,rtl->rht", questions, keys, preferred_element_type=jnp.float32
    ) * QK_DIM ** (-0.5)
    live = jnp.arange(keys.shape[1], dtype=jnp.int32)[None, None, :] < lens[:, None, None]
    scores = jnp.where(live, scores, jnp.float32(-1e30))
    top = jnp.max(scores, axis=2, keepdims=True)
    expo = jnp.exp(scores - top)
    probs = (expo / jnp.sum(expo, axis=2, keepdims=True)).astype(jnp.bfloat16)
    out = jnp.einsum("rht,rtv->rhv", probs, keys[:, :, :VDIM], preferred_element_type=jnp.float32)
    return out.astype(jnp.bfloat16)


def body(
    latent_cache,
    page_table,
    lengths,
    move_to,
    query,
    hidden,
    norm_gain,
    expert_ids,
    expert_gates,
    gate_weight,
    up_weight,
    down_weight,
):
    pool = latent_cache[0, 0]
    table = page_table[0, 0]
    requests = table.shape[0]
    moves = move_to[0, 0]
    rows = hidden[0, 0]
    width = rows.shape[1]
    devices = lax.axis_size("ep")
    experts_here = devices // SLICES

    onehot = (
        expert_ids[0, 0][:, :, None] == jnp.arange(experts_here, dtype=jnp.int32)
    ).astype(jnp.float32)
    mix = jnp.einsum("sk,skx->sx", expert_gates[0, 0], onehot, precision=lax.Precision.HIGHEST)
    mix_next = passed_along(mix[requests : requests + 1], "grp", -1)
    mix_prev = passed_along(mix[requests + 1 : requests + 2], "grp", 1)
    at = moves[:, None]
    mix_home = jnp.where(
        at == 0, mix[:requests], jnp.where(at == 1, mix_next, mix_prev)
    )

    wide = rows.astype(jnp.float32)
    normed = (
        wide * lax.rsqrt(jnp.mean(wide * wide, axis=-1, keepdims=True) + 1e-06) * norm_gain
    ).astype(jnp.bfloat16)
    outgoing = jnp.broadcast_to(normed[None], (devices, requests, width))
    received = lax.all_to_all(outgoing, "ep", split_axis=0, concat_axis=0, tiled=True)
    flat = received.reshape(devices * requests, width)
    gate = jnp.dot(flat, gate_weight[0], preferred_element_type=jnp.float32)
    upper = jnp.dot(flat, up_weight[0], preferred_element_type=jnp.float32)
    act = (jax.nn.silu(gate) * upper).astype(jnp.bfloat16)
    part = jnp.dot(act, down_weight[0], preferred_element_type=jnp.float32).astype(jnp.bfloat16)
    returned = lax.all_to_all(
        part.reshape(devices, requests, width), "ep", split_axis=0, concat_axis=0, tiled=True
    )
    summed = jnp.sum(
        returned.reshape(experts_here, SLICES, requests, width).astype(jnp.float32), axis=1
    )
    moe = jnp.sum(summed * mix_home.T[:, :, None], axis=0).astype(jnp.bfloat16)

    keys = pool[table.reshape(-1)].reshape(requests, table.shape[1] * pool.shape[1], pool.shape[2])
    attn = attend_rows(query[0, 0], keys, lengths[0, 0])
    heads = attn.shape[1]
    both = jnp.concatenate([attn, moe.reshape(requests, width // VDIM, VDIM)], axis=1)

    def picked(which):
        keep = (moves == which)[:, None, None]
        return jnp.sum(jnp.where(keep, both, jnp.zeros_like(both)), axis=0, dtype=jnp.bfloat16)

    from_prev = passed_along(picked(1), "grp", 1)
    from_next = passed_along(picked(2), "grp", -1)
    stay = jnp.where((moves == 0)[:, None, None], both, jnp.zeros_like(both))
    served = jnp.concatenate([stay, from_prev[None], from_next[None]], axis=0)
    return (
        served[None, None, :, :heads],
        served[:, heads:].reshape(1, 1, served.shape[0], width),
    )


def solution(mesh):
    in_specs = (
        P("grp", "ep", None, None, None),
        P("grp", "ep", None, None),
        P("grp", "ep", None),
        P("grp", "ep", None),
        P("grp", "ep", None, None, None),
        P("grp", "ep", None, None),
        P(),
        P("grp", "ep", None, None),
        P("grp", "ep", None, None),
        P("ep", None, None),
        P("ep", None, None),
        P("ep", None, None),
    )
    out_specs = (P("grp", "ep", None, None, None), P("grp", "ep", None, None))
    return jax.shard_map(body, mesh=mesh, in_specs=in_specs, out_specs=out_specs, check_vma=False)
```

time: 158 us -> 104 us (0.66)
  the two profiles are of different devices: /device:TPU:8 before, /device:TPU:1 now
where the time goes in v1:
time: 104 us
  waiting for transfers between devices  49.6 us (48%)
  starting transfers between devices  40.5 us (39%)
  local copies, waits for them, and re-layouts  5.22 us (5%)
  matrix products  4.28 us (4%)
  other arithmetic  3.24 us (3%)
    all_to_all x1, waiting for transfers between devices, body(): lax.all_to_all(outgoing, 'ep', split_axis=0, concat_axis=0, tiled=True)  26.7 us
    all_to_all x1, starting transfers between devices, body(): lax.all_to_all(outgoing, 'ep', split_axis=0, concat_axis=0, tiled=True)  17.8 us
    all_to_all x1, waiting for transfers between devices, body(): lax.all_to_all(part.reshape(devices, requests, width), 'ep', split_axis=0...  17.6 us
    ppermute x4, starting transfers between devices, passed_along(): lax.ppermute(shard, axis, [(i, (i + by) % length) for i in range(length)])  14.4 us
    all_to_all x1, starting transfers between devices, body(): lax.all_to_all(part.reshape(devices, requests, width), 'ep', split_axis=0...  8.35 us
    ppermute x4, waiting for transfers between devices, passed_along(): lax.ppermute(shard, axis, [(i, (i + by) % length) for i in range(length)])  5.28 us
  transfers between devices with their start and end apart: 6, of which 3 were waited for; matrix products, arithmetic and copies ran while one was open for 2% of the time, Pallas kernels for 0%

profile of v1, /device:TPU:1, one launch (start us, length us, event | category | flops | bytes accessed | tf_op | source)
XLA Modules:
  0.0 103.7 jit_solution(18087139418384027810)
XLA Ops:
  0.6 0.0 copy-start
  0.6 0.9 fusion.20
  1.6 0.8 fusion.22
  2.4 1.4 %broadcast_in_dim.95 = bf16[64,2,3584]{2,1,0:T(2,128)(2,1)} broadcast(bf16[2,3584]{1,0:T(2,128)(2,1)S(1)} %fusion.22), dimensions={1,2} | broadcast | bytes 931840 | tf_op jit(solution)/shard_map/broadcast_in_dim | solution.py:67
  3.8 17.8 %all-to-all-start = ((bf16[64,2,3584]{2,1,0:T(2,128)(2,1)}), bf16[64,2,3584]{2,1,0:T(2,128)(2,1)S(1)}, u32[]{:S(2)}, u32[]{:S(2)}) async-start(bf16[64,2,3584]{2,1,0:T(2,128)(2,1)} %broadcast_in_dim.95), calls=%async_computation | async-start | bytes 1835008 | tf_op jit(solution)/shard_map/all_to_all | solution.py:68
  21.6 0.2 fusion.23
  21.8 26.7 %all-to-all-done = bf16[64,2,3584]{2,1,0:T(2,128)(2,1)S(1)} async-done(((bf16[64,2,3584]{2,1,0:T(2,128)(2,1)}), bf16[64,2,3584]{2,1,0:T(2,128)(2,1)S(1)}, u32[]{:S(2)}, u32[]{:S(2)}) %all-to-all-start) | async-done | bytes 917536 | tf_op jit(solution)/shard_map/all_to_all | solution.py:68
  48.6 0.3 reshape.159
  48.9 1.6 %fusion.9 = f32[128,128]{1,0:T(8,128)S(1)} fusion(bf16[128,3584]{1,0:T(8,128)(2,1)S(1)} %reshape.159, bf16[1,3584,128]{2,1,0:T(8,128)(2,1)} %param.21), kind=kOutput, calls=%fused_computation.14 | convolution fusion | flops 117440512 | bytes 1900544 | tf_op jit(solution)/shard_map/dot_general | solution.py:70
  50.5 1.9 %convolution_convert_fusion = bf16[128,3584]{1,0:T(8,128)(2,1)S(1)} fusion(bf16[128,3584]{1,0:T(8,128)(2,1)S(1)} %reshape.159, bf16[1,128,3584]{2,1,0:T(8,128)(2,1)S(1)} %copy-done, bf16[1,3584,128]{2,1,0:T(8,128)(2,1)} %param.22, f32[128,128]{1,0:T(8,128)S(1)} %fusion.9), kind=kOutput, calls=%fused_computation.2 | convolution fusion | flops 235438080 | bytes 3735552 | tf_op jit(solution)/shard_map/dot_general | solution.py:73
  52.4 1.3 %reshape.160 = bf16[64,2,3584]{2,1,0:T(2,128)(2,1)} reshape(bf16[128,3584]{1,0:T(8,128)(2,1)S(1)} %convolution_convert_fusion) | data formatting | bytes 1835008 | tf_op jit(solution)/shard_map/reshape | solution.py:75
  53.7 8.3 %all-to-all-start.1 = ((bf16[64,2,3584]{2,1,0:T(2,128)(2,1)}), bf16[64,2,3584]{2,1,0:T(2,128)(2,1)S(1)}, u32[]{:S(2)}, u32[]{:S(2)}) async-start(bf16[64,2,3584]{2,1,0:T(2,128)(2,1)} %reshape.160), calls=%async_computation.1 | async-start | bytes 1835008 | tf_op jit(solution)/shard_map/all_to_all | solution.py:74
  62.1 3.1 %collective-permute-start.1 = (f32[1,8]{1,0:T(1,128)S(1)}, f32[1,8]{1,0:T(1,128)S(1)}, u32[]{:S(2)}, u32[]{:S(2)}) collective-permute-start(f32[1,8]{1,0:T(1,128)S(1)} %get-tuple-element.6), channel_id=1, source_target_pairs={{0,64},{64,128},{128,192},{192,256},{256,320},{320,384},{384,448},... | collective-permute-start | bytes 104 | tf_op jit(solution)/shard_map/ppermute | solution.py:13
  65.2 4.3 %collective-permute-start = (f32[1,8]{1,0:T(1,128)S(1)}, f32[1,8]{1,0:T(1,128)S(1)}, u32[]{:S(2)}, u32[]{:S(2)}) collective-permute-start(f32[1,8]{1,0:T(1,128)S(1)} %get-tuple-element.5), channel_id=1, source_target_pairs={{0,448},{64,0},{128,64},{192,128},{256,192},{320,256},{384,320},{4... | collective-permute-start | bytes 104 | tf_op jit(solution)/shard_map/ppermute | solution.py:13
  69.5 0.1 reshape_squeeze.3
  69.6 0.6 gather_fusion
  70.2 0.1 iota_compare_fusion.2
  70.3 0.3 fusion.4
  70.5 0.2 fusion.29
  70.7 0.4 convolution_convert_fusion.1
  71.1 0.0 collective-permute-done
  71.1 0.1 select_bitcast_fusion
  71.2 0.1 copy.20
  71.3 17.6 %all-to-all-done.1 = bf16[64,2,3584]{2,1,0:T(2,128)(2,1)S(1)} async-done(((bf16[64,2,3584]{2,1,0:T(2,128)(2,1)}), bf16[64,2,3584]{2,1,0:T(2,128)(2,1)S(1)}, u32[]{:S(2)}, u32[]{:S(2)}) %all-to-all-start.1) | async-done | bytes 917536 | tf_op jit(solution)/shard_map/all_to_all | solution.py:74
  88.8 0.8 convert_reduce_fusion
  89.6 0.2 multiply_reduce_fusion
  89.8 0.1 select_reduce_fusion.1
  90.0 5.1 %collective-permute-start.3 = (bf16[71,512]{1,0:T(8,128)(2,1)S(1)}, bf16[71,512]{1,0:T(8,128)(2,1)S(1)}, u32[]{:S(2)}, u32[]{:S(2)}) collective-permute-start(bf16[71,512]{1,0:T(8,128)(2,1)S(1)} %get-tuple-element.3), channel_id=1, source_target_pairs={{0,448},{64,0},{128,64},{192,128},{256,192},{320,256},{384,320},{4... | collective-permute-start | bytes 218120 | tf_op jit(solution)/shard_map/ppermute | solution.py:13
  95.0 1.9 %collective-permute-start.2 = (bf16[71,512]{1,0:T(8,128)(2,1)S(1)}, bf16[71,512]{1,0:T(8,128)(2,1)S(1)}, u32[]{:S(2)}, u32[]{:S(2)}) collective-permute-start(bf16[71,512]{1,0:T(8,128)(2,1)S(1)} %get-tuple-element.2), channel_id=1, source_target_pairs={{0,64},{64,128},{128,192},{192,256},{256,320},{320,384},{384,448},... | collective-permute-start | bytes 218120 | tf_op jit(solution)/shard_map/ppermute | solution.py:13
  97.0 5.3 %collective-permute-done.2 = bf16[71,512]{1,0:T(8,128)(2,1)S(1)} collective-permute-done((bf16[71,512]{1,0:T(8,128)(2,1)S(1)}, bf16[71,512]{1,0:T(8,128)(2,1)S(1)}, u32[]{:S(2)}, u32[]{:S(2)}) %collective-permute-start.2) | collective-permute-done | bytes 72736 | tf_op jit(solution)/shard_map/ppermute | solution.py:13
  102.3 0.7 slice_bitcast_fusion
  103.0 0.6 reshape.161
  (25 shorter events, 0.1 us)
Async XLA Ops:
  0.6 49.9 %copy-start = (bf16[1,128,3584]{2,1,0:T(8,128)(2,1)S(1)}, bf16[1,128,3584]{2,1,0:T(8,128)(2,1)}, u32[]{:S(2)}) copy-start(bf16[1,128,3584]{2,1,0:T(8,128)(2,1)} %param.23) | copy-start | bytes 2752516
  3.8 17.8 %copy-start.4 = (f32[1,1,4,6]{3,2,1,0:T(4,128)S(1)}, f32[1,1,4,6]{3,2,1,0:T(4,128)}, u32[]{:S(2)}) copy-start(f32[1,1,4,6]{3,2,1,0:T(4,128)} %param.20) | copy-start | bytes 292
  3.8 17.8 %copy-start.5 = (s32[1,1,4,6]{3,2,1,0:T(4,128)S(1)}, s32[1,1,4,6]{3,2,1,0:T(4,128)}, u32[]{:S(2)}) copy-start(s32[1,1,4,6]{3,2,1,0:T(4,128)} %param.19) | copy-start | bytes 292
  3.8 44.7 %all-to-all-start = ((bf16[64,2,3584]{2,1,0:T(2,128)(2,1)}), bf16[64,2,3584]{2,1,0:T(2,128)(2,1)S(1)}, u32[]{:S(2)}, u32[]{:S(2)}) async-start(bf16[64,2,3584]{2,1,0:T(2,128)(2,1)} %broadcast_in_dim.95), calls=%async_computation | async-start | bytes 1835008 | tf_op jit(solution)/shard_map/all_to_all | solution.py:68
  53.7 15.8 %copy-start.6 = (s32[1,1,2,2]{3,2,1,0:T(2,128)S(1)}, s32[1,1,2,2]{3,2,1,0:T(2,128)}, u32[]{:S(2)}) copy-start(s32[1,1,2,2]{3,2,1,0:T(2,128)} %param.13) | copy-start | bytes 52
  53.7 15.9 %copy-start.1 = (bf16[1,1,4,64,576]{4,3,2,1,0:T(8,128)(2,1)S(1)}, bf16[1,1,4,64,576]{4,3,2,1,0:T(8,128)(2,1)}, u32[]{:S(2)}) copy-start(bf16[1,1,4,64,576]{4,3,2,1,0:T(8,128)(2,1)} %param.12) | copy-start | bytes 884740
  53.7 16.5 %copy-start.7 = (s32[1,1,2]{2,1,0:T(1,128)S(1)}, s32[1,1,2]{2,1,0:T(1,128)}, u32[]{:S(2)}) copy-start(s32[1,1,2]{2,1,0:T(1,128)} %param.14) | copy-start | bytes 28
  53.7 16.6 %copy-start.2 = (bf16[1,1,2,64,576]{4,3,2,1,0:T(8,128)(2,1)S(1)}, bf16[1,1,2,64,576]{4,3,2,1,0:T(8,128)(2,1)}, u32[]{:S(2)}) copy-start(bf16[1,1,2,64,576]{4,3,2,1,0:T(8,128)(2,1)} %param.16) | copy-start | bytes 442372
  53.7 35.2 %all-to-all-start.1 = ((bf16[64,2,3584]{2,1,0:T(2,128)(2,1)}), bf16[64,2,3584]{2,1,0:T(2,128)(2,1)S(1)}, u32[]{:S(2)}, u32[]{:S(2)}) async-start(bf16[64,2,3584]{2,1,0:T(2,128)(2,1)} %reshape.160), calls=%async_computation.1 | async-start | bytes 1835008 | tf_op jit(solution)/shard_map/all_to_all | solution.py:74
  62.0 8.7 %copy-start.3 = (s32[1,1,2]{2,1,0:T(1,128)S(1)}, s32[1,1,2]{2,1,0:T(1,128)}, u32[]{:S(2)}) copy-start(s32[1,1,2]{2,1,0:T(1,128)} %param.15) | copy-start | bytes 28
  62.1 9.0 %collective-permute-start.1 = (f32[1,8]{1,0:T(1,128)S(1)}, f32[1,8]{1,0:T(1,128)S(1)}, u32[]{:S(2)}, u32[]{:S(2)}) collective-permute-start(f32[1,8]{1,0:T(1,128)S(1)} %get-tuple-element.6), channel_id=1, source_target_pairs={{0,64},{64,128},{128,192},{192,256},{256,320},{320,384},{384,448},... | collective-permute-start | bytes 104 | tf_op jit(solution)/shard_map/ppermute | solution.py:13
  65.2 5.9 %collective-permute-start = (f32[1,8]{1,0:T(1,128)S(1)}, f32[1,8]{1,0:T(1,128)S(1)}, u32[]{:S(2)}, u32[]{:S(2)}) collective-permute-start(f32[1,8]{1,0:T(1,128)S(1)} %get-tuple-element.5), channel_id=1, source_target_pairs={{0,448},{64,0},{128,64},{192,128},{256,192},{320,256},{384,320},{4... | collective-permute-start | bytes 104 | tf_op jit(solution)/shard_map/ppermute | solution.py:13
  90.0 7.0 %collective-permute-start.3 = (bf16[71,512]{1,0:T(8,128)(2,1)S(1)}, bf16[71,512]{1,0:T(8,128)(2,1)S(1)}, u32[]{:S(2)}, u32[]{:S(2)}) collective-permute-start(bf16[71,512]{1,0:T(8,128)(2,1)S(1)} %get-tuple-element.3), channel_id=1, source_target_pairs={{0,448},{64,0},{128,64},{192,128},{256,192},{320,256},{384,320},{4... | collective-permute-start | bytes 218120 | tf_op jit(solution)/shard_map/ppermute | solution.py:13
  95.0 7.2 %collective-permute-start.2 = (bf16[71,512]{1,0:T(8,128)(2,1)S(1)}, bf16[71,512]{1,0:T(8,128)(2,1)S(1)}, u32[]{:S(2)}, u32[]{:S(2)}) collective-permute-start(bf16[71,512]{1,0:T(8,128)(2,1)S(1)} %get-tuple-element.2), channel_id=1, source_target_pairs={{0,64},{64,128},{128,192},{192,256},{256,320},{320,384},{384,448},... | collective-permute-start | bytes 218120 | tf_op jit(solution)/shard_map/ppermute | solution.py:13

commit v2 on v1

--- a/solution.py
+++ b/solution.py
@@ -60,41 +60,56 @@
         at == 0, mix[:requests], jnp.where(at == 1, mix_next, mix_prev)
     )
 
+    keys = pool[table.reshape(-1)].reshape(requests, table.shape[1] * pool.shape[1], pool.shape[2])
+    attn = attend_rows(query[0, 0], keys, lengths[0, 0])
+
+    def picked(which, values):
+        keep = (moves == which).reshape((requests,) + (1,) * (values.ndim - 1))
+        return jnp.sum(jnp.where(keep, values, jnp.zeros_like(values)), axis=0, dtype=values.dtype)
+
+    def served(values, from_prev, from_next):
+        keep = (moves == 0).reshape((requests,) + (1,) * (values.ndim - 1))
+        stay = jnp.where(keep, values, jnp.zeros_like(values))
+        return jnp.concatenate([stay, from_prev[None], from_next[None]], axis=0)
+
+    attn_prev = passed_along(picked(1, attn), "grp", 1)
+    attn_next = passed_along(picked(2, attn), "grp", -1)
+
     wide = rows.astype(jnp.float32)
     normed = (
         wide * lax.rsqrt(jnp.mean(wide * wide, axis=-1, keepdims=True) + 1e-06) * norm_gain
     ).astype(jnp.bfloat16)
-    outgoing = jnp.broadcast_to(normed[None], (devices, requests, width))
+    chips = devices // requests
+    outgoing = jnp.broadcast_to(normed[None], (chips, requests, width)).reshape(devices, 1, width)
     received = lax.all_to_all(outgoing, "ep", split_axis=0, concat_axis=0, tiled=True)
-    flat = received.reshape(devices * requests, width)
-    gate = jnp.dot(flat, gate_weight[0], preferred_element_type=jnp.float32)
-    upper = jnp.dot(flat, up_weight[0], preferred_element_type=jnp.float32)
-    act = (jax.nn.silu(gate) * upper).astype(jnp.bfloat16)
-    part = jnp.dot(act, down_weight[0], preferred_element_type=jnp.float32).astype(jnp.bfloat16)
+    received, attn_prev, attn_next, mix_home = lax.optimization_barrier(
+        (received, attn_prev, attn_next, mix_home)
+    )
+    swap = [(i, i ^ 1) for i in range(devices)]
+    mine = received.reshape(devices, width)
+    theirs = lax.ppermute(mine, "ep", swap)
+
+    def experts(values):
+        gate = jnp.dot(values, gate_weight[0], preferred_element_type=jnp.float32)
+        upper = jnp.dot(values, up_weight[0], preferred_element_type=jnp.float32)
+        act = (jax.nn.silu(gate) * upper).astype(jnp.bfloat16)
+        return jnp.dot(act, down_weight[0], preferred_element_type=jnp.float32)
+
+    part_theirs = experts(theirs).astype(jnp.bfloat16)
+    part_mine = experts(mine)
+    pair = (part_mine + lax.ppermute(part_theirs, "ep", swap).astype(jnp.float32)).astype(jnp.bfloat16)
     returned = lax.all_to_all(
-        part.reshape(devices, requests, width), "ep", split_axis=0, concat_axis=0, tiled=True
+        pair.reshape(devices, 1, width), "ep", split_axis=0, concat_axis=0, tiled=True
     )
     summed = jnp.sum(
-        returned.reshape(experts_here, SLICES, requests, width).astype(jnp.float32), axis=1
+        returned.reshape(experts_here, SLICES // requests, requests, width).astype(jnp.float32), axis=1
     )
     moe = jnp.sum(summed * mix_home.T[:, :, None], axis=0).astype(jnp.bfloat16)
-
-    keys = pool[table.reshape(-1)].reshape(requests, table.shape[1] * pool.shape[1], pool.shape[2])
-    attn = attend_rows(query[0, 0], keys, lengths[0, 0])
-    heads = attn.shape[1]
-    both = jnp.concatenate([attn, moe.reshape(requests, width // VDIM, VDIM)], axis=1)
-
-    def picked(which):
-        keep = (moves == which)[:, None, None]
-        return jnp.sum(jnp.where(keep, both, jnp.zeros_like(both)), axis=0, dtype=jnp.bfloat16)
-
-    from_prev = passed_along(picked(1), "grp", 1)
-    from_next = passed_along(picked(2), "grp", -1)
-    stay = jnp.where((moves == 0)[:, None, None], both, jnp.zeros_like(both))
-    served = jnp.concatenate([stay, from_prev[None], from_next[None]], axis=0)
+    moe_prev = passed_along(picked(1, moe), "grp", 1)
+    moe_next = passed_along(picked(2, moe), "grp", -1)
     return (
-        served[None, None, :, :heads],
-        served[:, heads:].reshape(1, 1, served.shape[0], width),
+        served(attn, attn_prev, attn_next)[None, None],
+        served(moe, moe_prev, moe_next)[None, None],
     )
 
 

time: 104 us -> 110 us (1.058)
  waiting for transfers between devices: 49.6 us -> 24.7 us
  starting transfers between devices: 40.5 us -> 59.5 us
  other arithmetic: 3.24 us -> 11.2 us
  local copies, waits for them, and re-layouts: 5.22 us -> 7.44 us
    all_to_all x1, waiting for transfers between devices: 26.7 us -> 0.01 us  [body(): lax.all_to_all(outgoing, 'ep', split_axis=0, concat_axis=0, tiled=True)]
    ppermute x4 -> x6, starting transfers between devices: 14.4 us -> 22.6 us  [passed_along(): lax.ppermute(shard, axis, [(i, (i + by) % length) for i in range(length)])]
    ppermute x0 -> x2, starting transfers between devices: none -> 6.45 us  [the longest x1 4.19 us: body(): theirs = lax.ppermute(mine, 'ep', swap)]
    unnamed x16 -> x28, local copies, waits for them, and re-layouts: 0.04 us -> 4.61 us
    all_to_all x1, starting transfers between devices: 8.35 us -> 12.7 us  [body(): lax.all_to_all(pair.reshape(devices, 1, width), 'ep', split_axis=0, conca...]
    reshape x0 -> x2, other arithmetic: none -> 4.31 us  [the longest x1 3.39 us: body(): jnp.broadcast_to(normed[None], (chips, requests, width))]
    ppermute x0 -> x2, waiting for transfers between devices: none -> 2.88 us  [the longest x1 1.46 us: body(): lax.ppermute(part_theirs, 'ep', swap).astype(jnp.float32)]
    convert_element_type x0 -> x1, other arithmetic: none -> 2.57 us  [body(): returned.reshape(experts_here, SLICES // requests, requests, width)]
  transfers between devices with their start and end apart: 6 -> 10, of which waited for: 3 -> 5; matrix products, arithmetic and copies ran while one was open for 2% -> 3% of each run, Pallas kernels for 0% -> 0%
where the time goes in v2:
time: 110 us; the launch traced here: 109 us
  starting transfers between devices  59.5 us (54%)
  waiting for transfers between devices  24.7 us (22%)
  other arithmetic  11.2 us (10%)
  local copies, waits for them, and re-layouts  7.44 us (7%)
  matrix products  5.37 us (5%)
    ppermute x6, starting transfers between devices, passed_along(): lax.ppermute(shard, axis, [(i, (i + by) % length) for i in range(length)])  22.6 us
    all_to_all x1, starting transfers between devices, body(): lax.all_to_all(outgoing, 'ep', split_axis=0, concat_axis=0, tiled=True)  17.8 us
    all_to_all x1, waiting for transfers between devices, body(): lax.all_to_all(pair.reshape(devices, 1, width), 'ep', split_axis=0, conca...  17.2 us
    all_to_all x1, starting transfers between devices, body(): lax.all_to_all(pair.reshape(devices, 1, width), 'ep', split_axis=0, conca...  12.7 us
    unnamed x28, local copies, waits for them, and re-layouts  4.61 us
    ppermute x6, waiting for transfers between devices, passed_along(): lax.ppermute(shard, axis, [(i, (i + by) % length) for i in range(length)])  4.52 us
    ppermute x1, starting transfers between devices, body(): theirs = lax.ppermute(mine, 'ep', swap)  4.19 us
    dot_general x2, matrix products, experts(): return jnp.dot(act, down_weight[0], preferred_element_type=jnp.float32)  3.94 us
  transfers between devices with their start and end apart: 10, of which 5 were waited for; matrix products, arithmetic and copies ran while one was open for 3% of the time, Pallas kernels for 0%

profile of v2, /device:TPU:1, one launch (start us, length us, event | category | flops | bytes accessed | tf_op | source)
XLA Modules:
  0.0 109.1 jit_solution(10684778167421334455)
XLA Ops:
  0.7 0.9 fusion.30
  1.6 0.8 fusion.32
  3.1 0.5 broadcast.157
  3.6 3.4 %reduce.2 = bf16[64,3584]{1,0:T(8,128)(2,1)S(1)} reduce(bf16[64,1,3584]{2,1,0:T(2,128)(2,1)S(1)} %reshape.184, bf16[]{:T(256)} %broadcast.157), dimensions={1}, to_apply=%reshape.184.reduce_sub_computation | reduce | bytes 917506 | tf_op jit(solution)/shard_map/reshape | solution.py:83
  7.0 0.9 reshape.186
  7.8 17.8 %all-to-all-start = ((bf16[64,2,1792]{2,1,0:T(2,128)(2,1)}), bf16[64,2,1792]{2,1,0:T(2,128)(2,1)S(1)}, u32[]{:S(2)}, u32[]{:S(2)}) async-start(bf16[64,2,1792]{2,1,0:T(2,128)(2,1)} %reshape.186), calls=%async_computation | async-start | bytes 917504 | tf_op jit(solution)/shard_map/all_to_all | solution.py:84
  25.6 0.7 copy-done.10
  26.4 0.6 copy-done.11
  27.1 0.6 gather_fusion
  28.9 3.1 %collective-permute-start = (bf16[64,512]{1,0:T(8,128)(2,1)S(1)}, bf16[64,512]{1,0:T(8,128)(2,1)S(1)}, u32[]{:S(2)}, u32[]{:S(2)}) collective-permute-start(bf16[64,512]{1,0:T(8,128)(2,1)S(1)} %get-tuple-element.11), channel_id=1, source_target_pairs={{0,64},{64,128},{128,192},{192,256},{256,320},{320,384},{384,448},... | collective-permute-start | bytes 196616 | tf_op jit(solution)/shard_map/ppermute | solution.py:13
  32.0 4.3 %collective-permute-start.1 = (bf16[64,512]{1,0:T(8,128)(2,1)S(1)}, bf16[64,512]{1,0:T(8,128)(2,1)S(1)}, u32[]{:S(2)}, u32[]{:S(2)}) collective-permute-start(bf16[64,512]{1,0:T(8,128)(2,1)S(1)} %get-tuple-element.10), channel_id=1, source_target_pairs={{0,448},{64,0},{128,64},{192,128},{256,192},{320,256},{384,320},{4... | collective-permute-start | bytes 196616 | tf_op jit(solution)/shard_map/ppermute | solution.py:13
  36.5 1.9 %collective-permute-start.3 = (f32[1,8]{1,0:T(1,128)S(1)}, f32[1,8]{1,0:T(1,128)S(1)}, u32[]{:S(2)}, u32[]{:S(2)}) collective-permute-start(f32[1,8]{1,0:T(1,128)S(1)} %get-tuple-element.17), channel_id=1, source_target_pairs={{0,64},{64,128},{128,192},{192,256},{256,320},{320,384},{384,448},... | collective-permute-start | bytes 104 | tf_op jit(solution)/shard_map/ppermute | solution.py:13
  38.5 5.5 %collective-permute-start.2 = (f32[1,8]{1,0:T(1,128)S(1)}, f32[1,8]{1,0:T(1,128)S(1)}, u32[]{:S(2)}, u32[]{:S(2)}) collective-permute-start(f32[1,8]{1,0:T(1,128)S(1)} %get-tuple-element.16), channel_id=1, source_target_pairs={{0,448},{64,0},{128,64},{192,128},{256,192},{320,256},{384,320},{4... | collective-permute-start | bytes 104 | tf_op jit(solution)/shard_map/ppermute | solution.py:13
  44.0 0.7 collective-permute-done.2
  45.2 4.2 %collective-permute-start.4 = (bf16[64,3584]{1,0:T(8,128)(2,1)S(1)}, bf16[64,3584]{1,0:T(8,128)(2,1)S(1)}, u32[]{:S(2)}, u32[]{:S(2)}) collective-permute-start(bf16[64,3584]{1,0:T(8,128)(2,1)S(1)} %bitcast.74), channel_id=1, source_target_pairs={{0,1},{1,0},{2,3},{3,2},{4,5},{5,4},{6,7},{7,6},{8,9},{9,8},{10,11... | collective-permute-start | bytes 1376264 | tf_op jit(solution)/shard_map/ppermute | solution.py:90
  49.4 1.4 %collective-permute-done.4 = bf16[64,3584]{1,0:T(8,128)(2,1)S(1)} collective-permute-done((bf16[64,3584]{1,0:T(8,128)(2,1)S(1)}, bf16[64,3584]{1,0:T(8,128)(2,1)S(1)}, u32[]{:S(2)}, u32[]{:S(2)}) %collective-permute-start.4) | collective-permute-done | bytes 458784 | tf_op jit(solution)/shard_map/ppermute | solution.py:90
  50.8 0.8 copy-done.3
  51.9 2.4 %convolution_convert_fusion = bf16[64,3584]{1,0:T(8,128)(2,1)} fusion(bf16[1,128,3584]{2,1,0:T(8,128)(2,1)S(1)} %copy-done, f32[64,128]{1,0:T(8,128)S(1)} %fusion.9, bf16[64,3584]{1,0:T(8,128)(2,1)} %copy-done.3, bf16[1,3584,128]{2,1,0:T(8,128)(2,1)S(1)} %copy-done.2), kind=kOutput, calls=%fused_computation.2 | convolution fusion | flops 117719040 | bytes 2785280 | tf_op jit(solution)/shard_map/dot_general | solution.py:96
  54.3 2.3 %collective-permute-start.5 = (bf16[64,3584]{1,0:T(8,128)(2,1)}, bf16[64,3584]{1,0:T(8,128)(2,1)}, u32[]{:S(2)}, u32[]{:S(2)}) collective-permute-start(bf16[64,3584]{1,0:T(8,128)(2,1)} %convolution_convert_fusion), channel_id=1, source_target_pairs={{0,1},{1,0},{2,3},{3,2},{4,5},{5,4},{6,7},{7,6},{8,9},{9,8},{10,11... | collective-permute-start | bytes 1376264 | tf_op jit(solution)/shard_map/ppermute | solution.py:100
  56.9 1.5 %collective-permute-done.5 = bf16[64,3584]{1,0:T(8,128)(2,1)} collective-permute-done((bf16[64,3584]{1,0:T(8,128)(2,1)}, bf16[64,3584]{1,0:T(8,128)(2,1)}, u32[]{:S(2)}, u32[]{:S(2)}) %collective-permute-start.5) | collective-permute-done | bytes 458784 | tf_op jit(solution)/shard_map/ppermute | solution.py:100
  58.3 1.6 %fusion.17 = bf16[64,1,3584]{2,0,1:T(8,128)(2,1)S(1)} fusion(bf16[64,3584]{1,0:T(8,128)(2,1)} %collective-permute-done.5, bf16[1,128,3584]{2,1,0:T(8,128)(2,1)S(1)} %copy-done, bf16[64,3584]{1,0:T(8,128)(2,1)S(1)} %bitcast.76, bf16[1,3584,128]{2,1,0:T(8,128)(2,1)S(1)} %copy-done.1, f32[64,128]{1,0:T(8,128)S(1)} %fusion.15), kind=kOutput, calls=%fused_computation.23 | convolution fusion | flops 118177792 | bytes 3244032 | tf_op jit(solution)/shard_map/dot_general | solution.py:96
  59.9 0.9 reduce.3
  60.8 0.9 reshape.188
  61.7 12.7 %all-to-all-start.1 = ((bf16[64,2,1792]{2,1,0:T(2,128)(2,1)}), bf16[64,2,1792]{2,1,0:T(2,128)(2,1)S(1)}, u32[]{:S(2)}, u32[]{:S(2)}) async-start(bf16[64,2,1792]{2,1,0:T(2,128)(2,1)} %reshape.188), calls=%async_computation.1 | async-start | bytes 917504 | tf_op jit(solution)/shard_map/all_to_all | solution.py:101
  74.5 17.2 %all-to-all-done.1 = bf16[64,2,1792]{2,1,0:T(2,128)(2,1)S(1)} async-done(((bf16[64,2,1792]{2,1,0:T(2,128)(2,1)}), bf16[64,2,1792]{2,1,0:T(2,128)(2,1)S(1)}, u32[]{:S(2)}, u32[]{:S(2)}) %all-to-all-start.1) | async-done | bytes 458784 | tf_op jit(solution)/shard_map/all_to_all | solution.py:101
  92.1 2.6 %convert_reduce_fusion = f32[64,3584]{1,0:T(8,128)S(1)} fusion(bf16[64,1,3584]{2,1,0:T(2,128)(2,1)S(1)} %reshape.189), kind=kLoop, calls=%fused_computation.21 | loop fusion | flops 229376 | bytes 1376256 | tf_op jit(solution)/shard_map/convert_element_type | solution.py:105
  94.7 0.5 reshape.173
  96.0 5.9 %collective-permute-start.7 = (bf16[3584]{0:T(1024)(128)(2,1)S(1)}, bf16[3584]{0:T(1024)(128)(2,1)S(1)}, u32[]{:S(2)}, u32[]{:S(2)}) collective-permute-start(bf16[3584]{0:T(1024)(128)(2,1)S(1)} %get-tuple-element.13), channel_id=1, source_target_pairs={{0,448},{64,0},{128,64},{192,128},{256,192},{320,256},{384,320},{4... | collective-permute-start | bytes 21512 | tf_op jit(solution)/shard_map/ppermute | solution.py:13
  101.9 1.9 %collective-permute-start.6 = (bf16[3584]{0:T(1024)(128)(2,1)S(1)}, bf16[3584]{0:T(1024)(128)(2,1)S(1)}, u32[]{:S(2)}, u32[]{:S(2)}) collective-permute-start(bf16[3584]{0:T(1024)(128)(2,1)S(1)} %get-tuple-element.12), channel_id=1, source_target_pairs={{0,64},{64,128},{128,192},{192,256},{256,320},{320,384},{384,448},... | collective-permute-start | bytes 21512 | tf_op jit(solution)/shard_map/ppermute | solution.py:13
  103.9 0.7 maximum_bitcast_fusion
  104.6 3.8 %collective-permute-done.6 = bf16[3584]{0:T(1024)(128)(2,1)S(1)} collective-permute-done((bf16[3584]{0:T(1024)(128)(2,1)S(1)}, bf16[3584]{0:T(1024)(128)(2,1)S(1)}, u32[]{:S(2)}, u32[]{:S(2)}) %collective-permute-start.6) | collective-permute-done | bytes 7200 | tf_op jit(solution)/shard_map/ppermute | solution.py:13
  108.4 0.7 maximum_bitcast_fusion.1
  (51 shorter events, 4.6 us)
Async XLA Ops:
  0.6 51.3 %copy-start = (bf16[1,128,3584]{2,1,0:T(8,128)(2,1)S(1)}, bf16[1,128,3584]{2,1,0:T(8,128)(2,1)}, u32[]{:S(2)}) copy-start(bf16[1,128,3584]{2,1,0:T(8,128)(2,1)} %param.23) | copy-start | bytes 2752516
  0.6 1.0 copy-start.6
  7.8 17.8 %copy-start.7 = (s32[1,1,2]{2,1,0:T(1,128)S(1)}, s32[1,1,2]{2,1,0:T(1,128)}, u32[]{:S(2)}) copy-start(s32[1,1,2]{2,1,0:T(1,128)} %param.15) | copy-start | bytes 28
  7.8 19.3 %copy-start.4 = (bf16[1,1,4,64,576]{4,3,2,1,0:T(8,128)(2,1)S(1)}, bf16[1,1,4,64,576]{4,3,2,1,0:T(8,128)(2,1)}, u32[]{:S(2)}) copy-start(bf16[1,1,4,64,576]{4,3,2,1,0:T(8,128)(2,1)} %param.12) | copy-start | bytes 884740
  7.8 36.9 %all-to-all-start = ((bf16[64,2,1792]{2,1,0:T(2,128)(2,1)}), bf16[64,2,1792]{2,1,0:T(2,128)(2,1)S(1)}, u32[]{:S(2)}, u32[]{:S(2)}) async-start(bf16[64,2,1792]{2,1,0:T(2,128)(2,1)} %reshape.186), calls=%async_computation | async-start | bytes 917504 | tf_op jit(solution)/shard_map/all_to_all | solution.py:84
  25.6 0.7 copy-start.10
  26.4 0.7 copy-start.11
  27.1 0.9 copy-start.5
  28.9 16.2 %collective-permute-start = (bf16[64,512]{1,0:T(8,128)(2,1)S(1)}, bf16[64,512]{1,0:T(8,128)(2,1)S(1)}, u32[]{:S(2)}, u32[]{:S(2)}) collective-permute-start(bf16[64,512]{1,0:T(8,128)(2,1)S(1)} %get-tuple-element.11), channel_id=1, source_target_pairs={{0,64},{64,128},{128,192},{192,256},{256,320},{320,384},{384,448},... | collective-permute-start | bytes 196616 | tf_op jit(solution)/shard_map/ppermute | solution.py:13
  32.0 4.3 %copy-start.9 = (s32[1,1,4,6]{3,2,1,0:T(4,128)S(1)}, s32[1,1,4,6]{3,2,1,0:T(4,128)}, u32[]{:S(2)}) copy-start(s32[1,1,4,6]{3,2,1,0:T(4,128)} %param.19) | copy-start | bytes 292
  32.0 4.3 %copy-start.8 = (f32[1,1,4,6]{3,2,1,0:T(4,128)S(1)}, f32[1,1,4,6]{3,2,1,0:T(4,128)}, u32[]{:S(2)}) copy-start(f32[1,1,4,6]{3,2,1,0:T(4,128)} %param.20) | copy-start | bytes 292
  32.0 13.1 %collective-permute-start.1 = (bf16[64,512]{1,0:T(8,128)(2,1)S(1)}, bf16[64,512]{1,0:T(8,128)(2,1)S(1)}, u32[]{:S(2)}, u32[]{:S(2)}) collective-permute-start(bf16[64,512]{1,0:T(8,128)(2,1)S(1)} %get-tuple-element.10), channel_id=1, source_target_pairs={{0,448},{64,0},{128,64},{192,128},{256,192},{320,256},{384,320},{4... | collective-permute-start | bytes 196616 | tf_op jit(solution)/shard_map/ppermute | solution.py:13
  36.5 7.4 %collective-permute-start.3 = (f32[1,8]{1,0:T(1,128)S(1)}, f32[1,8]{1,0:T(1,128)S(1)}, u32[]{:S(2)}, u32[]{:S(2)}) collective-permute-start(f32[1,8]{1,0:T(1,128)S(1)} %get-tuple-element.17), channel_id=1, source_target_pairs={{0,64},{64,128},{128,192},{192,256},{256,320},{320,384},{384,448},... | collective-permute-start | bytes 104 | tf_op jit(solution)/shard_map/ppermute | solution.py:13
  38.5 6.2 %collective-permute-start.2 = (f32[1,8]{1,0:T(1,128)S(1)}, f32[1,8]{1,0:T(1,128)S(1)}, u32[]{:S(2)}, u32[]{:S(2)}) collective-permute-start(f32[1,8]{1,0:T(1,128)S(1)} %get-tuple-element.16), channel_id=1, source_target_pairs={{0,448},{64,0},{128,64},{192,128},{256,192},{320,256},{384,320},{4... | collective-permute-start | bytes 104 | tf_op jit(solution)/shard_map/ppermute | solution.py:13
  45.1 6.5 %copy-start.1 = (bf16[1,3584,128]{2,1,0:T(8,128)(2,1)S(1)}, bf16[1,3584,128]{2,1,0:T(8,128)(2,1)}, u32[]{:S(2)}) copy-start(bf16[1,3584,128]{2,1,0:T(8,128)(2,1)} %param.22) | copy-start | bytes 2752516
  45.2 6.7 %copy-start.2 = (bf16[1,3584,128]{2,1,0:T(8,128)(2,1)S(1)}, bf16[1,3584,128]{2,1,0:T(8,128)(2,1)}, u32[]{:S(2)}) copy-start(bf16[1,3584,128]{2,1,0:T(8,128)(2,1)} %param.21) | copy-start | bytes 2752516
  45.2 5.6 %collective-permute-start.4 = (bf16[64,3584]{1,0:T(8,128)(2,1)S(1)}, bf16[64,3584]{1,0:T(8,128)(2,1)S(1)}, u32[]{:S(2)}, u32[]{:S(2)}) collective-permute-start(bf16[64,3584]{1,0:T(8,128)(2,1)S(1)} %bitcast.74), channel_id=1, source_target_pairs={{0,1},{1,0},{2,3},{3,2},{4,5},{5,4},{6,7},{7,6},{8,9},{9,8},{10,11... | collective-permute-start | bytes 1376264 | tf_op jit(solution)/shard_map/ppermute | solution.py:90
  50.8 0.8 copy-start.3
  54.3 4.0 %collective-permute-start.5 = (bf16[64,3584]{1,0:T(8,128)(2,1)}, bf16[64,3584]{1,0:T(8,128)(2,1)}, u32[]{:S(2)}, u32[]{:S(2)}) collective-permute-start(bf16[64,3584]{1,0:T(8,128)(2,1)} %convolution_convert_fusion), channel_id=1, source_target_pairs={{0,1},{1,0},{2,3},{3,2},{4,5},{5,4},{6,7},{7,6},{8,9},{9,8},{10,11... | collective-permute-start | bytes 1376264 | tf_op jit(solution)/shard_map/ppermute | solution.py:100
  61.7 30.0 %all-to-all-start.1 = ((bf16[64,2,1792]{2,1,0:T(2,128)(2,1)}), bf16[64,2,1792]{2,1,0:T(2,128)(2,1)S(1)}, u32[]{:S(2)}, u32[]{:S(2)}) async-start(bf16[64,2,1792]{2,1,0:T(2,128)(2,1)} %reshape.188), calls=%async_computation.1 | async-start | bytes 917504 | tf_op jit(solution)/shard_map/all_to_all | solution.py:101
  96.0 8.6 %collective-permute-start.7 = (bf16[3584]{0:T(1024)(128)(2,1)S(1)}, bf16[3584]{0:T(1024)(128)(2,1)S(1)}, u32[]{:S(2)}, u32[]{:S(2)}) collective-permute-start(bf16[3584]{0:T(1024)(128)(2,1)S(1)} %get-tuple-element.13), channel_id=1, source_target_pairs={{0,448},{64,0},{128,64},{192,128},{256,192},{320,256},{384,320},{4... | collective-permute-start | bytes 21512 | tf_op jit(solution)/shard_map/ppermute | solution.py:13
  101.9 6.5 %collective-permute-start.6 = (bf16[3584]{0:T(1024)(128)(2,1)S(1)}, bf16[3584]{0:T(1024)(128)(2,1)S(1)}, u32[]{:S(2)}, u32[]{:S(2)}) collective-permute-start(bf16[3584]{0:T(1024)(128)(2,1)S(1)} %get-tuple-element.12), channel_id=1, source_target_pairs={{0,64},{64,128},{128,192},{192,256},{256,320},{320,384},{384,448},... | collective-permute-start | bytes 21512 | tf_op jit(solution)/shard_map/ppermute | solution.py:13

commit v3 on v2

--- a/solution.py
+++ b/solution.py
@@ -1,6 +1,8 @@
 import jax
 import jax.numpy as jnp
 from jax import lax
+from jax.experimental import pallas as pl
+from jax.experimental.pallas import tpu as pltpu
 from jax.sharding import PartitionSpec as P
 
 VDIM = 512
@@ -26,6 +28,44 @@
     return out.astype(jnp.bfloat16)
 
 
+def columns_of(ref, which, size):
+    return ref[:, pl.ds(pl.multiple_of(which * size, 128), size)]
+
+
+def dot(left, right):
+    return jnp.dot(left, right, preferred_element_type=jnp.float32)
+
+
+def experts_kernel(core, x, gain, w_gate, w_up, w_down, act, part):
+    rows, half = x.shape[0] // 2, x.shape[1]
+    low = x[:rows].astype(jnp.float32)
+    high = x[rows:].astype(jnp.float32)
+    square = jnp.sum(low * low, axis=1, keepdims=True) + jnp.sum(high * high, axis=1, keepdims=True)
+    scale = lax.rsqrt(square / (2 * half) + 1e-06)
+    low = (low * scale * gain[:, :half]).astype(jnp.bfloat16)
+    high = (high * scale * gain[:, half:]).astype(jnp.bfloat16)
+    gate = dot(low, w_gate[:half]) + dot(high, w_gate[half:])
+    upper = dot(low, w_up[:half]) + dot(high, w_up[half:])
+    hidden_units = (jax.nn.silu(gate) * upper).astype(jnp.bfloat16)
+    act[...] = hidden_units
+    part[...] = dot(hidden_units, columns_of(w_down, 1 - core[0], half)).astype(jnp.bfloat16)
+
+
+def join_kernel(core, act, other, w_down, pair):
+    half = other.shape[1]
+    mine = dot(act[...], columns_of(w_down, core[0], half))
+    pair[...] = (mine + other[...].astype(jnp.float32)).astype(jnp.bfloat16)
+
+
+def in_vmem(count):
+    return [pl.BlockSpec(memory_space=pltpu.SMEM)] + [
+        pl.BlockSpec(memory_space=pltpu.VMEM) for _ in range(count)
+    ]
+
+
+LIMIT = pltpu.CompilerParams(vmem_limit_bytes=24 * 1024 * 1024)
+
+
 def body(
     latent_cache,
     page_table,
@@ -49,17 +89,6 @@
     devices = lax.axis_size("ep")
     experts_here = devices // SLICES
 
-    onehot = (
-        expert_ids[0, 0][:, :, None] == jnp.arange(experts_here, dtype=jnp.int32)
-    ).astype(jnp.float32)
-    mix = jnp.einsum("sk,skx->sx", expert_gates[0, 0], onehot, precision=lax.Precision.HIGHEST)
-    mix_next = passed_along(mix[requests : requests + 1], "grp", -1)
-    mix_prev = passed_along(mix[requests + 1 : requests + 2], "grp", 1)
-    at = moves[:, None]
-    mix_home = jnp.where(
-        at == 0, mix[:requests], jnp.where(at == 1, mix_next, mix_prev)
-    )
-
     keys = pool[table.reshape(-1)].reshape(requests, table.shape[1] * pool.shape[1], pool.shape[2])
     attn = attend_rows(query[0, 0], keys, lengths[0, 0])
 
@@ -75,36 +104,64 @@
     attn_prev = passed_along(picked(1, attn), "grp", 1)
     attn_next = passed_along(picked(2, attn), "grp", -1)
 
-    wide = rows.astype(jnp.float32)
-    normed = (
-        wide * lax.rsqrt(jnp.mean(wide * wide, axis=-1, keepdims=True) + 1e-06) * norm_gain
-    ).astype(jnp.bfloat16)
-    chips = devices // requests
-    outgoing = jnp.broadcast_to(normed[None], (chips, requests, width)).reshape(devices, 1, width)
+    cores = 2
+    half = width // cores
+    chips = devices // cores
+    halves = rows.reshape(requests, cores, half).transpose(1, 0, 2)
+    outgoing = jnp.broadcast_to(halves[None], (chips, cores, requests, half)).reshape(
+        devices, requests, half
+    )
     received = lax.all_to_all(outgoing, "ep", split_axis=0, concat_axis=0, tiled=True)
-    received, attn_prev, attn_next, mix_home = lax.optimization_barrier(
-        (received, attn_prev, attn_next, mix_home)
+    received, attn_prev, attn_next = lax.optimization_barrier((received, attn_prev, attn_next))
+    pairs = [[cores * i + j for j in range(cores)] for i in range(chips)]
+    swap = [(i, i ^ 1) for i in range(devices)]
+    count = devices * requests
+    x = lax.all_gather(
+        received.reshape(count, half), "ep", axis_index_groups=pairs, axis=0, tiled=True
     )
-    swap = [(i, i ^ 1) for i in range(devices)]
-    mine = received.reshape(devices, width)
-    theirs = lax.ppermute(mine, "ep", swap)
+    core = (lax.axis_index("ep") % cores).astype(jnp.int32).reshape(1)
+    w_down = down_weight[0]
+    act, part = pl.pallas_call(
+        experts_kernel,
+        out_shape=(
+            jax.ShapeDtypeStruct((count, w_down.shape[0]), jnp.bfloat16),
+            jax.ShapeDtypeStruct((count, half), jnp.bfloat16),
+        ),
+        in_specs=in_vmem(5),
+        out_specs=tuple(in_vmem(2)[1:]),
+        compiler_params=LIMIT,
+    )(core, x, norm_gain[None, :], gate_weight[0], up_weight[0], w_down)
+    other = lax.ppermute(part, "ep", swap)
+    pair = pl.pallas_call(
+        join_kernel,
+        out_shape=jax.ShapeDtypeStruct((count, half), jnp.bfloat16),
+        in_specs=in_vmem(3),
+        out_specs=in_vmem(1)[1],
+        compiler_params=LIMIT,
+    )(core, act, other, w_down)
+    returned = lax.all_to_all(
+        pair.reshape(devices, requests, half), "ep", split_axis=0, concat_axis=0, tiled=True
+    )
 
-    def experts(values):
-        gate = jnp.dot(values, gate_weight[0], preferred_element_type=jnp.float32)
-        upper = jnp.dot(values, up_weight[0], preferred_element_type=jnp.float32)
-        act = (jax.nn.silu(gate) * upper).astype(jnp.bfloat16)
-        return jnp.dot(act, down_weight[0], preferred_element_type=jnp.float32)
+    ids, gates, _ = lax.optimization_barrier((expert_ids[0, 0], expert_gates[0, 0], pair))
+    onehot = (
+        ids[:, :, None] == jnp.arange(experts_here, dtype=jnp.int32)
+    ).astype(jnp.float32)
+    mix = jnp.einsum("sk,skx->sx", gates, onehot, precision=lax.Precision.HIGHEST)
+    mix_next = passed_along(mix[requests : requests + 1], "grp", -1)
+    mix_prev = passed_along(mix[requests + 1 : requests + 2], "grp", 1)
+    at = moves[:, None]
+    mix_home = jnp.where(
+        at == 0, mix[:requests], jnp.where(at == 1, mix_next, mix_prev)
+    )
 
-    part_theirs = experts(theirs).astype(jnp.bfloat16)
-    part_mine = experts(mine)
-    pair = (part_mine + lax.ppermute(part_theirs, "ep", swap).astype(jnp.float32)).astype(jnp.bfloat16)
-    returned = lax.all_to_all(
-        pair.reshape(devices, 1, width), "ep", split_axis=0, concat_axis=0, tiled=True
+
+    per_expert = jnp.sum(
+        returned.reshape(experts_here, SLICES // cores, cores, requests, half).astype(jnp.float32),
+        axis=1,
     )
-    summed = jnp.sum(
-        returned.reshape(experts_here, SLICES // requests, requests, width).astype(jnp.float32), axis=1
-    )
-    moe = jnp.sum(summed * mix_home.T[:, :, None], axis=0).astype(jnp.bfloat16)
+    mixed = jnp.sum(per_expert * mix_home.T[:, None, :, None], axis=0)
+    moe = mixed.transpose(1, 0, 2).reshape(requests, width).astype(jnp.bfloat16)
     moe_prev = passed_along(picked(1, moe), "grp", 1)
     moe_next = passed_along(picked(2, moe), "grp", -1)
     return (

time: 110 us -> 86.4 us (0.79)
  starting transfers between devices: 59.5 us -> 49.1 us
  other arithmetic: 11.2 us -> 2.55 us
  matrix products: 5.37 us -> 0.82 us
  blocking collectives: 0 us -> 2.71 us
  waiting for transfers between devices: 24.7 us -> 22.5 us
  local copies, waits for them, and re-layouts: 7.44 us -> 5.91 us
  Pallas kernels: 0 us -> 1.41 us
    all_to_all x1, waiting for transfers between devices: 17.2 us -> 6.77 us  [body(): lax.all_to_all(pair.reshape(devices, requests, half), 'ep', split_axis=0,...]
    ppermute x6, waiting for transfers between devices: 4.52 us -> 14.3 us  [passed_along(): lax.ppermute(shard, axis, [(i, (i + by) % length) for i in range(length)])]
    ppermute x6, starting transfers between devices: 22.6 us -> 17.8 us  [passed_along(): lax.ppermute(shard, axis, [(i, (i + by) % length) for i in range(length)])]
    dot_general x5 -> x1, matrix products: 4.74 us -> 0.2 us  [body(): jnp.einsum('sk,skx->sx', gates, onehot, precision=lax.Precision.HIGHEST)]
    reshape x2 -> x0, other arithmetic: 4.31 us -> none  [the longest x1 3.39 us: body(): jnp.broadcast_to(normed[None], (chips, requests, width))]
    ppermute x2 -> x1, starting transfers between devices: 6.45 us -> 2.29 us  [body(): other = lax.ppermute(part, 'ep', swap)]
    convert_element_type x2 -> x0, other arithmetic: 3.38 us -> none  [the longest x1 2.57 us: body(): returned.reshape(experts_here, SLICES // requests, requests, width)]
    all_gather x0 -> x1, blocking collectives: none -> 2.71 us  [body(): lax.all_gather(received.reshape(count, half), 'ep', axis_index_groups=pai...]
  transfers between devices with their start and end apart: 10 -> 9, of which waited for: 5 -> 6; matrix products, arithmetic and copies ran while one was open for 3% -> 3% of each run, Pallas kernels for 0% -> 0%
where the time goes in v3:
time: 86.4 us; the launch traced here: 85.9 us
  starting transfers between devices  49.1 us (57%)
  waiting for transfers between devices  22.5 us (26%)
  local copies, waits for them, and re-layouts  5.91 us (7%)
  blocking collectives  2.71 us (3%)
  other arithmetic  2.55 us (3%)
  Pallas kernels  1.41 us (2%)
  between operations  0.9 us (1%)
    ppermute x6, starting transfers between devices, passed_along(): lax.ppermute(shard, axis, [(i, (i + by) % length) for i in range(length)])  17.8 us
    all_to_all x1, starting transfers between devices, body(): lax.all_to_all(outgoing, 'ep', split_axis=0, concat_axis=0, tiled=True)  17.8 us
    ppermute x6, waiting for transfers between devices, passed_along(): lax.ppermute(shard, axis, [(i, (i + by) % length) for i in range(length)])  14.3 us
    all_to_all x1, starting transfers between devices, body(): lax.all_to_all(pair.reshape(devices, requests, half), 'ep', split_axis=0,...  11.3 us
    all_to_all x1, waiting for transfers between devices, body(): lax.all_to_all(pair.reshape(devices, requests, half), 'ep', split_axis=0,...  6.77 us
    all_gather x1, blocking collectives, body(): lax.all_gather(received.reshape(count, half), 'ep', axis_index_groups=pai...  2.71 us
    ppermute x1, starting transfers between devices, body(): other = lax.ppermute(part, 'ep', swap)  2.29 us
    unnamed x22, local copies, waits for them, and re-layouts  2.14 us
  transfers between devices with their start and end apart: 9, of which 6 were waited for; matrix products, arithmetic and copies ran while one was open for 3% of the time, Pallas kernels for 0%

profile of v3, /device:TPU:1, one launch (start us, length us, event | category | flops | bytes accessed | tf_op | source)
XLA Modules:
  0.0 85.9 jit_solution(8091917132280900936)
XLA Ops:
  0.6 0.8 reshape_squeeze.7
  1.4 1.0 %broadcast_in_dim.121 = bf16[32,2,2,1792]{3,2,1,0:T(2,128)(2,1)} broadcast(bf16[2,2,1792]{2,1,0:T(2,128)(2,1)S(1)} %copy.20), dimensions={1,2,3} | broadcast | bytes 473088 | tf_op jit(solution)/shard_map/broadcast_in_dim | solution.py:111
  2.4 17.8 %all-to-all-start = ((bf16[64,2,1792]{2,1,0:T(2,128)(2,1)}), bf16[64,2,1792]{2,1,0:T(2,128)(2,1)S(1)}, u32[]{:S(2)}, u32[]{:S(2)}) async-start(bf16[64,2,1792]{2,1,0:T(2,128)(2,1)} %bitcast.8), calls=%async_computation | async-start | bytes 917504 | tf_op jit(solution)/shard_map/all_to_all | solution.py:114
  20.3 0.7 copy-done.10
  21.1 0.6 gather_fusion
  21.7 0.3 copy-done.4
  22.0 0.3 fusion.4
  22.4 0.5 copy-done.6
  22.9 0.4 select_reduce_fusion
  23.3 5.3 %collective-permute-start.1 = (bf16[64,512]{1,0:T(8,128)(2,1)S(1)}, bf16[64,512]{1,0:T(8,128)(2,1)S(1)}, u32[]{:S(2)}, u32[]{:S(2)}) collective-permute-start(bf16[64,512]{1,0:T(8,128)(2,1)S(1)} %get-tuple-element.16), channel_id=1, source_target_pairs={{0,448},{64,0},{128,64},{192,128},{256,192},{320,256},{384,320},{4... | collective-permute-start | bytes 196616 | tf_op jit(solution)/shard_map/ppermute | solution.py:15
  28.6 1.9 %collective-permute-start = (bf16[64,512]{1,0:T(8,128)(2,1)S(1)}, bf16[64,512]{1,0:T(8,128)(2,1)S(1)}, u32[]{:S(2)}, u32[]{:S(2)}) collective-permute-start(bf16[64,512]{1,0:T(8,128)(2,1)S(1)} %get-tuple-element.17), channel_id=1, source_target_pairs={{0,64},{64,128},{128,192},{192,256},{256,320},{320,384},{384,448},... | collective-permute-start | bytes 196616 | tf_op jit(solution)/shard_map/ppermute | solution.py:15
  30.6 3.9 %collective-permute-done.1 = bf16[64,512]{1,0:T(8,128)(2,1)S(1)} collective-permute-done((bf16[64,512]{1,0:T(8,128)(2,1)S(1)}, bf16[64,512]{1,0:T(8,128)(2,1)S(1)}, u32[]{:S(2)}, u32[]{:S(2)}) %collective-permute-start.1) | collective-permute-done | bytes 65568 | tf_op jit(solution)/shard_map/ppermute | solution.py:15
  34.5 4.0 %collective-permute-done = bf16[64,512]{1,0:T(8,128)(2,1)S(1)} collective-permute-done((bf16[64,512]{1,0:T(8,128)(2,1)S(1)}, bf16[64,512]{1,0:T(8,128)(2,1)S(1)}, u32[]{:S(2)}, u32[]{:S(2)}) %collective-permute-start) | collective-permute-done | bytes 65568 | tf_op jit(solution)/shard_map/ppermute | solution.py:15
  38.7 2.7 %all_gather.3.x = bf16[256,1792]{1,0:T(8,128)(2,1)S(1)} all-gather(bf16[128,1792]{1,0:T(8,128)(2,1)S(1)} %reshape.144), channel_id=1, replica_groups={{0,1},{2,3},{4,5},{6,7},{8,9},{10,11},{12,13},{14,15},{16,17},{18,19},{..., dimensions={0}, use_global_device_ids=true | all-gather | bytes 1376256 | tf_op jit(solution)/shard_map/all_gather | solution.py:119
  41.4 1.1 %shard_map.131 = (bf16[128,128]{1,0:T(8,128)(2,1)S(1)}, bf16[128,1792]{1,0:T(8,128)(2,1)S(1)}) custom-call(s32[1]{0:T(128)} %bitcast.14.core, bf16[256,1792]{1,0:T(8,128)(2,1)S(1)} %all_gather.3.x, f32[1,3584]{1,0:T(1,128)S(1)} %broadcast_in_dim.128.gain, bf16[3584,128]{1,0:T(8,128)(2,1)S(1)} %bitcast.51, bf16[3584,128]{1,0:T(8,128)(2,1)S(1)} %bitcast.52, ...), custom_call_target="tpu_custom_call" | custom-call | tf_op jit(solution)/shard_map/pallas_call | solution.py:124
  42.5 2.3 %collective-permute-start.2 = (bf16[128,1792]{1,0:T(8,128)(2,1)S(1)}, bf16[128,1792]{1,0:T(8,128)(2,1)S(1)}, u32[]{:S(2)}, u32[]{:S(2)}) collective-permute-start(bf16[128,1792]{1,0:T(8,128)(2,1)S(1)} %get-tuple-element.13), channel_id=1, source_target_pairs={{0,1},{1,0},{2,3},{3,2},{4,5},{5,4},{6,7},{7,6},{8,9},{9,8},{10,11... | collective-permute-start | bytes 1376264 | tf_op jit(solution)/shard_map/ppermute | solution.py:134
  44.8 1.4 %collective-permute-done.2.other = bf16[128,1792]{1,0:T(8,128)(2,1)S(1)} collective-permute-done((bf16[128,1792]{1,0:T(8,128)(2,1)S(1)}, bf16[128,1792]{1,0:T(8,128)(2,1)S(1)}, u32[]{:S(2)}, u32[]{:S(2)}) %collective-permute-start.2) | collective-permute-done | bytes 458784 | tf_op jit(solution)/shard_map/ppermute | solution.py:134
  46.3 0.3 shard_map.132
  46.5 0.9 %reshape.145 = bf16[64,2,1792]{2,1,0:T(2,128)(2,1)} reshape(bf16[128,1792]{1,0:T(8,128)(2,1)S(1)} %shard_map.132) | data formatting | bytes 917504 | tf_op jit(solution)/shard_map/reshape | solution.py:143
  47.5 11.3 %all-to-all-start.1 = ((bf16[64,2,1792]{2,1,0:T(2,128)(2,1)}), bf16[64,2,1792]{2,1,0:T(2,128)(2,1)S(1)}, u32[]{:S(2)}, u32[]{:S(2)}) async-start(bf16[64,2,1792]{2,1,0:T(2,128)(2,1)} %reshape.145), calls=%async_computation.1 | async-start | bytes 917504 | tf_op jit(solution)/shard_map/all_to_all | solution.py:142
  58.8 0.7 maximum_bitcast_fusion
  59.5 0.7 copy-done.7
  60.2 0.2 fusion.8
  60.4 1.9 %collective-permute-start.3 = (f32[1,8]{1,0:T(1,128)S(1)}, f32[1,8]{1,0:T(1,128)S(1)}, u32[]{:S(2)}, u32[]{:S(2)}) collective-permute-start(f32[1,8]{1,0:T(1,128)S(1)} %get-tuple-element.21), channel_id=1, source_target_pairs={{0,448},{64,0},{128,64},{192,128},{256,192},{320,256},{384,320},{4... | collective-permute-start | bytes 104 | tf_op jit(solution)/shard_map/ppermute | solution.py:15
  62.3 3.4 %collective-permute-start.4 = (f32[1,8]{1,0:T(1,128)S(1)}, f32[1,8]{1,0:T(1,128)S(1)}, u32[]{:S(2)}, u32[]{:S(2)}) collective-permute-start(f32[1,8]{1,0:T(1,128)S(1)} %get-tuple-element.22), channel_id=1, source_target_pairs={{0,64},{64,128},{128,192},{192,256},{256,320},{320,384},{384,448},... | collective-permute-start | bytes 104 | tf_op jit(solution)/shard_map/ppermute | solution.py:15
  65.7 3.4 %collective-permute-done.4 = f32[1,8]{1,0:T(1,128)S(1)} collective-permute-done((f32[1,8]{1,0:T(1,128)S(1)}, f32[1,8]{1,0:T(1,128)S(1)}, u32[]{:S(2)}, u32[]{:S(2)}) %collective-permute-start.4) | collective-permute-done | bytes 64 | tf_op jit(solution)/shard_map/ppermute | solution.py:15
  69.2 6.8 %all-to-all-done.1 = bf16[64,2,1792]{2,1,0:T(2,128)(2,1)S(1)} async-done(((bf16[64,2,1792]{2,1,0:T(2,128)(2,1)}), bf16[64,2,1792]{2,1,0:T(2,128)(2,1)S(1)}, u32[]{:S(2)}, u32[]{:S(2)}) %all-to-all-start.1) | async-done | bytes 458784 | tf_op jit(solution)/shard_map/all_to_all | solution.py:142
  76.0 0.4 convert_reduce_fusion
  76.8 1.9 %collective-permute-start.6 = (bf16[3584]{0:T(1024)(128)(2,1)S(1)}, bf16[3584]{0:T(1024)(128)(2,1)S(1)}, u32[]{:S(2)}, u32[]{:S(2)}) collective-permute-start(bf16[3584]{0:T(1024)(128)(2,1)S(1)} %reduce_sum.75), channel_id=1, source_target_pairs={{0,448},{64,0},{128,64},{192,128},{256,192},{320,256},{384,320},{4... | collective-permute-start | bytes 21512 | tf_op jit(solution)/shard_map/ppermute | solution.py:15
  78.7 3.4 %collective-permute-start.5 = (bf16[3584]{0:T(1024)(128)(2,1)S(1)}, bf16[3584]{0:T(1024)(128)(2,1)S(1)}, u32[]{:S(2)}, u32[]{:S(2)}) collective-permute-start(bf16[3584]{0:T(1024)(128)(2,1)S(1)} %reduce_sum.73), channel_id=1, source_target_pairs={{0,64},{64,128},{128,192},{192,256},{256,320},{320,384},{384,448},... | collective-permute-start | bytes 21512 | tf_op jit(solution)/shard_map/ppermute | solution.py:15
  82.2 3.0 %collective-permute-done.5 = bf16[3584]{0:T(1024)(128)(2,1)S(1)} collective-permute-done((bf16[3584]{0:T(1024)(128)(2,1)S(1)}, bf16[3584]{0:T(1024)(128)(2,1)S(1)}, u32[]{:S(2)}, u32[]{:S(2)}) %collective-permute-start.5) | collective-permute-done | bytes 7200 | tf_op jit(solution)/shard_map/ppermute | solution.py:15
  85.2 0.7 maximum_bitcast_fusion.1
  (40 shorter events, 1.2 us)
Async XLA Ops:
  0.6 20.4 %copy-start = (bf16[1,1,4,64,576]{4,3,2,1,0:T(8,128)(2,1)S(1)}, bf16[1,1,4,64,576]{4,3,2,1,0:T(8,128)(2,1)}, u32[]{:S(2)}) copy-start(bf16[1,1,4,64,576]{4,3,2,1,0:T(8,128)(2,1)} %param.12) | copy-start | bytes 884740
  2.4 17.8 %copy-start.9 = (s32[1,1,2,2]{3,2,1,0:T(2,128)S(1)}, s32[1,1,2,2]{3,2,1,0:T(2,128)}, u32[]{:S(2)}) copy-start(s32[1,1,2,2]{3,2,1,0:T(2,128)} %param.13) | copy-start | bytes 52
  2.4 36.0 %all-to-all-start = ((bf16[64,2,1792]{2,1,0:T(2,128)(2,1)}), bf16[64,2,1792]{2,1,0:T(2,128)(2,1)S(1)}, u32[]{:S(2)}, u32[]{:S(2)}) async-start(bf16[64,2,1792]{2,1,0:T(2,128)(2,1)} %bitcast.8), calls=%async_computation | async-start | bytes 917504 | tf_op jit(solution)/shard_map/all_to_all | solution.py:114
  20.3 0.7 copy-start.10
  21.1 0.9 %copy-start.4 = (bf16[1,1,2,64,576]{4,3,2,1,0:T(8,128)(2,1)S(1)}, bf16[1,1,2,64,576]{4,3,2,1,0:T(8,128)(2,1)}, u32[]{:S(2)}) copy-start(bf16[1,1,2,64,576]{4,3,2,1,0:T(8,128)(2,1)} %param.16) | copy-start | bytes 442372
  22.2 0.7 copy-start.6
  22.9 18.5 %copy-start.3 = (bf16[1,3584,128]{2,1,0:T(8,128)(2,1)S(1)}, bf16[1,3584,128]{2,1,0:T(8,128)(2,1)}, u32[]{:S(2)}) copy-start(bf16[1,3584,128]{2,1,0:T(8,128)(2,1)} %param.22) | copy-start | bytes 2752516
  23.3 7.3 %copy-start.5 = (f32[3584]{0:T(1024)S(1)}, f32[3584]{0:T(1024)}, u32[]{:S(2)}) copy-start(f32[3584]{0:T(1024)} %param.18) | copy-start | bytes 43012
  23.3 11.2 %collective-permute-start.1 = (bf16[64,512]{1,0:T(8,128)(2,1)S(1)}, bf16[64,512]{1,0:T(8,128)(2,1)S(1)}, u32[]{:S(2)}, u32[]{:S(2)}) collective-permute-start(bf16[64,512]{1,0:T(8,128)(2,1)S(1)} %get-tuple-element.16), channel_id=1, source_target_pairs={{0,448},{64,0},{128,64},{192,128},{256,192},{320,256},{384,320},{4... | collective-permute-start | bytes 196616 | tf_op jit(solution)/shard_map/ppermute | solution.py:15
  28.6 9.9 %collective-permute-start = (bf16[64,512]{1,0:T(8,128)(2,1)S(1)}, bf16[64,512]{1,0:T(8,128)(2,1)S(1)}, u32[]{:S(2)}, u32[]{:S(2)}) collective-permute-start(bf16[64,512]{1,0:T(8,128)(2,1)S(1)} %get-tuple-element.17), channel_id=1, source_target_pairs={{0,64},{64,128},{128,192},{192,256},{256,320},{320,384},{384,448},... | collective-permute-start | bytes 196616 | tf_op jit(solution)/shard_map/ppermute | solution.py:15
  38.5 2.9 %copy-start.2 = (bf16[1,3584,128]{2,1,0:T(8,128)(2,1)S(1)}, bf16[1,3584,128]{2,1,0:T(8,128)(2,1)}, u32[]{:S(2)}) copy-start(bf16[1,3584,128]{2,1,0:T(8,128)(2,1)} %param.21) | copy-start | bytes 2752516
  38.7 2.7 %copy-start.1 = (bf16[1,128,3584]{2,1,0:T(8,128)(2,1)S(1)}, bf16[1,128,3584]{2,1,0:T(8,128)(2,1)}, u32[]{:S(2)}) copy-start(bf16[1,128,3584]{2,1,0:T(8,128)(2,1)} %param.23) | copy-start | bytes 2752516
  42.5 3.7 %collective-permute-start.2 = (bf16[128,1792]{1,0:T(8,128)(2,1)S(1)}, bf16[128,1792]{1,0:T(8,128)(2,1)S(1)}, u32[]{:S(2)}, u32[]{:S(2)}) collective-permute-start(bf16[128,1792]{1,0:T(8,128)(2,1)S(1)} %get-tuple-element.13), channel_id=1, source_target_pairs={{0,1},{1,0},{2,3},{3,2},{4,5},{5,4},{6,7},{7,6},{8,9},{9,8},{10,11... | collective-permute-start | bytes 1376264 | tf_op jit(solution)/shard_map/ppermute | solution.py:134
  47.5 28.5 %all-to-all-start.1 = ((bf16[64,2,1792]{2,1,0:T(2,128)(2,1)}), bf16[64,2,1792]{2,1,0:T(2,128)(2,1)S(1)}, u32[]{:S(2)}, u32[]{:S(2)}) async-start(bf16[64,2,1792]{2,1,0:T(2,128)(2,1)} %reshape.145), calls=%async_computation.1 | async-start | bytes 917504 | tf_op jit(solution)/shard_map/all_to_all | solution.py:142
  58.7 0.8 copy-start.8
  59.5 0.7 copy-start.7
  60.4 5.3 %collective-permute-start.3 = (f32[1,8]{1,0:T(1,128)S(1)}, f32[1,8]{1,0:T(1,128)S(1)}, u32[]{:S(2)}, u32[]{:S(2)}) collective-permute-start(f32[1,8]{1,0:T(1,128)S(1)} %get-tuple-element.21), channel_id=1, source_target_pairs={{0,448},{64,0},{128,64},{192,128},{256,192},{320,256},{384,320},{4... | collective-permute-start | bytes 104 | tf_op jit(solution)/shard_map/ppermute | solution.py:15
  62.3 6.7 %collective-permute-start.4 = (f32[1,8]{1,0:T(1,128)S(1)}, f32[1,8]{1,0:T(1,128)S(1)}, u32[]{:S(2)}, u32[]{:S(2)}) collective-permute-start(f32[1,8]{1,0:T(1,128)S(1)} %get-tuple-element.22), channel_id=1, source_target_pairs={{0,64},{64,128},{128,192},{192,256},{256,320},{320,384},{384,448},... | collective-permute-start | bytes 104 | tf_op jit(solution)/shard_map/ppermute | solution.py:15
  76.8 5.4 %collective-permute-start.6 = (bf16[3584]{0:T(1024)(128)(2,1)S(1)}, bf16[3584]{0:T(1024)(128)(2,1)S(1)}, u32[]{:S(2)}, u32[]{:S(2)}) collective-permute-start(bf16[3584]{0:T(1024)(128)(2,1)S(1)} %reduce_sum.75), channel_id=1, source_target_pairs={{0,448},{64,0},{128,64},{192,128},{256,192},{320,256},{384,320},{4... | collective-permute-start | bytes 21512 | tf_op jit(solution)/shard_map/ppermute | solution.py:15
  78.7 6.5 %collective-permute-start.5 = (bf16[3584]{0:T(1024)(128)(2,1)S(1)}, bf16[3584]{0:T(1024)(128)(2,1)S(1)}, u32[]{:S(2)}, u32[]{:S(2)}) collective-permute-start(bf16[3584]{0:T(1024)(128)(2,1)S(1)} %reduce_sum.73), channel_id=1, source_target_pairs={{0,64},{64,128},{128,192},{192,256},{256,320},{320,384},{384,448},... | collective-permute-start | bytes 21512 | tf_op jit(solution)/shard_map/ppermute | solution.py:15

commit v4 on v3

--- a/solution.py
+++ b/solution.py
@@ -28,33 +28,26 @@
     return out.astype(jnp.bfloat16)
 
 
-def columns_of(ref, which, size):
-    return ref[:, pl.ds(pl.multiple_of(which * size, 128), size)]
-
-
 def dot(left, right):
     return jnp.dot(left, right, preferred_element_type=jnp.float32)
 
 
-def experts_kernel(core, x, gain, w_gate, w_up, w_down, act, part):
-    rows, half = x.shape[0] // 2, x.shape[1]
-    low = x[:rows].astype(jnp.float32)
-    high = x[rows:].astype(jnp.float32)
-    square = jnp.sum(low * low, axis=1, keepdims=True) + jnp.sum(high * high, axis=1, keepdims=True)
-    scale = lax.rsqrt(square / (2 * half) + 1e-06)
-    low = (low * scale * gain[:, :half]).astype(jnp.bfloat16)
-    high = (high * scale * gain[:, half:]).astype(jnp.bfloat16)
-    gate = dot(low, w_gate[:half]) + dot(high, w_gate[half:])
-    upper = dot(low, w_up[:half]) + dot(high, w_up[half:])
-    hidden_units = (jax.nn.silu(gate) * upper).astype(jnp.bfloat16)
-    act[...] = hidden_units
-    part[...] = dot(hidden_units, columns_of(w_down, 1 - core[0], half)).astype(jnp.bfloat16)
+def share_of(ref, which):
+    rows = ref.shape[0] // 2
+    return ref[pl.ds(pl.multiple_of(which * rows, 16), rows), :]
 
 
-def join_kernel(core, act, other, w_down, pair):
-    half = other.shape[1]
-    mine = dot(act[...], columns_of(w_down, core[0], half))
-    pair[...] = (mine + other[...].astype(jnp.float32)).astype(jnp.bfloat16)
+def experts_kernel(core, x, gain, w_gate, w_up, w_down, act, part):
+    wide = x[...].astype(jnp.float32)
+    scale = lax.rsqrt(jnp.mean(wide * wide, axis=1, keepdims=True) + 1e-06)
+    normed = (wide * scale * gain[...]).astype(jnp.bfloat16)
+    act[...] = (jax.nn.silu(dot(normed, w_gate[...])) * dot(normed, w_up[...])).astype(jnp.bfloat16)
+    part[...] = dot(share_of(act, 1 - core[0]), w_down[...]).astype(jnp.bfloat16)
+
+
+def join_kernel(core, act, parts, w_down, pair):
+    mine = dot(share_of(act, core[0]), w_down[...])
+    pair[...] = (mine + share_of(parts, 1 - core[0]).astype(jnp.float32)).astype(jnp.bfloat16)
 
 
 def in_vmem(count):
@@ -105,42 +98,45 @@
     attn_next = passed_along(picked(2, attn), "grp", -1)
 
     cores = 2
-    half = width // cores
     chips = devices // cores
-    halves = rows.reshape(requests, cores, half).transpose(1, 0, 2)
-    outgoing = jnp.broadcast_to(halves[None], (chips, cores, requests, half)).reshape(
-        devices, requests, half
+    alike = [[cores * i + j for i in range(chips)] for j in range(cores)]
+    pairs = [[cores * i + j for j in range(cores)] for i in range(chips)]
+    count = chips * requests
+    outgoing = jnp.broadcast_to(rows[None], (chips, requests, width))
+    received = lax.all_to_all(
+        outgoing, "ep", split_axis=0, concat_axis=0, axis_index_groups=alike, tiled=True
     )
-    received = lax.all_to_all(outgoing, "ep", split_axis=0, concat_axis=0, tiled=True)
     received, attn_prev, attn_next = lax.optimization_barrier((received, attn_prev, attn_next))
-    pairs = [[cores * i + j for j in range(cores)] for i in range(chips)]
-    swap = [(i, i ^ 1) for i in range(devices)]
-    count = devices * requests
     x = lax.all_gather(
-        received.reshape(count, half), "ep", axis_index_groups=pairs, axis=0, tiled=True
+        received.reshape(count, width), "ep", axis_index_groups=pairs, axis=0, tiled=True
     )
     core = (lax.axis_index("ep") % cores).astype(jnp.int32).reshape(1)
     w_down = down_weight[0]
     act, part = pl.pallas_call(
         experts_kernel,
         out_shape=(
-            jax.ShapeDtypeStruct((count, w_down.shape[0]), jnp.bfloat16),
-            jax.ShapeDtypeStruct((count, half), jnp.bfloat16),
+            jax.ShapeDtypeStruct((cores * count, w_down.shape[0]), jnp.bfloat16),
+            jax.ShapeDtypeStruct((count, width), jnp.bfloat16),
         ),
         in_specs=in_vmem(5),
         out_specs=tuple(in_vmem(2)[1:]),
         compiler_params=LIMIT,
     )(core, x, norm_gain[None, :], gate_weight[0], up_weight[0], w_down)
-    other = lax.ppermute(part, "ep", swap)
+    parts = lax.all_gather(part, "ep", axis_index_groups=pairs, axis=0, tiled=True)
     pair = pl.pallas_call(
         join_kernel,
-        out_shape=jax.ShapeDtypeStruct((count, half), jnp.bfloat16),
+        out_shape=jax.ShapeDtypeStruct((count, width), jnp.bfloat16),
         in_specs=in_vmem(3),
         out_specs=in_vmem(1)[1],
         compiler_params=LIMIT,
-    )(core, act, other, w_down)
+    )(core, act, parts, w_down)
     returned = lax.all_to_all(
-        pair.reshape(devices, requests, half), "ep", split_axis=0, concat_axis=0, tiled=True
+        pair.reshape(chips, requests, width),
+        "ep",
+        split_axis=0,
+        concat_axis=0,
+        axis_index_groups=alike,
+        tiled=True,
     )
 
     ids, gates, _ = lax.optimization_barrier((expert_ids[0, 0], expert_gates[0, 0], pair))
@@ -155,13 +151,10 @@
         at == 0, mix[:requests], jnp.where(at == 1, mix_next, mix_prev)
     )
 
-
     per_expert = jnp.sum(
-        returned.reshape(experts_here, SLICES // cores, cores, requests, half).astype(jnp.float32),
-        axis=1,
+        returned.reshape(experts_here, SLICES // cores, requests, width).astype(jnp.float32), axis=1
     )
-    mixed = jnp.sum(per_expert * mix_home.T[:, None, :, None], axis=0)
-    moe = mixed.transpose(1, 0, 2).reshape(requests, width).astype(jnp.bfloat16)
+    moe = jnp.sum(per_expert * mix_home.T[:, :, None], axis=0).astype(jnp.bfloat16)
     moe_prev = passed_along(picked(1, moe), "grp", 1)
     moe_next = passed_along(picked(2, moe), "grp", -1)
     return (

time: 86.4 us -> 86.9 us (level)
  the two profiles are of different devices: /device:TPU:1 before, /device:TPU:14 now
where the time goes in v4:
time: 86.9 us; the launch traced here: 86.2 us
  starting transfers between devices  47.1 us (54%)
  waiting for transfers between devices  22.6 us (26%)
  local copies, waits for them, and re-layouts  5.82 us (7%)
  blocking collectives  5.06 us (6%)
  other arithmetic  2.5 us (3%)
  Pallas kernels  1.44 us (2%)
  between operations  0.87 us (1%)
    ppermute x6, starting transfers between devices, passed_along(): lax.ppermute(shard, axis, [(i, (i + by) % length) for i in range(length)])  24 us
    all_to_all x1, starting transfers between devices, body(): lax.all_to_all(outgoing, 'ep', split_axis=0, concat_axis=0, axis_index_gr...  16.3 us
    all_to_all x1, waiting for transfers between devices, body(): lax.all_to_all(pair.reshape(chips, requests, width), 'ep', split_axis=0,...  8.75 us
    ppermute x6, waiting for transfers between devices, passed_along(): lax.ppermute(shard, axis, [(i, (i + by) % length) for i in range(length)])  8.48 us
    all_to_all x1, starting transfers between devices, body(): lax.all_to_all(pair.reshape(chips, requests, width), 'ep', split_axis=0,...  6.78 us
    all_to_all x1, waiting for transfers between devices, body(): lax.all_to_all(outgoing, 'ep', split_axis=0, concat_axis=0, axis_index_gr...  5.36 us
    all_gather x1, blocking collectives, body(): lax.all_gather(received.reshape(count, width), 'ep', axis_index_groups=pa...  2.59 us
    all_gather x1, blocking collectives, body(): lax.all_gather(part, 'ep', axis_index_groups=pairs, axis=0, tiled=True)  2.46 us
  transfers between devices with their start and end apart: 8, of which 5 were waited for; matrix products, arithmetic and copies ran while one was open for 3% of the time, Pallas kernels for 0%

profile of v4, /device:TPU:14, one launch (start us, length us, event | category | flops | bytes accessed | tf_op | source)
XLA Modules:
  0.0 86.2 jit_solution(6055297890873760374)
XLA Ops:
  0.6 1.8 %broadcast_in_dim.123 = bf16[32,2,3584]{2,1,0:T(2,128)(2,1)} broadcast(bf16[2,3584]{1,0:T(2,128)(2,1)} %bitcast.54), dimensions={1,2} | broadcast | bytes 473088 | tf_op jit(solution)/shard_map/broadcast_in_dim | solution.py:105
  2.4 16.3 %all-to-all-start = ((bf16[32,2,3584]{2,1,0:T(2,128)(2,1)}), bf16[32,2,3584]{2,1,0:T(2,128)(2,1)S(1)}, u32[]{:S(2)}, u32[]{:S(2)}) async-start(bf16[32,2,3584]{2,1,0:T(2,128)(2,1)} %broadcast_in_dim.123), calls=%async_computation | async-start | bytes 917504 | tf_op jit(solution)/shard_map/all_to_all | solution.py:106
  18.8 0.7 copy-done.10
  19.6 0.6 gather_fusion
  20.2 0.3 copy-done.4
  20.5 0.3 fusion.4
  20.8 0.2 fusion.15
  20.9 0.5 copy-done.6
  21.4 0.4 select_reduce_fusion
  21.8 2.7 %collective-permute-start.1 = (bf16[64,512]{1,0:T(8,128)(2,1)S(1)}, bf16[64,512]{1,0:T(8,128)(2,1)S(1)}, u32[]{:S(2)}, u32[]{:S(2)}) collective-permute-start(bf16[64,512]{1,0:T(8,128)(2,1)S(1)} %get-tuple-element.16), channel_id=1, source_target_pairs={{0,448},{64,0},{128,64},{192,128},{256,192},{320,256},{384,320},{4... | collective-permute-start | bytes 196616 | tf_op jit(solution)/shard_map/ppermute | solution.py:15
  24.5 5.2 %collective-permute-start = (bf16[64,512]{1,0:T(8,128)(2,1)S(1)}, bf16[64,512]{1,0:T(8,128)(2,1)S(1)}, u32[]{:S(2)}, u32[]{:S(2)}) collective-permute-start(bf16[64,512]{1,0:T(8,128)(2,1)S(1)} %get-tuple-element.17), channel_id=1, source_target_pairs={{0,64},{64,128},{128,192},{192,256},{256,320},{320,384},{384,448},... | collective-permute-start | bytes 196616 | tf_op jit(solution)/shard_map/ppermute | solution.py:15
  29.8 2.2 %collective-permute-done.1 = bf16[64,512]{1,0:T(8,128)(2,1)S(1)} collective-permute-done((bf16[64,512]{1,0:T(8,128)(2,1)S(1)}, bf16[64,512]{1,0:T(8,128)(2,1)S(1)}, u32[]{:S(2)}, u32[]{:S(2)}) %collective-permute-start.1) | collective-permute-done | bytes 65568 | tf_op jit(solution)/shard_map/ppermute | solution.py:15
  32.0 5.4 %all-to-all-done = bf16[32,2,3584]{2,1,0:T(2,128)(2,1)S(1)} async-done(((bf16[32,2,3584]{2,1,0:T(2,128)(2,1)}), bf16[32,2,3584]{2,1,0:T(2,128)(2,1)S(1)}, u32[]{:S(2)}, u32[]{:S(2)}) %all-to-all-start) | async-done | bytes 458784 | tf_op jit(solution)/shard_map/all_to_all | solution.py:106
  37.4 0.2 reshape.126
  37.6 2.6 %all_gather.6.x = bf16[128,3584]{1,0:T(8,128)(2,1)S(1)} all-gather(bf16[64,3584]{1,0:T(8,128)(2,1)S(1)} %reshape.126), channel_id=1, replica_groups={{0,1},{2,3},{4,5},{6,7},{8,9},{10,11},{12,13},{14,15},{16,17},{18,19},{..., dimensions={0}, use_global_device_ids=true | all-gather | bytes 1376256 | tf_op jit(solution)/shard_map/all_gather | solution.py:110
  40.2 1.2 %shard_map.131 = (bf16[128,128]{1,0:T(8,128)(2,1)S(1)}, bf16[64,3584]{1,0:T(8,128)(2,1)S(1)}) custom-call(s32[1]{0:T(128)} %bitcast.13.core, bf16[128,3584]{1,0:T(8,128)(2,1)S(1)} %all_gather.6.x, f32[1,3584]{1,0:T(1,128)S(1)} %broadcast_in_dim.130.gain, bf16[3584,128]{1,0:T(8,128)(2,1)S(1)} %bitcast.48, bf16[3584,128]{1,0:T(8,128)(2,1)S(1)} %bitcast.49, ...), custom_call_target="tpu_custom_call" | custom-call | tf_op jit(solution)/shard_map/pallas_call | solution.py:115
  41.4 2.5 %all_gather.7.parts = bf16[128,3584]{1,0:T(8,128)(2,1)S(1)} all-gather(bf16[64,3584]{1,0:T(8,128)(2,1)S(1)} %get-tuple-element.13), channel_id=1, replica_groups={{0,1},{2,3},{4,5},{6,7},{8,9},{10,11},{12,13},{14,15},{16,17},{18,19},{..., dimensions={0}, use_global_device_ids=true | all-gather | bytes 1376256 | tf_op jit(solution)/shard_map/all_gather | solution.py:125
  43.8 0.3 shard_map.132
  44.1 0.9 %reshape.127 = bf16[32,2,3584]{2,1,0:T(2,128)(2,1)} reshape(bf16[64,3584]{1,0:T(8,128)(2,1)S(1)} %shard_map.132) | data formatting | bytes 917504 | tf_op jit(solution)/shard_map/reshape | solution.py:134
  45.1 6.8 %all-to-all-start.1 = ((bf16[32,2,3584]{2,1,0:T(2,128)(2,1)}), bf16[32,2,3584]{2,1,0:T(2,128)(2,1)S(1)}, u32[]{:S(2)}, u32[]{:S(2)}) async-start(bf16[32,2,3584]{2,1,0:T(2,128)(2,1)} %reshape.127), calls=%async_computation.1 | async-start | bytes 917504 | tf_op jit(solution)/shard_map/all_to_all | solution.py:133
  51.9 0.7 copy-done.7
  52.5 0.2 fusion.8
  52.8 1.9 %collective-permute-start.2 = (f32[1,8]{1,0:T(1,128)S(1)}, f32[1,8]{1,0:T(1,128)S(1)}, u32[]{:S(2)}, u32[]{:S(2)}) collective-permute-start(f32[1,8]{1,0:T(1,128)S(1)} %get-tuple-element.22), channel_id=1, source_target_pairs={{0,448},{64,0},{128,64},{192,128},{256,192},{320,256},{384,320},{4... | collective-permute-start | bytes 104 | tf_op jit(solution)/shard_map/ppermute | solution.py:15
  54.7 6.1 %collective-permute-start.3 = (f32[1,8]{1,0:T(1,128)S(1)}, f32[1,8]{1,0:T(1,128)S(1)}, u32[]{:S(2)}, u32[]{:S(2)}) collective-permute-start(f32[1,8]{1,0:T(1,128)S(1)} %get-tuple-element.23), channel_id=1, source_target_pairs={{0,64},{64,128},{128,192},{192,256},{256,320},{320,384},{384,448},... | collective-permute-start | bytes 104 | tf_op jit(solution)/shard_map/ppermute | solution.py:15
  60.8 1.3 %collective-permute-done.3 = f32[1,8]{1,0:T(1,128)S(1)} collective-permute-done((f32[1,8]{1,0:T(1,128)S(1)}, f32[1,8]{1,0:T(1,128)S(1)}, u32[]{:S(2)}, u32[]{:S(2)}) %collective-permute-start.3) | collective-permute-done | bytes 64 | tf_op jit(solution)/shard_map/ppermute | solution.py:15
  62.3 8.7 %all-to-all-done.1 = bf16[32,2,3584]{2,1,0:T(2,128)(2,1)S(1)} async-done(((bf16[32,2,3584]{2,1,0:T(2,128)(2,1)}), bf16[32,2,3584]{2,1,0:T(2,128)(2,1)S(1)}, u32[]{:S(2)}, u32[]{:S(2)}) %all-to-all-start.1) | async-done | bytes 458784 | tf_op jit(solution)/shard_map/all_to_all | solution.py:133
  71.0 0.4 convert_reduce_fusion
  71.8 6.1 %collective-permute-start.4 = (bf16[3584]{0:T(1024)(128)(2,1)S(1)}, bf16[3584]{0:T(1024)(128)(2,1)S(1)}, u32[]{:S(2)}, u32[]{:S(2)}) collective-permute-start(bf16[3584]{0:T(1024)(128)(2,1)S(1)} %get-tuple-element.18), channel_id=1, source_target_pairs={{0,64},{64,128},{128,192},{192,256},{256,320},{320,384},{384,448},... | collective-permute-start | bytes 21512 | tf_op jit(solution)/shard_map/ppermute | solution.py:15
  77.9 1.9 %collective-permute-start.5 = (bf16[3584]{0:T(1024)(128)(2,1)S(1)}, bf16[3584]{0:T(1024)(128)(2,1)S(1)}, u32[]{:S(2)}, u32[]{:S(2)}) collective-permute-start(bf16[3584]{0:T(1024)(128)(2,1)S(1)} %get-tuple-element.19), channel_id=1, source_target_pairs={{0,448},{64,0},{128,64},{192,128},{256,192},{320,256},{384,320},{4... | collective-permute-start | bytes 21512 | tf_op jit(solution)/shard_map/ppermute | solution.py:15
  79.8 0.7 maximum_bitcast_fusion
  80.6 5.0 %collective-permute-done.5 = bf16[3584]{0:T(1024)(128)(2,1)S(1)} collective-permute-done((bf16[3584]{0:T(1024)(128)(2,1)S(1)}, bf16[3584]{0:T(1024)(128)(2,1)S(1)}, u32[]{:S(2)}, u32[]{:S(2)}) %collective-permute-start.5) | collective-permute-done | bytes 7200 | tf_op jit(solution)/shard_map/ppermute | solution.py:15
  85.6 0.7 maximum_bitcast_fusion.1
  (34 shorter events, 0.8 us)
Async XLA Ops:
  0.6 18.9 %copy-start = (bf16[1,1,4,64,576]{4,3,2,1,0:T(8,128)(2,1)S(1)}, bf16[1,1,4,64,576]{4,3,2,1,0:T(8,128)(2,1)}, u32[]{:S(2)}) copy-start(bf16[1,1,4,64,576]{4,3,2,1,0:T(8,128)(2,1)} %param.12) | copy-start | bytes 884740
  2.4 16.3 %copy-start.9 = (s32[1,1,2,2]{3,2,1,0:T(2,128)S(1)}, s32[1,1,2,2]{3,2,1,0:T(2,128)}, u32[]{:S(2)}) copy-start(s32[1,1,2,2]{3,2,1,0:T(2,128)} %param.13) | copy-start | bytes 52
  2.4 35.0 %all-to-all-start = ((bf16[32,2,3584]{2,1,0:T(2,128)(2,1)}), bf16[32,2,3584]{2,1,0:T(2,128)(2,1)S(1)}, u32[]{:S(2)}, u32[]{:S(2)}) async-start(bf16[32,2,3584]{2,1,0:T(2,128)(2,1)} %broadcast_in_dim.123), calls=%async_computation | async-start | bytes 917504 | tf_op jit(solution)/shard_map/all_to_all | solution.py:106
  18.8 0.7 copy-start.10
  19.6 0.9 %copy-start.4 = (bf16[1,1,2,64,576]{4,3,2,1,0:T(8,128)(2,1)S(1)}, bf16[1,1,2,64,576]{4,3,2,1,0:T(8,128)(2,1)}, u32[]{:S(2)}) copy-start(bf16[1,1,2,64,576]{4,3,2,1,0:T(8,128)(2,1)} %param.16) | copy-start | bytes 442372
  20.7 0.7 copy-start.6
  21.4 18.8 %copy-start.3 = (bf16[1,3584,128]{2,1,0:T(8,128)(2,1)S(1)}, bf16[1,3584,128]{2,1,0:T(8,128)(2,1)}, u32[]{:S(2)}) copy-start(bf16[1,3584,128]{2,1,0:T(8,128)(2,1)} %param.22) | copy-start | bytes 2752516
  21.8 8.0 %copy-start.5 = (f32[3584]{0:T(1024)S(1)}, f32[3584]{0:T(1024)}, u32[]{:S(2)}) copy-start(f32[3584]{0:T(1024)} %param.18) | copy-start | bytes 43012
  21.8 10.2 %collective-permute-start.1 = (bf16[64,512]{1,0:T(8,128)(2,1)S(1)}, bf16[64,512]{1,0:T(8,128)(2,1)S(1)}, u32[]{:S(2)}, u32[]{:S(2)}) collective-permute-start(bf16[64,512]{1,0:T(8,128)(2,1)S(1)} %get-tuple-element.16), channel_id=1, source_target_pairs={{0,448},{64,0},{128,64},{192,128},{256,192},{320,256},{384,320},{4... | collective-permute-start | bytes 196616 | tf_op jit(solution)/shard_map/ppermute | solution.py:15
  24.5 7.5 %collective-permute-start = (bf16[64,512]{1,0:T(8,128)(2,1)S(1)}, bf16[64,512]{1,0:T(8,128)(2,1)S(1)}, u32[]{:S(2)}, u32[]{:S(2)}) collective-permute-start(bf16[64,512]{1,0:T(8,128)(2,1)S(1)} %get-tuple-element.17), channel_id=1, source_target_pairs={{0,64},{64,128},{128,192},{192,256},{256,320},{320,384},{384,448},... | collective-permute-start | bytes 196616 | tf_op jit(solution)/shard_map/ppermute | solution.py:15
  37.4 2.8 %copy-start.2 = (bf16[1,3584,128]{2,1,0:T(8,128)(2,1)S(1)}, bf16[1,3584,128]{2,1,0:T(8,128)(2,1)}, u32[]{:S(2)}) copy-start(bf16[1,3584,128]{2,1,0:T(8,128)(2,1)} %param.21) | copy-start | bytes 2752516
  37.6 2.6 %copy-start.1 = (bf16[1,128,3584]{2,1,0:T(8,128)(2,1)S(1)}, bf16[1,128,3584]{2,1,0:T(8,128)(2,1)}, u32[]{:S(2)}) copy-start(bf16[1,128,3584]{2,1,0:T(8,128)(2,1)} %param.23) | copy-start | bytes 2752516
  45.1 6.8 %copy-start.8 = (s32[1,1,4,6]{3,2,1,0:T(4,128)S(1)}, s32[1,1,4,6]{3,2,1,0:T(4,128)}, u32[]{:S(2)}) copy-start(s32[1,1,4,6]{3,2,1,0:T(4,128)} %param.19) | copy-start | bytes 292
  45.1 25.9 %all-to-all-start.1 = ((bf16[32,2,3584]{2,1,0:T(2,128)(2,1)}), bf16[32,2,3584]{2,1,0:T(2,128)(2,1)S(1)}, u32[]{:S(2)}, u32[]{:S(2)}) async-start(bf16[32,2,3584]{2,1,0:T(2,128)(2,1)} %reshape.127), calls=%async_computation.1 | async-start | bytes 917504 | tf_op jit(solution)/shard_map/all_to_all | solution.py:133
  51.9 0.7 copy-start.7
  52.8 8.1 %collective-permute-start.2 = (f32[1,8]{1,0:T(1,128)S(1)}, f32[1,8]{1,0:T(1,128)S(1)}, u32[]{:S(2)}, u32[]{:S(2)}) collective-permute-start(f32[1,8]{1,0:T(1,128)S(1)} %get-tuple-element.22), channel_id=1, source_target_pairs={{0,448},{64,0},{128,64},{192,128},{256,192},{320,256},{384,320},{4... | collective-permute-start | bytes 104 | tf_op jit(solution)/shard_map/ppermute | solution.py:15
  54.7 7.4 %collective-permute-start.3 = (f32[1,8]{1,0:T(1,128)S(1)}, f32[1,8]{1,0:T(1,128)S(1)}, u32[]{:S(2)}, u32[]{:S(2)}) collective-permute-start(f32[1,8]{1,0:T(1,128)S(1)} %get-tuple-element.23), channel_id=1, source_target_pairs={{0,64},{64,128},{128,192},{192,256},{256,320},{320,384},{384,448},... | collective-permute-start | bytes 104 | tf_op jit(solution)/shard_map/ppermute | solution.py:15
  71.8 8.8 %collective-permute-start.4 = (bf16[3584]{0:T(1024)(128)(2,1)S(1)}, bf16[3584]{0:T(1024)(128)(2,1)S(1)}, u32[]{:S(2)}, u32[]{:S(2)}) collective-permute-start(bf16[3584]{0:T(1024)(128)(2,1)S(1)} %get-tuple-element.18), channel_id=1, source_target_pairs={{0,64},{64,128},{128,192},{192,256},{256,320},{320,384},{384,448},... | collective-permute-start | bytes 21512 | tf_op jit(solution)/shard_map/ppermute | solution.py:15
  77.9 7.7 %collective-permute-start.5 = (bf16[3584]{0:T(1024)(128)(2,1)S(1)}, bf16[3584]{0:T(1024)(128)(2,1)S(1)}, u32[]{:S(2)}, u32[]{:S(2)}) collective-permute-start(bf16[3584]{0:T(1024)(128)(2,1)S(1)} %get-tuple-element.19), channel_id=1, source_target_pairs={{0,448},{64,0},{128,64},{192,128},{256,192},{320,256},{384,320},{4... | collective-permute-start | bytes 21512 | tf_op jit(solution)/shard_map/ppermute | solution.py:15

commit v5 on v4

v5 whole, which is shorter than its diff:
```python
import jax
import jax.numpy as jnp
from jax import lax
from jax.experimental import pallas as pl
from jax.experimental.pallas import tpu as pltpu
from jax.sharding import PartitionSpec as P

VDIM = 512
QK_DIM = 192
SLICES = 8


def attend_rows(questions, keys, lens):
    scores = jnp.einsum(
        "rhl,rtl->rht", questions, keys, preferred_element_type=jnp.float32
    ) * QK_DIM ** (-0.5)
    live = jnp.arange(keys.shape[1], dtype=jnp.int32)[None, None, :] < lens[:, None, None]
    scores = jnp.where(live, scores, jnp.float32(-1e30))
    top = jnp.max(scores, axis=2, keepdims=True)
    expo = jnp.exp(scores - top)
    probs = (expo / jnp.sum(expo, axis=2, keepdims=True)).astype(jnp.bfloat16)
    out = jnp.einsum("rht,rtv->rhv", probs, keys[:, :, :VDIM], preferred_element_type=jnp.float32)
    return out.astype(jnp.bfloat16)


def dot(left, right):
    return jnp.dot(left, right, preferred_element_type=jnp.float32)


def spread_kernel(rows, out):
    out[...] = jnp.broadcast_to(rows[...][None], out.shape)


def experts_kernel(x, gain, gate_a, up_a, down_a, gate_b, up_b, down_b, out):
    wide = x[...].astype(jnp.float32)
    scale = lax.rsqrt(jnp.mean(wide * wide, axis=1, keepdims=True) + 1e-06)
    normed = (wide * scale * gain[...]).astype(jnp.bfloat16)
    total = 0.0
    for gate, up, down in ((gate_a, up_a, down_a), (gate_b, up_b, down_b)):
        act = (jax.nn.silu(dot(normed, gate[...])) * dot(normed, up[...])).astype(jnp.bfloat16)
        total = total + dot(act, down[...])
    out[...] = total.astype(jnp.bfloat16).reshape(out.shape)


def in_vmem(count):
    return [pl.BlockSpec(memory_space=pltpu.VMEM) for _ in range(count)]


LIMIT = pltpu.CompilerParams(vmem_limit_bytes=16 * 1024 * 1024)


def body(
    latent_cache,
    page_table,
    lengths,
    move_to,
    query,
    hidden,
    norm_gain,
    expert_ids,
    expert_gates,
    gate_weight,
    up_weight,
    down_weight,
):
    pool = latent_cache[0, 0]
    table = page_table[0, 0]
    requests = table.shape[0]
    moves = move_to[0, 0]
    rows = hidden[0, 0]
    width = rows.shape[1]
    devices = lax.axis_size("ep")
    experts_here = devices // SLICES

    keys = pool[table.reshape(-1)].reshape(requests, table.shape[1] * pool.shape[1], pool.shape[2])
    attn = attend_rows(query[0, 0], keys, lengths[0, 0])

    def picked(which, values):
        keep = (moves == which).reshape((requests,) + (1,) * (values.ndim - 1))
        return jnp.sum(jnp.where(keep, values, jnp.zeros_like(values)), axis=0, dtype=values.dtype)

    def served(values, from_prev, from_next):
        keep = (moves == 0).reshape((requests,) + (1,) * (values.ndim - 1))
        stay = jnp.where(keep, values, jnp.zeros_like(values))
        return jnp.concatenate([stay, from_prev[None], from_next[None]], axis=0)

    def exchanged(forward, backward):
        groups = lax.axis_size("grp")
        even = lax.axis_index("grp") % 2 == 0
        outer = [(i, (i + 1) % groups if i % 2 else (i - 1) % groups) for i in range(groups)]
        inner = [(i, i ^ 1) for i in range(groups)]
        one = lax.ppermute(jnp.where(even, backward, forward), "grp", outer)
        two = lax.ppermute(jnp.where(even, forward, backward), "grp", inner)
        return jnp.where(even, one, two), jnp.where(even, two, one)

    cores = 2
    chips = devices // cores
    alike = [[cores * i + j for i in range(chips)] for j in range(cores)]
    count = chips * requests
    outgoing = pl.pallas_call(
        spread_kernel,
        out_shape=jax.ShapeDtypeStruct((chips, requests, width), jnp.bfloat16),
        in_specs=in_vmem(1),
        out_specs=in_vmem(1)[0],
    )(rows)
    received = lax.all_to_all(
        outgoing, "ep", split_axis=0, concat_axis=0, axis_index_groups=alike, tiled=True
    )
    swap = [(i, i ^ 1) for i in range(devices)]
    weights = (gate_weight[0], up_weight[0], down_weight[0])
    traded = tuple(lax.ppermute(weight, "ep", swap) for weight in weights)
    received, attn = lax.optimization_barrier((received, attn))
    pair = pl.pallas_call(
        experts_kernel,
        out_shape=jax.ShapeDtypeStruct((chips, requests, width), jnp.bfloat16),
        in_specs=in_vmem(8),
        out_specs=in_vmem(1)[0],
        compiler_params=LIMIT,
    )(received.reshape(count, width), norm_gain[None, :], *weights, *traded)
    returned = lax.all_to_all(
        pair,
        "ep",
        split_axis=0,
        concat_axis=0,
        axis_index_groups=alike,
        tiled=True,
    )

    ids, gates, attn, _ = lax.optimization_barrier((expert_ids[0, 0], expert_gates[0, 0], attn, pair))
    onehot = (
        ids[:, :, None] == jnp.arange(experts_here, dtype=jnp.int32)
    ).astype(jnp.float32)
    mix = jnp.einsum("sk,skx->sx", gates, onehot, precision=lax.Precision.HIGHEST)
    high = lax.reduce_precision(mix, 8, 7)
    middle = lax.reduce_precision(mix - high, 8, 7)
    low = lax.reduce_precision(mix - high - middle, 8, 7)
    pieces = jnp.concatenate([high, middle, low], axis=1).astype(jnp.bfloat16)
    pieces = jnp.pad(pieces, ((0, 0), (0, VDIM - pieces.shape[1])))[:, None, :]
    heads = attn.shape[1]
    behind = lambda row, values: jnp.concatenate([values, row], axis=0)
    got_prev, got_next = exchanged(
        behind(pieces[requests + 1], picked(1, attn)), behind(pieces[requests], picked(2, attn))
    )
    per_expert = jnp.sum(
        returned.reshape(experts_here, SLICES // cores, requests, width).astype(jnp.float32), axis=1
    )
    per_expert, got_prev, got_next = lax.optimization_barrier((per_expert, got_prev, got_next))
    attn_prev, attn_next = got_prev[:heads], got_next[:heads]

    def mix_of(got):
        three = got[heads, : 3 * experts_here].astype(jnp.float32).reshape(3, experts_here)
        return (three[0] + three[1] + three[2])[None]

    at = moves[:, None]
    mix_home = jnp.where(
        at == 0, mix[:requests], jnp.where(at == 1, mix_of(got_next), mix_of(got_prev))
    )
    moe = jnp.sum(per_expert * mix_home.T[:, :, None], axis=0).astype(jnp.bfloat16)
    moe_prev, moe_next = exchanged(picked(1, moe), picked(2, moe))
    return (
        served(attn, attn_prev, attn_next)[None, None],
        served(moe, moe_prev, moe_next)[None, None],
    )


def solution(mesh):
    in_specs = (
        P("grp", "ep", None, None, None),
        P("grp", "ep", None, None),
        P("grp", "ep", None),
        P("grp", "ep", None),
        P("grp", "ep", None, None, None),
        P("grp", "ep", None, None),
        P(),
        P("grp", "ep", None, None),
        P("grp", "ep", None, None),
        P("ep", None, None),
        P("ep", None, None),
        P("ep", None, None),
    )
    out_specs = (P("grp", "ep", None, None, None), P("grp", "ep", None, None))
    return jax.shard_map(body, mesh=mesh, in_specs=in_specs, out_specs=out_specs, check_vma=False)
```

time: 86.9 us -> 80.3 us (0.924)
  the two profiles are of different devices: /device:TPU:14 before, /device:TPU:8 now
where the time goes in v5:
time: 80.3 us; the launch traced here: 79.7 us
  starting transfers between devices  42.7 us (53%)
  waiting for transfers between devices  19.9 us (25%)
  Pallas kernels  5.31 us (7%)
  local copies, waits for them, and re-layouts  4.73 us (6%)
  other arithmetic  3.52 us (4%)
  matrix products  2.51 us (3%)
  between operations  0.99 us (1%)
    all_to_all x1, starting transfers between devices, body(): lax.all_to_all(outgoing, 'ep', split_axis=0, concat_axis=0, axis_index_gr...  16.2 us
    ppermute x2, starting transfers between devices, exchanged(): one = lax.ppermute(jnp.where(even, backward, forward), 'grp', outer)  11.1 us
    all_to_all x1, waiting for transfers between devices, body(): lax.all_to_all(outgoing, 'ep', split_axis=0, concat_axis=0, axis_index_gr...  7.12 us
    ppermute x2, waiting for transfers between devices, exchanged(): one = lax.ppermute(jnp.where(even, backward, forward), 'grp', outer)  6.27 us
    ppermute x3, starting transfers between devices, body(): traded = tuple((lax.ppermute(weight, 'ep', swap) for weight in weights))  6.25 us
    all_to_all x1, starting transfers between devices, body(): lax.all_to_all(pair, 'ep', split_axis=0, concat_axis=0, axis_index_groups...  5.22 us
    ppermute x2, starting transfers between devices, exchanged(): two = lax.ppermute(jnp.where(even, forward, backward), 'grp', inner)  3.84 us
    pallas_call x1, Pallas kernels, body(): pl.pallas_call(experts_kernel, out_shape=jax.ShapeDtypeStruct((chips, req...  3.69 us
  transfers between devices with their start and end apart: 9, of which 4 were waited for; matrix products, arithmetic and copies ran while one was open for 8% of the time, Pallas kernels for 0%

profile of v5, /device:TPU:8, one launch (start us, length us, event | category | flops | bytes accessed | tf_op | source)
XLA Modules:
  0.0 79.7 jit_solution(94926810594336185)
XLA Ops:
  0.7 1.6 %shard_map.131 = bf16[32,2,3584]{2,1,0:T(2,128)(2,1)} custom-call(bf16[2,3584]{1,0:T(2,128)(2,1)} %bitcast.57), custom_call_target="tpu_custom_call" | custom-call | tf_op jit(solution)/shard_map/pallas_call | solution.py:100
  2.3 16.2 %all-to-all-start = ((bf16[32,2,3584]{2,1,0:T(2,128)(2,1)}), bf16[32,2,3584]{2,1,0:T(2,128)(2,1)}, u32[]{:S(2)}, u32[]{:S(2)}) async-start(bf16[32,2,3584]{2,1,0:T(2,128)(2,1)} %shard_map.131), calls=%async_computation | async-start | bytes 917504 | tf_op jit(solution)/shard_map/all_to_all | solution.py:106
  18.5 1.9 %collective-permute-start = (bf16[3584,128]{1,0:T(8,128)(2,1)S(1)}, bf16[3584,128]{1,0:T(8,128)(2,1)}, u32[]{:S(2)}, u32[]{:S(2)}) collective-permute-start(bf16[3584,128]{1,0:T(8,128)(2,1)S(1)} %bitcast.49), channel_id=1, source_target_pairs={{0,1},{1,0},{2,3},{3,2},{4,5},{5,4},{6,7},{7,6},{8,9},{9,8},{10,11... | collective-permute-start | bytes 2752520 | tf_op jit(solution)/shard_map/ppermute | solution.py:111
  20.5 2.4 %collective-permute-start.1 = (bf16[3584,128]{1,0:T(8,128)(2,1)}, bf16[3584,128]{1,0:T(8,128)(2,1)}, u32[]{:S(2)}, u32[]{:S(2)}) collective-permute-start(bf16[3584,128]{1,0:T(8,128)(2,1)} %bitcast.51), channel_id=1, source_target_pairs={{0,1},{1,0},{2,3},{3,2},{4,5},{5,4},{6,7},{7,6},{8,9},{9,8},{10,11... | collective-permute-start | bytes 2752520 | tf_op jit(solution)/shard_map/ppermute | solution.py:111
  22.9 1.9 %collective-permute-start.2 = (bf16[128,3584]{1,0:T(8,128)(2,1)}, bf16[128,3584]{1,0:T(8,128)(2,1)}, u32[]{:S(2)}, u32[]{:S(2)}) collective-permute-start(bf16[128,3584]{1,0:T(8,128)(2,1)} %bitcast.53), channel_id=1, source_target_pairs={{0,1},{1,0},{2,3},{3,2},{4,5},{5,4},{6,7},{7,6},{8,9},{9,8},{10,11... | collective-permute-start | bytes 2752520 | tf_op jit(solution)/shard_map/ppermute | solution.py:111
  24.8 0.7 copy-done.12
  25.6 0.7 copy-done.13
  26.4 0.6 gather_fusion
  27.0 1.3 %fusion.4 = f32[2,64,128]{2,1,0:T(8,128)S(1)} fusion(bf16[2,128,576]{2,1,0:T(8,128)(2,1)S(1)} %bitcast.55, bf16[1,1,2,64,576]{4,3,2,1,0:T(8,128)(2,1)} %param.16, pred[2,128]{1,0:T(4,128)(4,1)S(1)} %iota_compare_fusion.3), kind=kOutput, calls=%fused_computation.7 | convolution fusion | flops 18907136 | bytes 508160 | tf_op jit(solution)/shard_map/rhl,rtl->rht/dot_general | solution.py:14
  28.3 0.2 fusion.22
  28.5 0.6 compare_bitcast_fusion.2
  29.1 1.0 %convolution_convert_fusion = bf16[2,64,512]{2,1,0:T(8,128)(2,1)} fusion(bf16[2,128,576]{2,1,0:T(8,128)(2,1)S(1)} %bitcast.56, f32[2,64]{1,0:T(2,128)S(1)} %fusion.22, f32[2,64,128]{2,1,0:T(8,128)S(1)} %fusion.4), kind=kOutput, calls=%fused_computation.2 | convolution fusion | flops 16892160 | bytes 492032 | tf_op jit(solution)/shard_map/rht,rtv->rhv/dot_general | solution.py:22
  30.1 7.1 %all-to-all-done = bf16[32,2,3584]{2,1,0:T(2,128)(2,1)} async-done(((bf16[32,2,3584]{2,1,0:T(2,128)(2,1)}), bf16[32,2,3584]{2,1,0:T(2,128)(2,1)}, u32[]{:S(2)}, u32[]{:S(2)}) %all-to-all-start) | async-done | bytes 458784 | tf_op jit(solution)/shard_map/all_to_all | solution.py:106
  37.2 1.2 %reshape.160.x = bf16[64,3584]{1,0:T(8,128)(2,1)S(1)} reshape(bf16[32,2,3584]{2,1,0:T(2,128)(2,1)} %all-to-all-done) | data formatting | bytes 917504 | tf_op jit(solution)/shard_map/reshape | solution.py:119
  38.5 3.7 %shard_map.132 = bf16[32,2,3584]{2,1,0:T(2,128)(2,1)} custom-call(bf16[64,3584]{1,0:T(8,128)(2,1)S(1)} %reshape.160.x, f32[1,3584]{1,0:T(1,128)S(1)} %broadcast_in_dim.114.gain, bf16[3584,128]{1,0:T(8,128)(2,1)S(1)} %bitcast.50, bf16[3584,128]{1,0:T(8,128)(2,1)S(1)} %bitcast.52, bf16[128,3584]{1,0:T(8,128)(2,1)S(1)} %bitcast.54, ...), custom_call_target="tpu_custom_call" | custom-call | tf_op jit(solution)/shard_map/pallas_call | solution.py:113
  42.2 5.2 %all-to-all-start.1 = ((bf16[32,2,3584]{2,1,0:T(2,128)(2,1)}), bf16[32,2,3584]{2,1,0:T(2,128)(2,1)S(1)}, u32[]{:S(2)}, u32[]{:S(2)}) async-start(bf16[32,2,3584]{2,1,0:T(2,128)(2,1)} %shard_map.132), calls=%async_computation.1 | async-start | bytes 917504 | tf_op jit(solution)/shard_map/all_to_all | solution.py:120
  47.4 0.7 copy-done.10
  48.1 0.2 fusion.8
  48.4 0.6 copy-done.6
  49.1 0.1 select_reduce_fusion.1
  49.3 5.6 %collective-permute-start.3 = (bf16[65,512]{1,0:T(8,128)(2,1)S(1)}, bf16[65,512]{1,0:T(8,128)(2,1)S(1)}, u32[]{:S(2)}, u32[]{:S(2)}) collective-permute-start(bf16[65,512]{1,0:T(8,128)(2,1)S(1)} %get-tuple-element.25), channel_id=1, source_target_pairs={{0,448},{64,128},{128,64},{192,256},{256,192},{320,384},{384,320},... | collective-permute-start | bytes 199688 | tf_op jit(solution)/shard_map/ppermute | solution.py:92
  54.8 1.9 %collective-permute-start.4 = (bf16[65,512]{1,0:T(8,128)(2,1)S(1)}, bf16[65,512]{1,0:T(8,128)(2,1)S(1)}, u32[]{:S(2)}, u32[]{:S(2)}) collective-permute-start(bf16[65,512]{1,0:T(8,128)(2,1)S(1)} %get-tuple-element.24), channel_id=1, source_target_pairs={{0,64},{64,0},{128,192},{192,128},{256,320},{320,256},{384,448},{4... | collective-permute-start | bytes 199688 | tf_op jit(solution)/shard_map/ppermute | solution.py:93
  56.8 6.3 %collective-permute-done.3 = bf16[65,512]{1,0:T(8,128)(2,1)S(1)} collective-permute-done((bf16[65,512]{1,0:T(8,128)(2,1)S(1)}, bf16[65,512]{1,0:T(8,128)(2,1)S(1)}, u32[]{:S(2)}, u32[]{:S(2)}) %collective-permute-start.3) | collective-permute-done | bytes 66592 | tf_op jit(solution)/shard_map/ppermute | solution.py:92
  63.0 3.7 %all-to-all-done.1 = bf16[32,2,3584]{2,1,0:T(2,128)(2,1)S(1)} async-done(((bf16[32,2,3584]{2,1,0:T(2,128)(2,1)}), bf16[32,2,3584]{2,1,0:T(2,128)(2,1)S(1)}, u32[]{:S(2)}, u32[]{:S(2)}) %all-to-all-start.1) | async-done | bytes 458784 | tf_op jit(solution)/shard_map/all_to_all | solution.py:120
  66.7 0.4 convert_reduce_fusion
  67.5 0.2 multiply_reduce_fusion
  67.7 0.2 fusion.9
  67.8 5.6 %collective-permute-start.5 = (bf16[3584]{0:T(1024)(128)(2,1)S(1)}, bf16[3584]{0:T(1024)(128)(2,1)S(1)}, u32[]{:S(2)}, u32[]{:S(2)}) collective-permute-start(bf16[3584]{0:T(1024)(128)(2,1)S(1)} %get-tuple-element.29), channel_id=1, source_target_pairs={{0,448},{64,128},{128,64},{192,256},{256,192},{320,384},{384,320},... | collective-permute-start | bytes 21512 | tf_op jit(solution)/shard_map/ppermute | solution.py:92
  73.4 1.9 %collective-permute-start.6 = (bf16[3584]{0:T(1024)(128)(2,1)S(1)}, bf16[3584]{0:T(1024)(128)(2,1)S(1)}, u32[]{:S(2)}, u32[]{:S(2)}) collective-permute-start(bf16[3584]{0:T(1024)(128)(2,1)S(1)} %get-tuple-element.30), channel_id=1, source_target_pairs={{0,64},{64,0},{128,192},{192,128},{256,320},{320,256},{384,448},{4... | collective-permute-start | bytes 21512 | tf_op jit(solution)/shard_map/ppermute | solution.py:93
  75.3 0.7 maximum_bitcast_fusion
  76.1 2.9 %collective-permute-done.6 = bf16[3584]{0:T(1024)(128)(2,1)S(1)} collective-permute-done((bf16[3584]{0:T(1024)(128)(2,1)S(1)}, bf16[3584]{0:T(1024)(128)(2,1)S(1)}, u32[]{:S(2)}, u32[]{:S(2)}) %collective-permute-start.6) | collective-permute-done | bytes 7200 | tf_op jit(solution)/shard_map/ppermute | solution.py:93
  79.0 0.7 maximum_bitcast_fusion.1
  (49 shorter events, 0.8 us)
Async XLA Ops:
  0.6 25.7 %copy-start = (bf16[1,1,4,64,576]{4,3,2,1,0:T(8,128)(2,1)S(1)}, bf16[1,1,4,64,576]{4,3,2,1,0:T(8,128)(2,1)}, u32[]{:S(2)}) copy-start(bf16[1,1,4,64,576]{4,3,2,1,0:T(8,128)(2,1)} %param.12) | copy-start | bytes 884740
  0.6 17.9 %copy-start.1 = (bf16[1,3584,128]{2,1,0:T(8,128)(2,1)S(1)}, bf16[1,3584,128]{2,1,0:T(8,128)(2,1)}, u32[]{:S(2)}) copy-start(bf16[1,3584,128]{2,1,0:T(8,128)(2,1)} %param.21) | copy-start | bytes 2752516
  2.3 35.0 %all-to-all-start = ((bf16[32,2,3584]{2,1,0:T(2,128)(2,1)}), bf16[32,2,3584]{2,1,0:T(2,128)(2,1)}, u32[]{:S(2)}, u32[]{:S(2)}) async-start(bf16[32,2,3584]{2,1,0:T(2,128)(2,1)} %shard_map.131), calls=%async_computation | async-start | bytes 917504 | tf_op jit(solution)/shard_map/all_to_all | solution.py:106
  18.5 19.9 %collective-permute-start = (bf16[3584,128]{1,0:T(8,128)(2,1)S(1)}, bf16[3584,128]{1,0:T(8,128)(2,1)}, u32[]{:S(2)}, u32[]{:S(2)}) collective-permute-start(bf16[3584,128]{1,0:T(8,128)(2,1)S(1)} %bitcast.49), channel_id=1, source_target_pairs={{0,1},{1,0},{2,3},{3,2},{4,5},{5,4},{6,7},{7,6},{8,9},{9,8},{10,11... | collective-permute-start | bytes 2752520 | tf_op jit(solution)/shard_map/ppermute | solution.py:111
  20.4 5.9 %copy-start.5 = (f32[3584]{0:T(1024)S(1)}, f32[3584]{0:T(1024)}, u32[]{:S(2)}) copy-start(f32[3584]{0:T(1024)} %param.18) | copy-start | bytes 43012
  20.5 18.0 %collective-permute-start.1 = (bf16[3584,128]{1,0:T(8,128)(2,1)}, bf16[3584,128]{1,0:T(8,128)(2,1)}, u32[]{:S(2)}, u32[]{:S(2)}) collective-permute-start(bf16[3584,128]{1,0:T(8,128)(2,1)} %bitcast.51), channel_id=1, source_target_pairs={{0,1},{1,0},{2,3},{3,2},{4,5},{5,4},{6,7},{7,6},{8,9},{9,8},{10,11... | collective-permute-start | bytes 2752520 | tf_op jit(solution)/shard_map/ppermute | solution.py:111
  22.9 15.6 %collective-permute-start.2 = (bf16[128,3584]{1,0:T(8,128)(2,1)}, bf16[128,3584]{1,0:T(8,128)(2,1)}, u32[]{:S(2)}, u32[]{:S(2)}) collective-permute-start(bf16[128,3584]{1,0:T(8,128)(2,1)} %bitcast.53), channel_id=1, source_target_pairs={{0,1},{1,0},{2,3},{3,2},{4,5},{5,4},{6,7},{7,6},{8,9},{9,8},{10,11... | collective-permute-start | bytes 2752520 | tf_op jit(solution)/shard_map/ppermute | solution.py:111
  24.8 0.7 copy-start.12
  25.6 0.7 copy-start.13
  26.4 2.1 %copy-start.9 = (s32[1,1,2]{2,1,0:T(1,128)S(1)}, s32[1,1,2]{2,1,0:T(1,128)}, u32[]{:S(2)}) copy-start(s32[1,1,2]{2,1,0:T(1,128)} %param.15) | copy-start | bytes 28
  27.0 11.5 %copy-start.2 = (bf16[1,3584,128]{2,1,0:T(8,128)(2,1)S(1)}, bf16[1,3584,128]{2,1,0:T(8,128)(2,1)}, u32[]{:S(2)}) copy-start(bf16[1,3584,128]{2,1,0:T(8,128)(2,1)} %param.22) | copy-start | bytes 2752516
  27.0 11.5 %copy-start.3 = (bf16[1,128,3584]{2,1,0:T(8,128)(2,1)S(1)}, bf16[1,128,3584]{2,1,0:T(8,128)(2,1)}, u32[]{:S(2)}) copy-start(bf16[1,128,3584]{2,1,0:T(8,128)(2,1)} %param.23) | copy-start | bytes 2752516
  42.2 5.2 %copy-start.11 = (s32[1,1,4,6]{3,2,1,0:T(4,128)S(1)}, s32[1,1,4,6]{3,2,1,0:T(4,128)}, u32[]{:S(2)}) copy-start(s32[1,1,4,6]{3,2,1,0:T(4,128)} %param.19) | copy-start | bytes 292
  42.2 6.3 %copy-start.4 = (bf16[2,64,512]{2,1,0:T(8,128)(2,1)S(1)}, bf16[2,64,512]{2,1,0:T(8,128)(2,1)}, u32[]{:S(2)}) copy-start(bf16[2,64,512]{2,1,0:T(8,128)(2,1)} %convolution_convert_fusion) | copy-start | bytes 393220
  42.2 24.5 %all-to-all-start.1 = ((bf16[32,2,3584]{2,1,0:T(2,128)(2,1)}), bf16[32,2,3584]{2,1,0:T(2,128)(2,1)S(1)}, u32[]{:S(2)}, u32[]{:S(2)}) async-start(bf16[32,2,3584]{2,1,0:T(2,128)(2,1)} %shard_map.132), calls=%async_computation.1 | async-start | bytes 917504 | tf_op jit(solution)/shard_map/all_to_all | solution.py:120
  47.4 0.7 copy-start.10
  48.4 0.7 copy-start.6
  48.4 0.7 copy-start.7
  48.4 0.7 copy-start.8
  49.3 13.8 %collective-permute-start.3 = (bf16[65,512]{1,0:T(8,128)(2,1)S(1)}, bf16[65,512]{1,0:T(8,128)(2,1)S(1)}, u32[]{:S(2)}, u32[]{:S(2)}) collective-permute-start(bf16[65,512]{1,0:T(8,128)(2,1)S(1)} %get-tuple-element.25), channel_id=1, source_target_pairs={{0,448},{64,128},{128,64},{192,256},{256,192},{320,384},{384,320},... | collective-permute-start | bytes 199688 | tf_op jit(solution)/shard_map/ppermute | solution.py:92
  54.8 8.2 %collective-permute-start.4 = (bf16[65,512]{1,0:T(8,128)(2,1)S(1)}, bf16[65,512]{1,0:T(8,128)(2,1)S(1)}, u32[]{:S(2)}, u32[]{:S(2)}) collective-permute-start(bf16[65,512]{1,0:T(8,128)(2,1)S(1)} %get-tuple-element.24), channel_id=1, source_target_pairs={{0,64},{64,0},{128,192},{192,128},{256,320},{320,256},{384,448},{4... | collective-permute-start | bytes 199688 | tf_op jit(solution)/shard_map/ppermute | solution.py:93
  67.8 8.3 %collective-permute-start.5 = (bf16[3584]{0:T(1024)(128)(2,1)S(1)}, bf16[3584]{0:T(1024)(128)(2,1)S(1)}, u32[]{:S(2)}, u32[]{:S(2)}) collective-permute-start(bf16[3584]{0:T(1024)(128)(2,1)S(1)} %get-tuple-element.29), channel_id=1, source_target_pairs={{0,448},{64,128},{128,64},{192,256},{256,192},{320,384},{384,320},... | collective-permute-start | bytes 21512 | tf_op jit(solution)/shard_map/ppermute | solution.py:92
  73.4 5.5 %collective-permute-start.6 = (bf16[3584]{0:T(1024)(128)(2,1)S(1)}, bf16[3584]{0:T(1024)(128)(2,1)S(1)}, u32[]{:S(2)}, u32[]{:S(2)}) collective-permute-start(bf16[3584]{0:T(1024)(128)(2,1)S(1)} %get-tuple-element.30), channel_id=1, source_target_pairs={{0,64},{64,0},{128,192},{192,128},{256,320},{320,256},{384,448},{4... | collective-permute-start | bytes 21512 | tf_op jit(solution)/shard_map/ppermute | solution.py:93

commit v6 on v5

v6 whole, which is shorter than its diff:
```python
import functools

import jax
import jax.numpy as jnp
from jax import lax
from jax.experimental import pallas as pl
from jax.experimental.pallas import tpu as pltpu
from jax.sharding import PartitionSpec as P

VDIM = 512
QK_DIM = 192
SLICES = 8
BEHIND = 16


def dot(left, right):
    return jnp.dot(left, right, preferred_element_type=jnp.float32)


def one_of(choices, which, wanted):
    found = jnp.zeros_like(choices[0])
    for j, choice in enumerate(choices):
        found = jnp.where(which[j] == wanted, choice, found)
    return found


def spread_kernel(rows, out):
    out[...] = jnp.broadcast_to(rows[...][None], out.shape)


def attend_kernel(
    table, lens, moves, odd, ids, gates, pool, query, outer, inner, stay, mix
):
    requests, heads = query.shape[0], query.shape[1]
    results = []
    for j in range(requests):
        keys = jnp.concatenate([pool[table[j, p]] for p in range(table.shape[1])], axis=0)
        scores = lax.dot_general(
            query[j], keys, (((1,), (1,)), ((), ())), preferred_element_type=jnp.float32
        ) * QK_DIM ** (-0.5)
        live = lax.broadcasted_iota(jnp.int32, scores.shape, 1) < lens[j]
        scores = jnp.where(live, scores, jnp.float32(-1e30))
        expo = jnp.exp(scores - jnp.max(scores, axis=1, keepdims=True))
        probs = (expo / jnp.sum(expo, axis=1, keepdims=True)).astype(jnp.bfloat16)
        results.append(dot(probs, keys[:, :VDIM]))
        stay[j] = jnp.where(moves[j] == 0, results[j], jnp.zeros_like(results[j])).astype(jnp.bfloat16)
    lane = lax.broadcasted_iota(jnp.int32, mix.shape, 1)
    total = jnp.zeros(mix.shape, jnp.float32)
    for k in range(ids.shape[1]):
        total = total + jnp.where(ids[:, k : k + 1] == lane, gates[:, k : k + 1], 0.0)
    mix[...] = total
    high = total.astype(jnp.bfloat16).astype(jnp.float32)
    middle = (total - high).astype(jnp.bfloat16).astype(jnp.float32)
    low = total - high - middle
    pieces = jnp.concatenate([high, middle, low, jnp.zeros_like(low)], axis=1)
    forward, backward = one_of(results, moves, 1), one_of(results, moves, 2)
    behind = outer.shape[0] - heads
    row_forward = jnp.broadcast_to(pieces[requests + 1 : requests + 2], (behind, pieces.shape[1]))
    row_backward = jnp.broadcast_to(pieces[requests : requests + 1], (behind, pieces.shape[1]))
    is_odd = odd[0] == 1
    outer[:heads] = jnp.where(is_odd, forward, backward).astype(jnp.bfloat16)
    outer[heads:] = jnp.where(is_odd, row_forward, row_backward).astype(jnp.bfloat16)
    inner[:heads] = jnp.where(is_odd, backward, forward).astype(jnp.bfloat16)
    inner[heads:] = jnp.where(is_odd, row_backward, row_forward).astype(jnp.bfloat16)


def experts_kernel(
    x, gain, gate_a, up_a, down_a, gate_there, up_there, down_there, out, gate_b, up_b, down_b, sems
):
    pairs = ((gate_there, gate_b), (up_there, up_b), (down_there, down_b))
    copies = [pltpu.make_async_copy(*pair, sems.at[i]) for i, pair in enumerate(pairs)]
    for copy in copies:
        copy.start()
    wide = x[...].reshape(x.shape[0] * x.shape[1], x.shape[2]).astype(jnp.float32)
    scale = lax.rsqrt(jnp.mean(wide * wide, axis=1, keepdims=True) + 1e-06)
    normed = (wide * scale * gain[...]).astype(jnp.bfloat16)
    act = (jax.nn.silu(dot(normed, gate_a[...])) * dot(normed, up_a[...])).astype(jnp.bfloat16)
    total = dot(act, down_a[...])
    copies[0].wait()
    gate = dot(normed, gate_b[...])
    copies[1].wait()
    act = (jax.nn.silu(gate) * dot(normed, up_b[...])).astype(jnp.bfloat16)
    copies[2].wait()
    total = total + dot(act, down_b[...])
    out[...] = total.astype(jnp.bfloat16).reshape(out.shape)


def gather_kernel(experts_here, moves, odd, returned, mix, got_outer, got_inner, outer, inner, stay):
    chips, requests, width = returned.shape
    experts = experts_here
    is_odd = odd[0] == 1
    heads = got_outer.shape[0] - BEHIND

    def mix_of(got):
        row = got[heads : heads + BEHIND].astype(jnp.float32)[:1]
        step = mix.shape[1]
        return row[:, :step] + row[:, step : 2 * step] + row[:, 2 * step : 3 * step]

    mix_outer, mix_inner = mix_of(got_outer), mix_of(got_inner)
    mix_next = jnp.where(is_odd, mix_outer, mix_inner)
    mix_prev = jnp.where(is_odd, mix_inner, mix_outer)
    lane = lax.broadcasted_iota(jnp.int32, (1, chips * requests), 1)
    weights = []
    for j in range(requests):
        own = mix[j : j + 1]
        home = jnp.where(moves[j] == 0, own, jnp.where(moves[j] == 1, mix_next, mix_prev))
        spread = jnp.zeros(lane.shape, jnp.float32)
        per_expert = chips * requests // experts
        for x in range(experts):
            spread = jnp.where(lane // per_expert == x, home[:, x : x + 1], spread)
        weights.append(jnp.where(lane % requests == j, spread, 0.0))
    weights = jnp.concatenate(weights, axis=0)
    flat = returned[...].reshape(chips * requests, width)
    high = weights.astype(jnp.bfloat16)
    rest = weights - high.astype(jnp.float32)
    middle = rest.astype(jnp.bfloat16)
    low = (rest - middle.astype(jnp.float32)).astype(jnp.bfloat16)
    moe = dot(high, flat) + dot(middle, flat) + dot(low, flat)
    rows = [moe[j : j + 1] for j in range(requests)]
    forward, backward = one_of(rows, moves, 1), one_of(rows, moves, 2)
    outer[...] = jnp.where(is_odd, forward, backward).astype(jnp.bfloat16)
    inner[...] = jnp.where(is_odd, backward, forward).astype(jnp.bfloat16)
    kept = [jnp.where(moves[j] == 0, rows[j], jnp.zeros_like(rows[j])) for j in range(requests)]
    stay[...] = jnp.concatenate(kept, axis=0).astype(jnp.bfloat16)


def in_vmem(count):
    return [pl.BlockSpec(memory_space=pltpu.VMEM) for _ in range(count)]


def in_smem(count):
    return [pl.BlockSpec(memory_space=pltpu.SMEM) for _ in range(count)]


SMALL = pltpu.CompilerParams(vmem_limit_bytes=6 * 1024 * 1024)
LIMIT = pltpu.CompilerParams(vmem_limit_bytes=10 * 1024 * 1024)


def body(
    latent_cache,
    page_table,
    lengths,
    move_to,
    query,
    hidden,
    norm_gain,
    expert_ids,
    expert_gates,
    gate_weight,
    up_weight,
    down_weight,
):
    pool = latent_cache[0, 0]
    table = page_table[0, 0]
    requests = table.shape[0]
    moves = move_to[0, 0]
    rows = hidden[0, 0]
    width = rows.shape[1]
    devices = lax.axis_size("ep")

    groups = lax.axis_size("grp")
    group_odd = (lax.axis_index("grp") % 2).astype(jnp.int32).reshape(1)
    outer_pairs = [(i, (i + 1) % groups if i % 2 else (i - 1) % groups) for i in range(groups)]
    inner_pairs = [(i, i ^ 1) for i in range(groups)]

    def exchanged(outer, inner):
        return lax.ppermute(outer, "grp", outer_pairs), lax.ppermute(inner, "grp", inner_pairs)

    def served(stay, got_outer, got_inner):
        odd = group_odd[0] == 1
        from_prev = jnp.where(odd, got_inner, got_outer)
        from_next = jnp.where(odd, got_outer, got_inner)
        return jnp.concatenate([stay, from_prev, from_next], axis=0)[None, None]

    heads = query.shape[3]
    payload = jax.ShapeDtypeStruct((heads + BEHIND, VDIM), jnp.bfloat16)
    send_outer, send_inner, attn_stay, mix = pl.pallas_call(
        attend_kernel,
        out_shape=(
            payload,
            payload,
            jax.ShapeDtypeStruct((requests, heads, VDIM), jnp.bfloat16),
            jax.ShapeDtypeStruct((expert_ids.shape[2], 128), jnp.float32),
        ),
        in_specs=in_smem(4) + in_vmem(4),
        out_specs=tuple(in_vmem(4)),
        compiler_params=SMALL,
        cost_estimate=pl.CostEstimate(flops=40_000_000_000, bytes_accessed=400_000_000, transcendentals=100_000_000),
    )(
        table, lengths[0, 0], moves, group_odd, expert_ids[0, 0], expert_gates[0, 0], pool, query[0, 0]
    )

    cores = 2
    chips = devices // cores
    alike = [[cores * i + j for i in range(chips)] for j in range(cores)]
    count = chips * requests
    outgoing = pl.pallas_call(
        spread_kernel,
        out_shape=jax.ShapeDtypeStruct((chips, requests, width), jnp.bfloat16),
        in_specs=in_vmem(1),
        out_specs=in_vmem(1)[0],
        compiler_params=pltpu.CompilerParams(vmem_limit_bytes=2 * 1024 * 1024),
    )(rows)
    received = lax.all_to_all(
        outgoing, "ep", split_axis=0, concat_axis=0, axis_index_groups=alike, tiled=True
    )
    swap = [(i, i ^ 1) for i in range(devices)]
    weights = (gate_weight[0], up_weight[0], down_weight[0])
    traded = tuple(lax.ppermute(weight, "ep", swap) for weight in weights)
    received, send_outer, send_inner, attn_stay, mix = lax.optimization_barrier(
        (received, send_outer, send_inner, attn_stay, mix)
    )
    pair = pl.pallas_call(
        experts_kernel,
        out_shape=jax.ShapeDtypeStruct((chips, requests, width), jnp.bfloat16),
        in_specs=in_vmem(5) + [pl.BlockSpec(memory_space=pl.ANY) for _ in traded],
        out_specs=in_vmem(1)[0],
        scratch_shapes=[pltpu.VMEM(weight.shape, weight.dtype) for weight in traded]
        + [pltpu.SemaphoreType.DMA((len(traded),))],
        compiler_params=LIMIT,
    )(received, norm_gain[None, :], *weights, *traded)
    returned = lax.all_to_all(
        pair,
        "ep",
        split_axis=0,
        concat_axis=0,
        axis_index_groups=alike,
        tiled=True,
    )

    send_outer, send_inner, attn_stay, _ = lax.optimization_barrier(
        (send_outer, send_inner, attn_stay, pair)
    )
    got_outer, got_inner = exchanged(send_outer, send_inner)
    returned, got_outer, got_inner = lax.optimization_barrier((returned, got_outer, got_inner))
    line = jax.ShapeDtypeStruct((1, width), jnp.bfloat16)
    moe_outer, moe_inner, moe_stay = pl.pallas_call(
        functools.partial(gather_kernel, devices // SLICES),
        out_shape=(line, line, jax.ShapeDtypeStruct((requests, width), jnp.bfloat16)),
        in_specs=in_smem(2) + in_vmem(4),
        out_specs=tuple(in_vmem(3)),
        compiler_params=SMALL,
    )(moves, group_odd, returned, mix, got_outer, got_inner)
    return (
        served(attn_stay, got_outer[None, :heads], got_inner[None, :heads]),
        served(moe_stay, *exchanged(moe_outer, moe_inner)),
    )


def solution(mesh):
    in_specs = (
        P("grp", "ep", None, None, None),
        P("grp", "ep", None, None),
        P("grp", "ep", None),
        P("grp", "ep", None),
        P("grp", "ep", None, None, None),
        P("grp", "ep", None, None),
        P(),
        P("grp", "ep", None, None),
        P("grp", "ep", None, None),
        P("ep", None, None),
        P("ep", None, None),
        P("ep", None, None),
    )
    out_specs = (P("grp", "ep", None, None, None), P("grp", "ep", None, None))
    return jax.shard_map(body, mesh=mesh, in_specs=in_specs, out_specs=out_specs, check_vma=False)
```

time: 80.3 us -> 77.8 us (0.969)
  matrix products: 2.51 us -> 0 us
  other arithmetic: 3.52 us -> 1.45 us
  waiting for transfers between devices: 19.9 us -> 21.7 us
  Pallas kernels: 5.31 us -> 6.36 us
  local copies, waits for them, and re-layouts: 4.73 us -> 3.73 us
    dot_general x3 -> x0, matrix products: 2.51 us -> none  [the longest x1 1.3 us: attend_rows(): jnp.einsum('rhl,rtl->rht', questions, keys, preferred_element_type=jnp.fl...]
    pallas_call x0 -> x2, Pallas kernels: none -> 2.39 us  [the longest x1 1.44 us: body(): pl.pallas_call(attend_kernel, out_shape=(payload, payload, jax.ShapeDtype...]
    reshape x1 -> x0, local copies, waits for them, and re-layouts: 1.19 us -> none  [body(): received.reshape(count, width)]
    ppermute x4, waiting for transfers between devices: 9.14 us -> 10.2 us  [the longest x2 10.2 us: exchanged(): lax.ppermute(outer, 'grp', outer_pairs)]
    unnamed x28 -> x32, local copies, waits for them, and re-layouts: 2.71 us -> 3.72 us
    reduce_sum x4 -> x0, other arithmetic: 0.89 us -> none  [the longest x1 0.43 us: body(): jnp.sum(returned.reshape(experts_here, SLICES // cores, requests, width)....]
    ppermute x4, starting transfers between devices: 15 us -> 15.8 us  [the longest x2 10.5 us: exchanged(): lax.ppermute(outer, 'grp', outer_pairs)]
    all_to_all x1, waiting for transfers between devices: 7.12 us -> 7.94 us  [body(): lax.all_to_all(outgoing, 'ep', split_axis=0, concat_axis=0, axis_index_gr...]
  transfers between devices with their start and end apart: 9 -> 9, of which waited for: 4 -> 4; matrix products, arithmetic and copies ran while one was open for 8% -> 1% of each run, Pallas kernels for 0% -> 2%
where the time goes in v6:
time: 77.8 us; the launch traced here: 77.1 us
  starting transfers between devices  42.9 us (55%)
  waiting for transfers between devices  21.7 us (28%)
  Pallas kernels  6.36 us (8%)
  local copies, waits for them, and re-layouts  3.73 us (5%)
  other arithmetic  1.45 us (2%)
  between operations  0.9 us (1%)
    all_to_all x1, starting transfers between devices, body(): lax.all_to_all(outgoing, 'ep', split_axis=0, concat_axis=0, axis_index_gr...  16.3 us
    ppermute x2, starting transfers between devices, exchanged(): lax.ppermute(outer, 'grp', outer_pairs)  10.5 us
    ppermute x2, waiting for transfers between devices, exchanged(): lax.ppermute(outer, 'grp', outer_pairs)  10.2 us
    all_to_all x1, waiting for transfers between devices, body(): lax.all_to_all(outgoing, 'ep', split_axis=0, concat_axis=0, axis_index_gr...  7.94 us
    ppermute x3, starting transfers between devices, body(): traded = tuple((lax.ppermute(weight, 'ep', swap) for weight in weights))  6.25 us
    ppermute x2, starting transfers between devices, exchanged(): lax.ppermute(inner, 'grp', inner_pairs)  5.33 us
    all_to_all x1, starting transfers between devices, body(): lax.all_to_all(pair, 'ep', split_axis=0, concat_axis=0, axis_index_groups...  4.57 us
    unnamed x32, local copies, waits for them, and re-layouts  3.72 us
  transfers between devices with their start and end apart: 9, of which 4 were waited for; matrix products, arithmetic and copies ran while one was open for 1% of the time, Pallas kernels for 2%

profile of v6, /device:TPU:8, one launch (start us, length us, event | category | flops | bytes accessed | tf_op | source)
XLA Modules:
  0.0 77.1 jit_solution(16060927943114933643)
XLA Ops:
  0.6 0.8 %copy-done.3 = bf16[1,1,2,3584]{3,2,1,0:T(2,128)(2,1)S(1)} copy-done((bf16[1,1,2,3584]{3,2,1,0:T(2,128)(2,1)S(1)}, bf16[1,1,2,3584]{3,2,1,0:T(2,128)(2,1)}, u32[]{:S(2)}) %copy-start.3) | copy-done | bytes 14360
  1.4 0.8 %shard_map.131 = bf16[32,2,3584]{2,1,0:T(2,128)(2,1)} custom-call(bf16[2,3584]{1,0:T(2,128)(2,1)S(1)} %bitcast.26), custom_call_target="tpu_custom_call" | custom-call | tf_op jit(solution)/shard_map/pallas_call | solution.py:197
  2.2 16.3 %all-to-all-start = ((bf16[32,2,3584]{2,1,0:T(2,128)(2,1)}), bf16[32,2,3584]{2,1,0:T(2,128)(2,1)S(1)}, u32[]{:S(2)}, u32[]{:S(2)}) async-start(bf16[32,2,3584]{2,1,0:T(2,128)(2,1)} %shard_map.131), calls=%async_computation | async-start | bytes 917504 | tf_op jit(solution)/shard_map/all_to_all | solution.py:204
  18.6 1.9 %collective-permute-start = (bf16[3584,128]{1,0:T(8,128)(2,1)S(1)}, bf16[3584,128]{1,0:T(8,128)(2,1)}, u32[]{:S(2)}, u32[]{:S(2)}) collective-permute-start(bf16[3584,128]{1,0:T(8,128)(2,1)S(1)} %bitcast.20), channel_id=1, source_target_pairs={{0,1},{1,0},{2,3},{3,2},{4,5},{5,4},{6,7},{7,6},{8,9},{9,8},{10,11... | collective-permute-start | bytes 2752520 | tf_op jit(solution)/shard_map/ppermute | solution.py:209
  20.5 2.4 %collective-permute-start.1 = (bf16[3584,128]{1,0:T(8,128)(2,1)}, bf16[3584,128]{1,0:T(8,128)(2,1)}, u32[]{:S(2)}, u32[]{:S(2)}) collective-permute-start(bf16[3584,128]{1,0:T(8,128)(2,1)} %bitcast.22), channel_id=1, source_target_pairs={{0,1},{1,0},{2,3},{3,2},{4,5},{5,4},{6,7},{7,6},{8,9},{9,8},{10,11... | collective-permute-start | bytes 2752520 | tf_op jit(solution)/shard_map/ppermute | solution.py:209
  22.9 1.9 %collective-permute-start.2 = (bf16[128,3584]{1,0:T(8,128)(2,1)}, bf16[128,3584]{1,0:T(8,128)(2,1)}, u32[]{:S(2)}, u32[]{:S(2)}) collective-permute-start(bf16[128,3584]{1,0:T(8,128)(2,1)} %bitcast.24), channel_id=1, source_target_pairs={{0,1},{1,0},{2,3},{3,2},{4,5},{5,4},{6,7},{7,6},{8,9},{9,8},{10,11... | collective-permute-start | bytes 2752520 | tf_op jit(solution)/shard_map/ppermute | solution.py:209
  24.8 0.0 copy-start.12
  24.9 0.0 copy-start.14
  24.9 0.0 copy-start.11
  24.9 0.0 copy-start.4
  24.9 0.0 copy-start.13
  24.9 0.6 copy-done.12
  25.5 0.0 copy-done.11
  25.6 0.0 copy-done.13
  25.6 1.0 %copy-done.5 = bf16[1,1,4,64,576]{4,3,2,1,0:T(8,128)(2,1)S(1)} copy-done((bf16[1,1,4,64,576]{4,3,2,1,0:T(8,128)(2,1)S(1)}, bf16[1,1,4,64,576]{4,3,2,1,0:T(8,128)(2,1)}, u32[]{:S(2)}) %copy-start.5) | copy-done | bytes 294936
  26.6 1.4 %shard_map.132 = (bf16[80,512]{1,0:T(8,128)(2,1)S(1)}, bf16[80,512]{1,0:T(8,128)(2,1)S(1)}, bf16[2,64,512]{2,1,0:T(8,128)(2,1)S(1)}, f32[4,128]{1,0:T(4,128)S(1)}) custom-call(s32[2,2]{1,0:T(2,128)S(1)} %bitcast.33, s32[2]{0:T(128)S(1)} %bitcast.34, s32[2]{0:T(128)S(1)} %bitcast.27, s32[1]{0:T(128)} %bitcast.4.odd, s32[4,6]{1,0:T(4,128)S(1)} %bitcast.31, ...), custom_call_target="tpu_custom_call" | custom-call | flops 40000000000 | bytes 400000000 | tf_op jit(solution)/shard_map/pallas_call | solution.py:177
  28.0 0.6 copy-done.7
  28.6 0.6 copy-done.9
  29.3 7.9 %all-to-all-done.x = bf16[32,2,3584]{2,1,0:T(2,128)(2,1)S(1)} async-done(((bf16[32,2,3584]{2,1,0:T(2,128)(2,1)}), bf16[32,2,3584]{2,1,0:T(2,128)(2,1)S(1)}, u32[]{:S(2)}, u32[]{:S(2)}) %all-to-all-start) | async-done | bytes 458784 | tf_op jit(solution)/shard_map/all_to_all | solution.py:204
  37.3 3.2 %shard_map.133 = bf16[32,2,3584]{2,1,0:T(2,128)(2,1)} custom-call(bf16[32,2,3584]{2,1,0:T(2,128)(2,1)S(1)} %all-to-all-done.x, f32[1,3584]{1,0:T(1,128)S(1)} %broadcast_in_dim.11.gain, bf16[3584,128]{1,0:T(8,128)(2,1)S(1)} %bitcast.21, bf16[3584,128]{1,0:T(8,128)(2,1)S(1)} %bitcast.23, bf16[128,3584]{1,0:T(8,128)(2,1)S(1)} %bitcast.25, ...), custom_call_target="tpu_custom_call" | custom-call | tf_op jit(solution)/shard_map/pallas_call | solution.py:213
  40.4 0.0 copy-start.10
  40.5 4.6 %all-to-all-start.1 = ((bf16[32,2,3584]{2,1,0:T(2,128)(2,1)}), bf16[32,2,3584]{2,1,0:T(2,128)(2,1)S(1)}, u32[]{:S(2)}, u32[]{:S(2)}) async-start(bf16[32,2,3584]{2,1,0:T(2,128)(2,1)} %shard_map.133), calls=%async_computation.1 | async-start | bytes 917504 | tf_op jit(solution)/shard_map/all_to_all | solution.py:222
  45.0 5.6 %collective-permute-start.3 = (bf16[80,512]{1,0:T(8,128)(2,1)S(1)}, bf16[80,512]{1,0:T(8,128)(2,1)S(1)}, u32[]{:S(2)}, u32[]{:S(2)}) collective-permute-start(bf16[80,512]{1,0:T(8,128)(2,1)S(1)} %copy-done.10), channel_id=1, source_target_pairs={{0,448},{64,128},{128,64},{192,256},{256,192},{320,384},{384,320},... | collective-permute-start | bytes 245768 | tf_op jit(solution)/shard_map/ppermute | solution.py:167
  50.6 1.9 %collective-permute-start.4 = (bf16[80,512]{1,0:T(8,128)(2,1)S(1)}, bf16[80,512]{1,0:T(8,128)(2,1)S(1)}, u32[]{:S(2)}, u32[]{:S(2)}) collective-permute-start(bf16[80,512]{1,0:T(8,128)(2,1)S(1)} %copy-done.8), channel_id=1, source_target_pairs={{0,64},{64,0},{128,192},{192,128},{256,320},{320,256},{384,448},{4... | collective-permute-start | bytes 245768 | tf_op jit(solution)/shard_map/ppermute | solution.py:167
  52.6 8.1 %collective-permute-done.3.got_outer = bf16[80,512]{1,0:T(8,128)(2,1)S(1)} collective-permute-done((bf16[80,512]{1,0:T(8,128)(2,1)S(1)}, bf16[80,512]{1,0:T(8,128)(2,1)S(1)}, u32[]{:S(2)}, u32[]{:S(2)}) %collective-permute-start.3) | collective-permute-done | bytes 81952 | tf_op jit(solution)/shard_map/ppermute | solution.py:167
  60.7 3.6 %all-to-all-done.1.returned = bf16[32,2,3584]{2,1,0:T(2,128)(2,1)S(1)} async-done(((bf16[32,2,3584]{2,1,0:T(2,128)(2,1)}), bf16[32,2,3584]{2,1,0:T(2,128)(2,1)S(1)}, u32[]{:S(2)}, u32[]{:S(2)}) %all-to-all-start.1) | async-done | bytes 458784 | tf_op jit(solution)/shard_map/all_to_all | solution.py:222
  64.3 0.9 %shard_map.134 = (bf16[1,3584]{1,0:T(2,128)(2,1)S(1)}, bf16[1,3584]{1,0:T(2,128)(2,1)S(1)}, bf16[2,3584]{1,0:T(2,128)(2,1)S(1)}) custom-call(s32[2]{0:T(128)S(1)} %bitcast.28, s32[1]{0:T(128)} %bitcast.4.odd, bf16[32,2,3584]{2,1,0:T(2,128)(2,1)S(1)} %all-to-all-done.1.returned, f32[4,128]{1,0:T(4,128)S(1)} %get-tuple-element.34.mix, ...), custom_call_target="tpu_custom_call" | custom-call | tf_op jit(solution)/shard_map/pallas_call | solution.py:237
  65.3 3.4 %collective-permute-start.5 = (bf16[1,3584]{1,0:T(2,128)(2,1)S(1)}, bf16[1,3584]{1,0:T(2,128)(2,1)S(1)}, u32[]{:S(2)}, u32[]{:S(2)}) collective-permute-start(bf16[1,3584]{1,0:T(2,128)(2,1)S(1)} %get-tuple-element.36), channel_id=1, source_target_pairs={{0,64},{64,0},{128,192},{192,128},{256,320},{320,256},{384,448},{4... | collective-permute-start | bytes 21512 | tf_op jit(solution)/shard_map/ppermute | solution.py:167
  68.7 4.9 %collective-permute-start.6 = (bf16[1,3584]{1,0:T(2,128)(2,1)S(1)}, bf16[1,3584]{1,0:T(2,128)(2,1)S(1)}, u32[]{:S(2)}, u32[]{:S(2)}) collective-permute-start(bf16[1,3584]{1,0:T(2,128)(2,1)S(1)} %get-tuple-element.37), channel_id=1, source_target_pairs={{0,448},{64,128},{128,64},{192,256},{256,192},{320,384},{384,320},... | collective-permute-start | bytes 21512 | tf_op jit(solution)/shard_map/ppermute | solution.py:167
  73.6 0.7 maximum_bitcast_fusion
  74.4 2.0 %collective-permute-done.6 = bf16[1,3584]{1,0:T(2,128)(2,1)S(1)} collective-permute-done((bf16[1,3584]{1,0:T(2,128)(2,1)S(1)}, bf16[1,3584]{1,0:T(2,128)(2,1)S(1)}, u32[]{:S(2)}, u32[]{:S(2)}) %collective-permute-start.6) | collective-permute-done | bytes 7200 | tf_op jit(solution)/shard_map/ppermute | solution.py:167
  76.5 0.7 maximum_bitcast_fusion.1
  (27 shorter events, 0.1 us)
Async XLA Ops:
  0.6 17.9 %copy-start = (bf16[1,3584,128]{2,1,0:T(8,128)(2,1)S(1)}, bf16[1,3584,128]{2,1,0:T(8,128)(2,1)}, u32[]{:S(2)}) copy-start(bf16[1,3584,128]{2,1,0:T(8,128)(2,1)} %param.21) | copy-start | bytes 2752516
  0.6 0.8 %copy-start.3 = (bf16[1,1,2,3584]{3,2,1,0:T(2,128)(2,1)S(1)}, bf16[1,1,2,3584]{3,2,1,0:T(2,128)(2,1)}, u32[]{:S(2)}) copy-start(bf16[1,1,2,3584]{3,2,1,0:T(2,128)(2,1)} %param.17) | copy-start | bytes 43012
  2.2 22.7 %copy-start.6 = (bf16[1,1,2,64,576]{4,3,2,1,0:T(8,128)(2,1)S(1)}, bf16[1,1,2,64,576]{4,3,2,1,0:T(8,128)(2,1)}, u32[]{:S(2)}) copy-start(bf16[1,1,2,64,576]{4,3,2,1,0:T(8,128)(2,1)} %param.16) | copy-start | bytes 442372
  2.2 35.0 %all-to-all-start = ((bf16[32,2,3584]{2,1,0:T(2,128)(2,1)}), bf16[32,2,3584]{2,1,0:T(2,128)(2,1)S(1)}, u32[]{:S(2)}, u32[]{:S(2)}) async-start(bf16[32,2,3584]{2,1,0:T(2,128)(2,1)} %shard_map.131), calls=%async_computation | async-start | bytes 917504 | tf_op jit(solution)/shard_map/all_to_all | solution.py:204
  18.6 18.7 %collective-permute-start = (bf16[3584,128]{1,0:T(8,128)(2,1)S(1)}, bf16[3584,128]{1,0:T(8,128)(2,1)}, u32[]{:S(2)}, u32[]{:S(2)}) collective-permute-start(bf16[3584,128]{1,0:T(8,128)(2,1)S(1)} %bitcast.20), channel_id=1, source_target_pairs={{0,1},{1,0},{2,3},{3,2},{4,5},{5,4},{6,7},{7,6},{8,9},{9,8},{10,11... | collective-permute-start | bytes 2752520 | tf_op jit(solution)/shard_map/ppermute | solution.py:209
  20.5 16.7 %collective-permute-start.1 = (bf16[3584,128]{1,0:T(8,128)(2,1)}, bf16[3584,128]{1,0:T(8,128)(2,1)}, u32[]{:S(2)}, u32[]{:S(2)}) collective-permute-start(bf16[3584,128]{1,0:T(8,128)(2,1)} %bitcast.22), channel_id=1, source_target_pairs={{0,1},{1,0},{2,3},{3,2},{4,5},{5,4},{6,7},{7,6},{8,9},{9,8},{10,11... | collective-permute-start | bytes 2752520 | tf_op jit(solution)/shard_map/ppermute | solution.py:209
  22.9 14.3 %collective-permute-start.2 = (bf16[128,3584]{1,0:T(8,128)(2,1)}, bf16[128,3584]{1,0:T(8,128)(2,1)}, u32[]{:S(2)}, u32[]{:S(2)}) collective-permute-start(bf16[128,3584]{1,0:T(8,128)(2,1)} %bitcast.24), channel_id=1, source_target_pairs={{0,1},{1,0},{2,3},{3,2},{4,5},{5,4},{6,7},{7,6},{8,9},{9,8},{10,11... | collective-permute-start | bytes 2752520 | tf_op jit(solution)/shard_map/ppermute | solution.py:209
  24.8 0.7 copy-start.12
  24.9 0.7 copy-start.14
  24.9 0.7 copy-start.11
  24.9 0.7 copy-start.4
  24.9 0.7 copy-start.13
  25.6 1.0 %copy-start.5 = (bf16[1,1,4,64,576]{4,3,2,1,0:T(8,128)(2,1)S(1)}, bf16[1,1,4,64,576]{4,3,2,1,0:T(8,128)(2,1)}, u32[]{:S(2)}) copy-start(bf16[1,1,4,64,576]{4,3,2,1,0:T(8,128)(2,1)} %param.12) | copy-start | bytes 884740
  26.6 2.7 %copy-start.15 = (f32[3584]{0:T(1024)S(1)}, f32[3584]{0:T(1024)}, u32[]{:S(2)}) copy-start(f32[3584]{0:T(1024)} %param.18) | copy-start | bytes 43012
  26.6 10.7 %copy-start.1 = (bf16[1,3584,128]{2,1,0:T(8,128)(2,1)S(1)}, bf16[1,3584,128]{2,1,0:T(8,128)(2,1)}, u32[]{:S(2)}) copy-start(bf16[1,3584,128]{2,1,0:T(8,128)(2,1)} %param.22) | copy-start | bytes 2752516
  26.6 10.7 %copy-start.2 = (bf16[1,128,3584]{2,1,0:T(8,128)(2,1)S(1)}, bf16[1,128,3584]{2,1,0:T(8,128)(2,1)}, u32[]{:S(2)}) copy-start(bf16[1,128,3584]{2,1,0:T(8,128)(2,1)} %param.23) | copy-start | bytes 2752516
  28.0 0.6 copy-start.7
  28.6 0.6 copy-start.9
  40.4 4.6 %copy-start.10 = (bf16[80,512]{1,0:T(8,128)(2,1)S(1)}, bf16[80,512]{1,0:T(8,128)(2,1)}, u32[]{:S(2)}) copy-start(bf16[80,512]{1,0:T(8,128)(2,1)} %copy-done.9) | copy-start | bytes 245764
  40.4 10.2 %copy-start.8 = (bf16[80,512]{1,0:T(8,128)(2,1)S(1)}, bf16[80,512]{1,0:T(8,128)(2,1)}, u32[]{:S(2)}) copy-start(bf16[80,512]{1,0:T(8,128)(2,1)} %copy-done.7) | copy-start | bytes 245764
  40.5 23.9 %all-to-all-start.1 = ((bf16[32,2,3584]{2,1,0:T(2,128)(2,1)}), bf16[32,2,3584]{2,1,0:T(2,128)(2,1)S(1)}, u32[]{:S(2)}, u32[]{:S(2)}) async-start(bf16[32,2,3584]{2,1,0:T(2,128)(2,1)} %shard_map.133), calls=%async_computation.1 | async-start | bytes 917504 | tf_op jit(solution)/shard_map/all_to_all | solution.py:222
  45.0 15.7 %collective-permute-start.3 = (bf16[80,512]{1,0:T(8,128)(2,1)S(1)}, bf16[80,512]{1,0:T(8,128)(2,1)S(1)}, u32[]{:S(2)}, u32[]{:S(2)}) collective-permute-start(bf16[80,512]{1,0:T(8,128)(2,1)S(1)} %copy-done.10), channel_id=1, source_target_pairs={{0,448},{64,128},{128,64},{192,256},{256,192},{320,384},{384,320},... | collective-permute-start | bytes 245768 | tf_op jit(solution)/shard_map/ppermute | solution.py:167
  50.6 10.1 %collective-permute-start.4 = (bf16[80,512]{1,0:T(8,128)(2,1)S(1)}, bf16[80,512]{1,0:T(8,128)(2,1)S(1)}, u32[]{:S(2)}, u32[]{:S(2)}) collective-permute-start(bf16[80,512]{1,0:T(8,128)(2,1)S(1)} %copy-done.8), channel_id=1, source_target_pairs={{0,64},{64,0},{128,192},{192,128},{256,320},{320,256},{384,448},{4... | collective-permute-start | bytes 245768 | tf_op jit(solution)/shard_map/ppermute | solution.py:167
  65.3 9.1 %collective-permute-start.5 = (bf16[1,3584]{1,0:T(2,128)(2,1)S(1)}, bf16[1,3584]{1,0:T(2,128)(2,1)S(1)}, u32[]{:S(2)}, u32[]{:S(2)}) collective-permute-start(bf16[1,3584]{1,0:T(2,128)(2,1)S(1)} %get-tuple-element.36), channel_id=1, source_target_pairs={{0,64},{64,0},{128,192},{192,128},{256,320},{320,256},{384,448},{4... | collective-permute-start | bytes 21512 | tf_op jit(solution)/shard_map/ppermute | solution.py:167
  68.7 7.7 %collective-permute-start.6 = (bf16[1,3584]{1,0:T(2,128)(2,1)S(1)}, bf16[1,3584]{1,0:T(2,128)(2,1)S(1)}, u32[]{:S(2)}, u32[]{:S(2)}) collective-permute-start(bf16[1,3584]{1,0:T(2,128)(2,1)S(1)} %get-tuple-element.37), channel_id=1, source_target_pairs={{0,448},{64,128},{128,64},{192,256},{256,192},{320,384},{384,320},... | collective-permute-start | bytes 21512 | tf_op jit(solution)/shard_map/ppermute | solution.py:167

commit v7 on v6

--- a/solution.py
+++ b/solution.py
@@ -44,11 +44,18 @@
         probs = (expo / jnp.sum(expo, axis=1, keepdims=True)).astype(jnp.bfloat16)
         results.append(dot(probs, keys[:, :VDIM]))
         stay[j] = jnp.where(moves[j] == 0, results[j], jnp.zeros_like(results[j])).astype(jnp.bfloat16)
-    lane = lax.broadcasted_iota(jnp.int32, mix.shape, 1)
-    total = jnp.zeros(mix.shape, jnp.float32)
+    rows = ids.shape[0]
+    lane = lax.broadcasted_iota(jnp.int32, (rows, mix.shape[1]), 1)
+    total = jnp.zeros(lane.shape, jnp.float32)
     for k in range(ids.shape[1]):
         total = total + jnp.where(ids[:, k : k + 1] == lane, gates[:, k : k + 1], 0.0)
-    mix[...] = total
+    mix[:rows] = total
+    flags = [moves[j] for j in range(requests)] + [odd[0]]
+    place = lax.broadcasted_iota(jnp.int32, (mix.shape[0] - rows, mix.shape[1]), 0)
+    kept = jnp.zeros(place.shape, jnp.int32)
+    for j, flag in enumerate(flags):
+        kept = jnp.where(place == j, flag, kept)
+    mix[rows:] = kept.astype(jnp.float32)
     high = total.astype(jnp.bfloat16).astype(jnp.float32)
     middle = (total - high).astype(jnp.bfloat16).astype(jnp.float32)
     low = total - high - middle
@@ -85,10 +92,12 @@
     out[...] = total.astype(jnp.bfloat16).reshape(out.shape)
 
 
-def gather_kernel(experts_here, moves, odd, returned, mix, got_outer, got_inner, outer, inner, stay):
+def gather_kernel(experts, returned, mix, got_outer, got_inner, outer, inner, stay):
     chips, requests, width = returned.shape
-    experts = experts_here
-    is_odd = odd[0] == 1
+    rows_served = mix.shape[0] - requests - 2
+    moves = [mix[rows_served + j : rows_served + j + 1] for j in range(requests)]
+    odd = mix[rows_served + requests : rows_served + requests + 1]
+    is_odd = odd == 1.0
     heads = got_outer.shape[0] - BEHIND
 
     def mix_of(got):
@@ -117,6 +126,8 @@
     low = (rest - middle.astype(jnp.float32)).astype(jnp.bfloat16)
     moe = dot(high, flat) + dot(middle, flat) + dot(low, flat)
     rows = [moe[j : j + 1] for j in range(requests)]
+    moves = [jnp.broadcast_to(move[:, :1], (1, width)) for move in moves]
+    is_odd = jnp.broadcast_to(odd[:, :1], (1, width)) == 1.0
     forward, backward = one_of(rows, moves, 1), one_of(rows, moves, 2)
     outer[...] = jnp.where(is_odd, forward, backward).astype(jnp.bfloat16)
     inner[...] = jnp.where(is_odd, backward, forward).astype(jnp.bfloat16)
@@ -180,7 +191,7 @@
             payload,
             payload,
             jax.ShapeDtypeStruct((requests, heads, VDIM), jnp.bfloat16),
-            jax.ShapeDtypeStruct((expert_ids.shape[2], 128), jnp.float32),
+            jax.ShapeDtypeStruct((expert_ids.shape[2] + requests + 2, 128), jnp.float32),
         ),
         in_specs=in_smem(4) + in_vmem(4),
         out_specs=tuple(in_vmem(4)),
@@ -237,10 +248,10 @@
     moe_outer, moe_inner, moe_stay = pl.pallas_call(
         functools.partial(gather_kernel, devices // SLICES),
         out_shape=(line, line, jax.ShapeDtypeStruct((requests, width), jnp.bfloat16)),
-        in_specs=in_smem(2) + in_vmem(4),
+        in_specs=in_vmem(4),
         out_specs=tuple(in_vmem(3)),
         compiler_params=SMALL,
-    )(moves, group_odd, returned, mix, got_outer, got_inner)
+    )(returned, mix, got_outer, got_inner)
     return (
         served(attn_stay, got_outer[None, :heads], got_inner[None, :heads]),
         served(moe_stay, *exchanged(moe_outer, moe_inner)),

time: 77.8 us -> 77.2 us (level)
  no operation moved by 1% of the time
where the time goes in v7:
time: 77.2 us; the launch traced here: 76.6 us
  starting transfers between devices  42.9 us (56%)
  waiting for transfers between devices  21.8 us (28%)
  Pallas kernels  5.82 us (8%)
  local copies, waits for them, and re-layouts  3.72 us (5%)
  other arithmetic  1.45 us (2%)
  between operations  0.89 us (1%)
    all_to_all x1, starting transfers between devices, body(): lax.all_to_all(outgoing, 'ep', split_axis=0, concat_axis=0, axis_index_gr...  16.3 us
    ppermute x2, starting transfers between devices, exchanged(): lax.ppermute(outer, 'grp', outer_pairs)  10.5 us
    ppermute x2, waiting for transfers between devices, exchanged(): lax.ppermute(outer, 'grp', outer_pairs)  10.2 us
    all_to_all x1, waiting for transfers between devices, body(): lax.all_to_all(outgoing, 'ep', split_axis=0, concat_axis=0, axis_index_gr...  7.95 us
    ppermute x3, starting transfers between devices, body(): traded = tuple((lax.ppermute(weight, 'ep', swap) for weight in weights))  6.25 us
    ppermute x2, starting transfers between devices, exchanged(): lax.ppermute(inner, 'grp', inner_pairs)  5.31 us
    all_to_all x1, starting transfers between devices, body(): lax.all_to_all(pair, 'ep', split_axis=0, concat_axis=0, axis_index_groups...  4.57 us
    unnamed x32, local copies, waits for them, and re-layouts  3.71 us
  transfers between devices with their start and end apart: 9, of which 4 were waited for; matrix products, arithmetic and copies ran while one was open for 1% of the time, Pallas kernels for 2%

profile of v7, /device:TPU:8, one launch (start us, length us, event | category | flops | bytes accessed | tf_op | source)
XLA Modules:
  0.0 76.6 jit_solution(15729106460316755150)
XLA Ops:
  0.6 0.8 %copy-done.3 = bf16[1,1,2,3584]{3,2,1,0:T(2,128)(2,1)S(1)} copy-done((bf16[1,1,2,3584]{3,2,1,0:T(2,128)(2,1)S(1)}, bf16[1,1,2,3584]{3,2,1,0:T(2,128)(2,1)}, u32[]{:S(2)}) %copy-start.3) | copy-done | bytes 14360
  1.4 0.8 %shard_map.131 = bf16[32,2,3584]{2,1,0:T(2,128)(2,1)} custom-call(bf16[2,3584]{1,0:T(2,128)(2,1)S(1)} %bitcast.26), custom_call_target="tpu_custom_call" | custom-call | tf_op jit(solution)/shard_map/pallas_call | solution.py:208
  2.2 16.3 %all-to-all-start = ((bf16[32,2,3584]{2,1,0:T(2,128)(2,1)}), bf16[32,2,3584]{2,1,0:T(2,128)(2,1)S(1)}, u32[]{:S(2)}, u32[]{:S(2)}) async-start(bf16[32,2,3584]{2,1,0:T(2,128)(2,1)} %shard_map.131), calls=%async_computation | async-start | bytes 917504 | tf_op jit(solution)/shard_map/all_to_all | solution.py:215
  18.6 1.9 %collective-permute-start = (bf16[3584,128]{1,0:T(8,128)(2,1)S(1)}, bf16[3584,128]{1,0:T(8,128)(2,1)}, u32[]{:S(2)}, u32[]{:S(2)}) collective-permute-start(bf16[3584,128]{1,0:T(8,128)(2,1)S(1)} %bitcast.20), channel_id=1, source_target_pairs={{0,1},{1,0},{2,3},{3,2},{4,5},{5,4},{6,7},{7,6},{8,9},{9,8},{10,11... | collective-permute-start | bytes 2752520 | tf_op jit(solution)/shard_map/ppermute | solution.py:220
  20.5 2.4 %collective-permute-start.1 = (bf16[3584,128]{1,0:T(8,128)(2,1)}, bf16[3584,128]{1,0:T(8,128)(2,1)}, u32[]{:S(2)}, u32[]{:S(2)}) collective-permute-start(bf16[3584,128]{1,0:T(8,128)(2,1)} %bitcast.22), channel_id=1, source_target_pairs={{0,1},{1,0},{2,3},{3,2},{4,5},{5,4},{6,7},{7,6},{8,9},{9,8},{10,11... | collective-permute-start | bytes 2752520 | tf_op jit(solution)/shard_map/ppermute | solution.py:220
  22.9 1.9 %collective-permute-start.2 = (bf16[128,3584]{1,0:T(8,128)(2,1)}, bf16[128,3584]{1,0:T(8,128)(2,1)}, u32[]{:S(2)}, u32[]{:S(2)}) collective-permute-start(bf16[128,3584]{1,0:T(8,128)(2,1)} %bitcast.24), channel_id=1, source_target_pairs={{0,1},{1,0},{2,3},{3,2},{4,5},{5,4},{6,7},{7,6},{8,9},{9,8},{10,11... | collective-permute-start | bytes 2752520 | tf_op jit(solution)/shard_map/ppermute | solution.py:220
  24.8 0.0 copy-start.11
  24.9 0.0 copy-start.14
  24.9 0.0 copy-start.10
  24.9 0.0 copy-start.12
  24.9 0.0 copy-start.13
  24.9 0.6 copy-done.11
  25.5 0.0 copy-done.10
  25.6 0.0 copy-done.12
  25.6 1.0 %copy-done.4 = bf16[1,1,4,64,576]{4,3,2,1,0:T(8,128)(2,1)S(1)} copy-done((bf16[1,1,4,64,576]{4,3,2,1,0:T(8,128)(2,1)S(1)}, bf16[1,1,4,64,576]{4,3,2,1,0:T(8,128)(2,1)}, u32[]{:S(2)}) %copy-start.4) | copy-done | bytes 294936
  26.6 1.4 %shard_map.132 = (bf16[80,512]{1,0:T(8,128)(2,1)S(1)}, bf16[80,512]{1,0:T(8,128)(2,1)S(1)}, bf16[2,64,512]{2,1,0:T(8,128)(2,1)S(1)}, f32[8,128]{1,0:T(8,128)S(1)}) custom-call(s32[2,2]{1,0:T(2,128)S(1)} %bitcast.31, s32[2]{0:T(128)S(1)} %bitcast.32, s32[2]{0:T(128)S(1)} %bitcast.33, s32[1]{0:T(128)} %bitcast.4.odd, s32[4,6]{1,0:T(4,128)S(1)} %bitcast.29, ...), custom_call_target="tpu_custom_call" | custom-call | flops 40000000000 | bytes 400000000 | tf_op jit(solution)/shard_map/pallas_call | solution.py:188
  28.0 0.6 copy-done.6
  28.6 0.6 copy-done.8
  29.3 7.9 %all-to-all-done.x = bf16[32,2,3584]{2,1,0:T(2,128)(2,1)S(1)} async-done(((bf16[32,2,3584]{2,1,0:T(2,128)(2,1)}), bf16[32,2,3584]{2,1,0:T(2,128)(2,1)S(1)}, u32[]{:S(2)}, u32[]{:S(2)}) %all-to-all-start) | async-done | bytes 458784 | tf_op jit(solution)/shard_map/all_to_all | solution.py:215
  37.3 3.2 %shard_map.133 = bf16[32,2,3584]{2,1,0:T(2,128)(2,1)} custom-call(bf16[32,2,3584]{2,1,0:T(2,128)(2,1)S(1)} %all-to-all-done.x, f32[1,3584]{1,0:T(1,128)S(1)} %broadcast_in_dim.11.gain, bf16[3584,128]{1,0:T(8,128)(2,1)S(1)} %bitcast.21, bf16[3584,128]{1,0:T(8,128)(2,1)S(1)} %bitcast.23, bf16[128,3584]{1,0:T(8,128)(2,1)S(1)} %bitcast.25, ...), custom_call_target="tpu_custom_call" | custom-call | tf_op jit(solution)/shard_map/pallas_call | solution.py:224
  40.4 0.0 copy-start.9
  40.5 4.6 %all-to-all-start.1 = ((bf16[32,2,3584]{2,1,0:T(2,128)(2,1)}), bf16[32,2,3584]{2,1,0:T(2,128)(2,1)S(1)}, u32[]{:S(2)}, u32[]{:S(2)}) async-start(bf16[32,2,3584]{2,1,0:T(2,128)(2,1)} %shard_map.133), calls=%async_computation.1 | async-start | bytes 917504 | tf_op jit(solution)/shard_map/all_to_all | solution.py:233
  45.0 5.6 %collective-permute-start.3 = (bf16[80,512]{1,0:T(8,128)(2,1)S(1)}, bf16[80,512]{1,0:T(8,128)(2,1)S(1)}, u32[]{:S(2)}, u32[]{:S(2)}) collective-permute-start(bf16[80,512]{1,0:T(8,128)(2,1)S(1)} %copy-done.9), channel_id=1, source_target_pairs={{0,448},{64,128},{128,64},{192,256},{256,192},{320,384},{384,320},... | collective-permute-start | bytes 245768 | tf_op jit(solution)/shard_map/ppermute | solution.py:178
  50.6 1.9 %collective-permute-start.4 = (bf16[80,512]{1,0:T(8,128)(2,1)S(1)}, bf16[80,512]{1,0:T(8,128)(2,1)S(1)}, u32[]{:S(2)}, u32[]{:S(2)}) collective-permute-start(bf16[80,512]{1,0:T(8,128)(2,1)S(1)} %copy-done.7), channel_id=1, source_target_pairs={{0,64},{64,0},{128,192},{192,128},{256,320},{320,256},{384,448},{4... | collective-permute-start | bytes 245768 | tf_op jit(solution)/shard_map/ppermute | solution.py:178
  52.6 8.1 %collective-permute-done.3.got_outer = bf16[80,512]{1,0:T(8,128)(2,1)S(1)} collective-permute-done((bf16[80,512]{1,0:T(8,128)(2,1)S(1)}, bf16[80,512]{1,0:T(8,128)(2,1)S(1)}, u32[]{:S(2)}, u32[]{:S(2)}) %collective-permute-start.3) | collective-permute-done | bytes 81952 | tf_op jit(solution)/shard_map/ppermute | solution.py:178
  60.7 3.6 %all-to-all-done.1.returned = bf16[32,2,3584]{2,1,0:T(2,128)(2,1)S(1)} async-done(((bf16[32,2,3584]{2,1,0:T(2,128)(2,1)}), bf16[32,2,3584]{2,1,0:T(2,128)(2,1)S(1)}, u32[]{:S(2)}, u32[]{:S(2)}) %all-to-all-start.1) | async-done | bytes 458784 | tf_op jit(solution)/shard_map/all_to_all | solution.py:233
  64.3 0.4 shard_map.134
  64.7 3.4 %collective-permute-start.5 = (bf16[1,3584]{1,0:T(2,128)(2,1)S(1)}, bf16[1,3584]{1,0:T(2,128)(2,1)S(1)}, u32[]{:S(2)}, u32[]{:S(2)}) collective-permute-start(bf16[1,3584]{1,0:T(2,128)(2,1)S(1)} %get-tuple-element.36), channel_id=1, source_target_pairs={{0,64},{64,0},{128,192},{192,128},{256,320},{320,256},{384,448},{4... | collective-permute-start | bytes 21512 | tf_op jit(solution)/shard_map/ppermute | solution.py:178
  68.2 4.9 %collective-permute-start.6 = (bf16[1,3584]{1,0:T(2,128)(2,1)S(1)}, bf16[1,3584]{1,0:T(2,128)(2,1)S(1)}, u32[]{:S(2)}, u32[]{:S(2)}) collective-permute-start(bf16[1,3584]{1,0:T(2,128)(2,1)S(1)} %get-tuple-element.37), channel_id=1, source_target_pairs={{0,448},{64,128},{128,64},{192,256},{256,192},{320,384},{384,320},... | collective-permute-start | bytes 21512 | tf_op jit(solution)/shard_map/ppermute | solution.py:178
  73.1 0.7 maximum_bitcast_fusion
  73.8 2.1 %collective-permute-done.6 = bf16[1,3584]{1,0:T(2,128)(2,1)S(1)} collective-permute-done((bf16[1,3584]{1,0:T(2,128)(2,1)S(1)}, bf16[1,3584]{1,0:T(2,128)(2,1)S(1)}, u32[]{:S(2)}, u32[]{:S(2)}) %collective-permute-start.6) | collective-permute-done | bytes 7200 | tf_op jit(solution)/shard_map/ppermute | solution.py:178
  75.9 0.7 maximum_bitcast_fusion.1
  (27 shorter events, 0.1 us)
Async XLA Ops:
  0.6 17.9 %copy-start = (bf16[1,3584,128]{2,1,0:T(8,128)(2,1)S(1)}, bf16[1,3584,128]{2,1,0:T(8,128)(2,1)}, u32[]{:S(2)}) copy-start(bf16[1,3584,128]{2,1,0:T(8,128)(2,1)} %param.21) | copy-start | bytes 2752516
  0.6 0.8 %copy-start.3 = (bf16[1,1,2,3584]{3,2,1,0:T(2,128)(2,1)S(1)}, bf16[1,1,2,3584]{3,2,1,0:T(2,128)(2,1)}, u32[]{:S(2)}) copy-start(bf16[1,1,2,3584]{3,2,1,0:T(2,128)(2,1)} %param.17) | copy-start | bytes 43012
  2.2 22.7 %copy-start.5 = (bf16[1,1,2,64,576]{4,3,2,1,0:T(8,128)(2,1)S(1)}, bf16[1,1,2,64,576]{4,3,2,1,0:T(8,128)(2,1)}, u32[]{:S(2)}) copy-start(bf16[1,1,2,64,576]{4,3,2,1,0:T(8,128)(2,1)} %param.16) | copy-start | bytes 442372
  2.2 35.0 %all-to-all-start = ((bf16[32,2,3584]{2,1,0:T(2,128)(2,1)}), bf16[32,2,3584]{2,1,0:T(2,128)(2,1)S(1)}, u32[]{:S(2)}, u32[]{:S(2)}) async-start(bf16[32,2,3584]{2,1,0:T(2,128)(2,1)} %shard_map.131), calls=%async_computation | async-start | bytes 917504 | tf_op jit(solution)/shard_map/all_to_all | solution.py:215
  18.6 18.7 %collective-permute-start = (bf16[3584,128]{1,0:T(8,128)(2,1)S(1)}, bf16[3584,128]{1,0:T(8,128)(2,1)}, u32[]{:S(2)}, u32[]{:S(2)}) collective-permute-start(bf16[3584,128]{1,0:T(8,128)(2,1)S(1)} %bitcast.20), channel_id=1, source_target_pairs={{0,1},{1,0},{2,3},{3,2},{4,5},{5,4},{6,7},{7,6},{8,9},{9,8},{10,11... | collective-permute-start | bytes 2752520 | tf_op jit(solution)/shard_map/ppermute | solution.py:220
  20.5 16.7 %collective-permute-start.1 = (bf16[3584,128]{1,0:T(8,128)(2,1)}, bf16[3584,128]{1,0:T(8,128)(2,1)}, u32[]{:S(2)}, u32[]{:S(2)}) collective-permute-start(bf16[3584,128]{1,0:T(8,128)(2,1)} %bitcast.22), channel_id=1, source_target_pairs={{0,1},{1,0},{2,3},{3,2},{4,5},{5,4},{6,7},{7,6},{8,9},{9,8},{10,11... | collective-permute-start | bytes 2752520 | tf_op jit(solution)/shard_map/ppermute | solution.py:220
  22.9 14.3 %collective-permute-start.2 = (bf16[128,3584]{1,0:T(8,128)(2,1)}, bf16[128,3584]{1,0:T(8,128)(2,1)}, u32[]{:S(2)}, u32[]{:S(2)}) collective-permute-start(bf16[128,3584]{1,0:T(8,128)(2,1)} %bitcast.24), channel_id=1, source_target_pairs={{0,1},{1,0},{2,3},{3,2},{4,5},{5,4},{6,7},{7,6},{8,9},{9,8},{10,11... | collective-permute-start | bytes 2752520 | tf_op jit(solution)/shard_map/ppermute | solution.py:220
  24.8 0.7 copy-start.11
  24.9 0.7 copy-start.14
  24.9 0.7 copy-start.10
  24.9 0.7 copy-start.12
  24.9 0.7 copy-start.13
  25.6 1.0 %copy-start.4 = (bf16[1,1,4,64,576]{4,3,2,1,0:T(8,128)(2,1)S(1)}, bf16[1,1,4,64,576]{4,3,2,1,0:T(8,128)(2,1)}, u32[]{:S(2)}) copy-start(bf16[1,1,4,64,576]{4,3,2,1,0:T(8,128)(2,1)} %param.12) | copy-start | bytes 884740
  26.6 2.7 %copy-start.15 = (f32[3584]{0:T(1024)S(1)}, f32[3584]{0:T(1024)}, u32[]{:S(2)}) copy-start(f32[3584]{0:T(1024)} %param.18) | copy-start | bytes 43012
  26.6 10.7 %copy-start.1 = (bf16[1,3584,128]{2,1,0:T(8,128)(2,1)S(1)}, bf16[1,3584,128]{2,1,0:T(8,128)(2,1)}, u32[]{:S(2)}) copy-start(bf16[1,3584,128]{2,1,0:T(8,128)(2,1)} %param.22) | copy-start | bytes 2752516
  26.6 10.7 %copy-start.2 = (bf16[1,128,3584]{2,1,0:T(8,128)(2,1)S(1)}, bf16[1,128,3584]{2,1,0:T(8,128)(2,1)}, u32[]{:S(2)}) copy-start(bf16[1,128,3584]{2,1,0:T(8,128)(2,1)} %param.23) | copy-start | bytes 2752516
  28.0 0.6 copy-start.6
  28.6 0.6 copy-start.8
  40.4 4.6 %copy-start.9 = (bf16[80,512]{1,0:T(8,128)(2,1)S(1)}, bf16[80,512]{1,0:T(8,128)(2,1)}, u32[]{:S(2)}) copy-start(bf16[80,512]{1,0:T(8,128)(2,1)} %copy-done.8) | copy-start | bytes 245764
  40.4 10.2 %copy-start.7 = (bf16[80,512]{1,0:T(8,128)(2,1)S(1)}, bf16[80,512]{1,0:T(8,128)(2,1)}, u32[]{:S(2)}) copy-start(bf16[80,512]{1,0:T(8,128)(2,1)} %copy-done.6) | copy-start | bytes 245764
  40.5 23.9 %all-to-all-start.1 = ((bf16[32,2,3584]{2,1,0:T(2,128)(2,1)}), bf16[32,2,3584]{2,1,0:T(2,128)(2,1)S(1)}, u32[]{:S(2)}, u32[]{:S(2)}) async-start(bf16[32,2,3584]{2,1,0:T(2,128)(2,1)} %shard_map.133), calls=%async_computation.1 | async-start | bytes 917504 | tf_op jit(solution)/shard_map/all_to_all | solution.py:233
  45.0 15.7 %collective-permute-start.3 = (bf16[80,512]{1,0:T(8,128)(2,1)S(1)}, bf16[80,512]{1,0:T(8,128)(2,1)S(1)}, u32[]{:S(2)}, u32[]{:S(2)}) collective-permute-start(bf16[80,512]{1,0:T(8,128)(2,1)S(1)} %copy-done.9), channel_id=1, source_target_pairs={{0,448},{64,128},{128,64},{192,256},{256,192},{320,384},{384,320},... | collective-permute-start | bytes 245768 | tf_op jit(solution)/shard_map/ppermute | solution.py:178
  50.6 10.1 %collective-permute-start.4 = (bf16[80,512]{1,0:T(8,128)(2,1)S(1)}, bf16[80,512]{1,0:T(8,128)(2,1)S(1)}, u32[]{:S(2)}, u32[]{:S(2)}) collective-permute-start(bf16[80,512]{1,0:T(8,128)(2,1)S(1)} %copy-done.7), channel_id=1, source_target_pairs={{0,64},{64,0},{128,192},{192,128},{256,320},{320,256},{384,448},{4... | collective-permute-start | bytes 245768 | tf_op jit(solution)/shard_map/ppermute | solution.py:178
  64.7 9.1 %collective-permute-start.5 = (bf16[1,3584]{1,0:T(2,128)(2,1)S(1)}, bf16[1,3584]{1,0:T(2,128)(2,1)S(1)}, u32[]{:S(2)}, u32[]{:S(2)}) collective-permute-start(bf16[1,3584]{1,0:T(2,128)(2,1)S(1)} %get-tuple-element.36), channel_id=1, source_target_pairs={{0,64},{64,0},{128,192},{192,128},{256,320},{320,256},{384,448},{4... | collective-permute-start | bytes 21512 | tf_op jit(solution)/shard_map/ppermute | solution.py:178
  68.2 7.7 %collective-permute-start.6 = (bf16[1,3584]{1,0:T(2,128)(2,1)S(1)}, bf16[1,3584]{1,0:T(2,128)(2,1)S(1)}, u32[]{:S(2)}, u32[]{:S(2)}) collective-permute-start(bf16[1,3584]{1,0:T(2,128)(2,1)S(1)} %get-tuple-element.37), channel_id=1, source_target_pairs={{0,448},{64,128},{128,64},{192,256},{256,192},{320,384},{384,320},... | collective-permute-start | bytes 21512 | tf_op jit(solution)/shard_map/ppermute | solution.py:178

commit v8 on v7

--- a/solution.py
+++ b/solution.py
@@ -11,6 +11,7 @@
 QK_DIM = 192
 SLICES = 8
 BEHIND = 16
+PIECES = 2
 
 
 def dot(left, right):
@@ -72,7 +73,7 @@
 
 
 def experts_kernel(
-    x, gain, gate_a, up_a, down_a, gate_there, up_there, down_there, out, gate_b, up_b, down_b, sems
+    x, gain, gate_a, up_a, down_a, gate_there, up_there, down_there, out, gate_b, up_b, down_b, pieces, sems, out_sems
 ):
     pairs = ((gate_there, gate_b), (up_there, up_b), (down_there, down_b))
     copies = [pltpu.make_async_copy(*pair, sems.at[i]) for i, pair in enumerate(pairs)]
@@ -88,8 +89,16 @@
     copies[1].wait()
     act = (jax.nn.silu(gate) * dot(normed, up_b[...])).astype(jnp.bfloat16)
     copies[2].wait()
-    total = total + dot(act, down_b[...])
-    out[...] = total.astype(jnp.bfloat16).reshape(out.shape)
+    leaving = []
+    for i in range(PIECES):
+        size = out.shape[2] // PIECES
+        columns = slice(i * size, (i + 1) * size)
+        piece = total[:, columns] + dot(act, down_b[:, columns])
+        pieces[i] = piece.astype(jnp.bfloat16).reshape(pieces.shape[1:])
+        leaving.append(pltpu.make_async_copy(pieces.at[i], out.at[:, :, columns], out_sems.at[i]))
+        leaving[i].start()
+    for copy in leaving:
+        copy.wait()
 
 
 def gather_kernel(experts, returned, mix, got_outer, got_inner, outer, inner, stay):
@@ -116,7 +125,7 @@
         spread = jnp.zeros(lane.shape, jnp.float32)
         per_expert = chips * requests // experts
         for x in range(experts):
-            spread = jnp.where(lane // per_expert == x, home[:, x : x + 1], spread)
+            spread = jnp.where(lane // per_expert == experts - 1 - x, home[:, x : x + 1], spread)
         weights.append(jnp.where(lane % requests == j, spread, 0.0))
     weights = jnp.concatenate(weights, axis=0)
     flat = returned[...].reshape(chips * requests, width)
@@ -203,7 +212,7 @@
 
     cores = 2
     chips = devices // cores
-    alike = [[cores * i + j for i in range(chips)] for j in range(cores)]
+    alike = [[cores * i + j for i in reversed(range(chips))] for j in range(cores)]
     count = chips * requests
     outgoing = pl.pallas_call(
         spread_kernel,
@@ -225,9 +234,10 @@
         experts_kernel,
         out_shape=jax.ShapeDtypeStruct((chips, requests, width), jnp.bfloat16),
         in_specs=in_vmem(5) + [pl.BlockSpec(memory_space=pl.ANY) for _ in traded],
-        out_specs=in_vmem(1)[0],
+        out_specs=pl.BlockSpec(memory_space=pl.ANY),
         scratch_shapes=[pltpu.VMEM(weight.shape, weight.dtype) for weight in traded]
-        + [pltpu.SemaphoreType.DMA((len(traded),))],
+        + [pltpu.VMEM((PIECES, chips, requests, width // PIECES), jnp.bfloat16)]
+        + [pltpu.SemaphoreType.DMA((len(traded),)), pltpu.SemaphoreType.DMA((PIECES,))],
         compiler_params=LIMIT,
     )(received, norm_gain[None, :], *weights, *traded)
     returned = lax.all_to_all(

time: 77.2 us -> 72.7 us (0.942)
  the two profiles are of different devices: /device:TPU:8 before, /device:TPU:1 now
where the time goes in v8:
time: 72.7 us; the launch traced here: 72 us
  starting transfers between devices  47.2 us (65%)
  waiting for transfers between devices  13.3 us (18%)
  Pallas kernels  5.47 us (8%)
  local copies, waits for them, and re-layouts  3.72 us (5%)
  other arithmetic  1.45 us (2%)
  between operations  0.9 us (1%)
    all_to_all x1, starting transfers between devices, body(): lax.all_to_all(outgoing, 'ep', split_axis=0, concat_axis=0, axis_index_gr...  16.8 us
    ppermute x2, waiting for transfers between devices, exchanged(): lax.ppermute(outer, 'grp', outer_pairs)  13.2 us
    all_to_all x1, starting transfers between devices, body(): lax.all_to_all(pair, 'ep', split_axis=0, concat_axis=0, axis_index_groups...  11.7 us
    ppermute x3, starting transfers between devices, body(): traded = tuple((lax.ppermute(weight, 'ep', swap) for weight in weights))  7.48 us
    ppermute x2, starting transfers between devices, exchanged(): lax.ppermute(outer, 'grp', outer_pairs)  7.33 us
    ppermute x2, starting transfers between devices, exchanged(): lax.ppermute(inner, 'grp', inner_pairs)  3.84 us
    unnamed x32, local copies, waits for them, and re-layouts  3.71 us
    pallas_call x1, Pallas kernels, body(): pl.pallas_call(experts_kernel, out_shape=jax.ShapeDtypeStruct((chips, req...  2.81 us
  transfers between devices with their start and end apart: 9, of which 3 were waited for; matrix products, arithmetic and copies ran while one was open for 1% of the time, Pallas kernels for 2%

profile of v8, /device:TPU:1, one launch (start us, length us, event | category | flops | bytes accessed | tf_op | source)
XLA Modules:
  0.0 72.0 jit_solution(6536270232568170953)
XLA Ops:
  0.6 0.8 %copy-done.3 = bf16[1,1,2,3584]{3,2,1,0:T(2,128)(2,1)S(1)} copy-done((bf16[1,1,2,3584]{3,2,1,0:T(2,128)(2,1)S(1)}, bf16[1,1,2,3584]{3,2,1,0:T(2,128)(2,1)}, u32[]{:S(2)}) %copy-start.3) | copy-done | bytes 14360
  1.4 0.8 %shard_map.131 = bf16[32,2,3584]{2,1,0:T(2,128)(2,1)} custom-call(bf16[2,3584]{1,0:T(2,128)(2,1)S(1)} %bitcast.26), custom_call_target="tpu_custom_call" | custom-call | tf_op jit(solution)/shard_map/pallas_call | solution.py:217
  2.2 16.8 %all-to-all-start = ((bf16[32,2,3584]{2,1,0:T(2,128)(2,1)}), bf16[32,2,3584]{2,1,0:T(2,128)(2,1)S(1)}, u32[]{:S(2)}, u32[]{:S(2)}) async-start(bf16[32,2,3584]{2,1,0:T(2,128)(2,1)} %shard_map.131), calls=%async_computation | async-start | bytes 917504 | tf_op jit(solution)/shard_map/all_to_all | solution.py:224
  19.0 3.1 %collective-permute-start = (bf16[3584,128]{1,0:T(8,128)(2,1)S(1)}, bf16[3584,128]{1,0:T(8,128)(2,1)}, u32[]{:S(2)}, u32[]{:S(2)}) collective-permute-start(bf16[3584,128]{1,0:T(8,128)(2,1)S(1)} %bitcast.20), channel_id=1, source_target_pairs={{0,1},{1,0},{2,3},{3,2},{4,5},{5,4},{6,7},{7,6},{8,9},{9,8},{10,11... | collective-permute-start | bytes 2752520 | tf_op jit(solution)/shard_map/ppermute | solution.py:229
  22.2 1.9 %collective-permute-start.1 = (bf16[3584,128]{1,0:T(8,128)(2,1)}, bf16[3584,128]{1,0:T(8,128)(2,1)}, u32[]{:S(2)}, u32[]{:S(2)}) collective-permute-start(bf16[3584,128]{1,0:T(8,128)(2,1)} %bitcast.22), channel_id=1, source_target_pairs={{0,1},{1,0},{2,3},{3,2},{4,5},{5,4},{6,7},{7,6},{8,9},{9,8},{10,11... | collective-permute-start | bytes 2752520 | tf_op jit(solution)/shard_map/ppermute | solution.py:229
  24.1 2.4 %collective-permute-start.2 = (bf16[128,3584]{1,0:T(8,128)(2,1)}, bf16[128,3584]{1,0:T(8,128)(2,1)}, u32[]{:S(2)}, u32[]{:S(2)}) collective-permute-start(bf16[128,3584]{1,0:T(8,128)(2,1)} %bitcast.24), channel_id=1, source_target_pairs={{0,1},{1,0},{2,3},{3,2},{4,5},{5,4},{6,7},{7,6},{8,9},{9,8},{10,11... | collective-permute-start | bytes 2752520 | tf_op jit(solution)/shard_map/ppermute | solution.py:229
  26.5 0.0 copy-start.11
  26.6 0.0 copy-start.14
  26.6 0.0 copy-start.10
  26.6 0.0 copy-start.12
  26.6 0.0 copy-start.13
  26.6 0.6 copy-done.11
  27.2 0.0 copy-done.10
  27.3 0.0 copy-done.12
  27.3 1.0 %copy-done.4 = bf16[1,1,4,64,576]{4,3,2,1,0:T(8,128)(2,1)S(1)} copy-done((bf16[1,1,4,64,576]{4,3,2,1,0:T(8,128)(2,1)S(1)}, bf16[1,1,4,64,576]{4,3,2,1,0:T(8,128)(2,1)}, u32[]{:S(2)}) %copy-start.4) | copy-done | bytes 294936
  28.3 1.4 %shard_map.132 = (bf16[80,512]{1,0:T(8,128)(2,1)S(1)}, bf16[80,512]{1,0:T(8,128)(2,1)S(1)}, bf16[2,64,512]{2,1,0:T(8,128)(2,1)S(1)}, f32[8,128]{1,0:T(8,128)S(1)}) custom-call(s32[2,2]{1,0:T(2,128)S(1)} %bitcast.31, s32[2]{0:T(128)S(1)} %bitcast.32, s32[2]{0:T(128)S(1)} %bitcast.33, s32[1]{0:T(128)} %bitcast.4.odd, s32[4,6]{1,0:T(4,128)S(1)} %bitcast.29, ...), custom_call_target="tpu_custom_call" | custom-call | flops 40000000000 | bytes 400000000 | tf_op jit(solution)/shard_map/pallas_call | solution.py:197
  29.7 0.6 copy-done.6
  30.3 0.6 copy-done.8
  31.0 0.1 all-to-all-done.x
  31.0 0.0 collective-permute-done.1.up_there
  31.1 2.8 %shard_map.133 = bf16[32,2,3584]{2,1,0:T(2,128)(2,1)} custom-call(bf16[32,2,3584]{2,1,0:T(2,128)(2,1)S(1)} %all-to-all-done.x, f32[1,3584]{1,0:T(1,128)S(1)} %broadcast_in_dim.11.gain, bf16[3584,128]{1,0:T(8,128)(2,1)S(1)} %bitcast.21, bf16[3584,128]{1,0:T(8,128)(2,1)S(1)} %bitcast.23, bf16[128,3584]{1,0:T(8,128)(2,1)S(1)} %bitcast.25, ...), custom_call_target="tpu_custom_call" | custom-call | tf_op jit(solution)/shard_map/pallas_call | solution.py:233
  33.9 0.0 copy-start.9
  33.9 11.7 %all-to-all-start.1 = ((bf16[32,2,3584]{2,1,0:T(2,128)(2,1)}), bf16[32,2,3584]{2,1,0:T(2,128)(2,1)S(1)}, u32[]{:S(2)}, u32[]{:S(2)}) async-start(bf16[32,2,3584]{2,1,0:T(2,128)(2,1)} %shard_map.133), calls=%async_computation.1 | async-start | bytes 917504 | tf_op jit(solution)/shard_map/all_to_all | solution.py:243
  45.7 5.3 %collective-permute-start.3 = (bf16[80,512]{1,0:T(8,128)(2,1)S(1)}, bf16[80,512]{1,0:T(8,128)(2,1)S(1)}, u32[]{:S(2)}, u32[]{:S(2)}) collective-permute-start(bf16[80,512]{1,0:T(8,128)(2,1)S(1)} %copy-done.9), channel_id=1, source_target_pairs={{0,448},{64,128},{128,64},{192,256},{256,192},{320,384},{384,320},... | collective-permute-start | bytes 245768 | tf_op jit(solution)/shard_map/ppermute | solution.py:187
  51.0 1.9 %collective-permute-start.4 = (bf16[80,512]{1,0:T(8,128)(2,1)S(1)}, bf16[80,512]{1,0:T(8,128)(2,1)S(1)}, u32[]{:S(2)}, u32[]{:S(2)}) collective-permute-start(bf16[80,512]{1,0:T(8,128)(2,1)S(1)} %copy-done.7), channel_id=1, source_target_pairs={{0,64},{64,0},{128,192},{192,128},{256,320},{320,256},{384,448},{4... | collective-permute-start | bytes 245768 | tf_op jit(solution)/shard_map/ppermute | solution.py:187
  52.9 9.4 %collective-permute-done.3.got_outer = bf16[80,512]{1,0:T(8,128)(2,1)S(1)} collective-permute-done((bf16[80,512]{1,0:T(8,128)(2,1)S(1)}, bf16[80,512]{1,0:T(8,128)(2,1)S(1)}, u32[]{:S(2)}, u32[]{:S(2)}) %collective-permute-start.3) | collective-permute-done | bytes 81952 | tf_op jit(solution)/shard_map/ppermute | solution.py:187
  62.4 0.4 shard_map.134
  62.8 1.9 %collective-permute-start.5 = (bf16[1,3584]{1,0:T(2,128)(2,1)S(1)}, bf16[1,3584]{1,0:T(2,128)(2,1)S(1)}, u32[]{:S(2)}, u32[]{:S(2)}) collective-permute-start(bf16[1,3584]{1,0:T(2,128)(2,1)S(1)} %get-tuple-element.36), channel_id=1, source_target_pairs={{0,64},{64,0},{128,192},{192,128},{256,320},{320,256},{384,448},{4... | collective-permute-start | bytes 21512 | tf_op jit(solution)/shard_map/ppermute | solution.py:187
  64.7 2.0 %collective-permute-start.6 = (bf16[1,3584]{1,0:T(2,128)(2,1)S(1)}, bf16[1,3584]{1,0:T(2,128)(2,1)S(1)}, u32[]{:S(2)}, u32[]{:S(2)}) collective-permute-start(bf16[1,3584]{1,0:T(2,128)(2,1)S(1)} %get-tuple-element.37), channel_id=1, source_target_pairs={{0,448},{64,128},{128,64},{192,256},{256,192},{320,384},{384,320},... | collective-permute-start | bytes 21512 | tf_op jit(solution)/shard_map/ppermute | solution.py:187
  66.8 0.7 %maximum_bitcast_fusion = bf16[1,1,4,64,512]{4,3,2,1,0:T(8,128)(2,1)} fusion(bf16[1,64,512]{2,1,0:T(8,128)(2,1)S(1)} %get-tuple-element.39, bf16[1,64,512]{2,1,0:T(8,128)(2,1)S(1)} %get-tuple-element.38, bf16[2,64,512]{2,1,0:T(8,128)(2,1)S(1)} %get-tuple-element.28), kind=kLoop, calls=%fused_computation | loop fusion | flops 262144 | bytes 524288 | tf_op jit(solution)/shard_map/broadcast_in_dim | solution.py:193
  67.5 3.8 %collective-permute-done.6 = bf16[1,3584]{1,0:T(2,128)(2,1)S(1)} collective-permute-done((bf16[1,3584]{1,0:T(2,128)(2,1)S(1)}, bf16[1,3584]{1,0:T(2,128)(2,1)S(1)}, u32[]{:S(2)}, u32[]{:S(2)}) %collective-permute-start.6) | collective-permute-done | bytes 7200 | tf_op jit(solution)/shard_map/ppermute | solution.py:187
  71.3 0.7 maximum_bitcast_fusion.1
  (27 shorter events, 0.1 us)
Async XLA Ops:
  0.6 18.4 %copy-start = (bf16[1,3584,128]{2,1,0:T(8,128)(2,1)S(1)}, bf16[1,3584,128]{2,1,0:T(8,128)(2,1)}, u32[]{:S(2)}) copy-start(bf16[1,3584,128]{2,1,0:T(8,128)(2,1)} %param.21) | copy-start | bytes 2752516
  0.6 0.8 %copy-start.3 = (bf16[1,1,2,3584]{3,2,1,0:T(2,128)(2,1)S(1)}, bf16[1,1,2,3584]{3,2,1,0:T(2,128)(2,1)}, u32[]{:S(2)}) copy-start(bf16[1,1,2,3584]{3,2,1,0:T(2,128)(2,1)} %param.17) | copy-start | bytes 43012
  2.2 24.4 %copy-start.5 = (bf16[1,1,2,64,576]{4,3,2,1,0:T(8,128)(2,1)S(1)}, bf16[1,1,2,64,576]{4,3,2,1,0:T(8,128)(2,1)}, u32[]{:S(2)}) copy-start(bf16[1,1,2,64,576]{4,3,2,1,0:T(8,128)(2,1)} %param.16) | copy-start | bytes 442372
  2.2 28.8 %all-to-all-start = ((bf16[32,2,3584]{2,1,0:T(2,128)(2,1)}), bf16[32,2,3584]{2,1,0:T(2,128)(2,1)S(1)}, u32[]{:S(2)}, u32[]{:S(2)}) async-start(bf16[32,2,3584]{2,1,0:T(2,128)(2,1)} %shard_map.131), calls=%async_computation | async-start | bytes 917504 | tf_op jit(solution)/shard_map/all_to_all | solution.py:224
  19.0 12.0 %collective-permute-start = (bf16[3584,128]{1,0:T(8,128)(2,1)S(1)}, bf16[3584,128]{1,0:T(8,128)(2,1)}, u32[]{:S(2)}, u32[]{:S(2)}) collective-permute-start(bf16[3584,128]{1,0:T(8,128)(2,1)S(1)} %bitcast.20), channel_id=1, source_target_pairs={{0,1},{1,0},{2,3},{3,2},{4,5},{5,4},{6,7},{7,6},{8,9},{9,8},{10,11... | collective-permute-start | bytes 2752520 | tf_op jit(solution)/shard_map/ppermute | solution.py:229
  22.2 8.9 %collective-permute-start.1 = (bf16[3584,128]{1,0:T(8,128)(2,1)}, bf16[3584,128]{1,0:T(8,128)(2,1)}, u32[]{:S(2)}, u32[]{:S(2)}) collective-permute-start(bf16[3584,128]{1,0:T(8,128)(2,1)} %bitcast.22), channel_id=1, source_target_pairs={{0,1},{1,0},{2,3},{3,2},{4,5},{5,4},{6,7},{7,6},{8,9},{9,8},{10,11... | collective-permute-start | bytes 2752520 | tf_op jit(solution)/shard_map/ppermute | solution.py:229
  24.1 6.9 %collective-permute-start.2 = (bf16[128,3584]{1,0:T(8,128)(2,1)}, bf16[128,3584]{1,0:T(8,128)(2,1)}, u32[]{:S(2)}, u32[]{:S(2)}) collective-permute-start(bf16[128,3584]{1,0:T(8,128)(2,1)} %bitcast.24), channel_id=1, source_target_pairs={{0,1},{1,0},{2,3},{3,2},{4,5},{5,4},{6,7},{7,6},{8,9},{9,8},{10,11... | collective-permute-start | bytes 2752520 | tf_op jit(solution)/shard_map/ppermute | solution.py:229
  26.5 0.7 copy-start.11
  26.6 0.7 copy-start.14
  26.6 0.7 copy-start.10
  26.6 0.7 copy-start.12
  26.6 0.7 copy-start.13
  27.3 1.0 %copy-start.4 = (bf16[1,1,4,64,576]{4,3,2,1,0:T(8,128)(2,1)S(1)}, bf16[1,1,4,64,576]{4,3,2,1,0:T(8,128)(2,1)}, u32[]{:S(2)}) copy-start(bf16[1,1,4,64,576]{4,3,2,1,0:T(8,128)(2,1)} %param.12) | copy-start | bytes 884740
  28.3 2.7 %copy-start.15 = (f32[3584]{0:T(1024)S(1)}, f32[3584]{0:T(1024)}, u32[]{:S(2)}) copy-start(f32[3584]{0:T(1024)} %param.18) | copy-start | bytes 43012
  28.3 2.8 %copy-start.1 = (bf16[1,3584,128]{2,1,0:T(8,128)(2,1)S(1)}, bf16[1,3584,128]{2,1,0:T(8,128)(2,1)}, u32[]{:S(2)}) copy-start(bf16[1,3584,128]{2,1,0:T(8,128)(2,1)} %param.22) | copy-start | bytes 2752516
  28.3 2.8 %copy-start.2 = (bf16[1,128,3584]{2,1,0:T(8,128)(2,1)S(1)}, bf16[1,128,3584]{2,1,0:T(8,128)(2,1)}, u32[]{:S(2)}) copy-start(bf16[1,128,3584]{2,1,0:T(8,128)(2,1)} %param.23) | copy-start | bytes 2752516
  29.7 0.6 copy-start.6
  30.3 0.6 copy-start.8
  33.9 11.8 %copy-start.9 = (bf16[80,512]{1,0:T(8,128)(2,1)S(1)}, bf16[80,512]{1,0:T(8,128)(2,1)}, u32[]{:S(2)}) copy-start(bf16[80,512]{1,0:T(8,128)(2,1)} %copy-done.8) | copy-start | bytes 245764
  33.9 17.1 %copy-start.7 = (bf16[80,512]{1,0:T(8,128)(2,1)S(1)}, bf16[80,512]{1,0:T(8,128)(2,1)}, u32[]{:S(2)}) copy-start(bf16[80,512]{1,0:T(8,128)(2,1)} %copy-done.6) | copy-start | bytes 245764
  33.9 28.4 %all-to-all-start.1 = ((bf16[32,2,3584]{2,1,0:T(2,128)(2,1)}), bf16[32,2,3584]{2,1,0:T(2,128)(2,1)S(1)}, u32[]{:S(2)}, u32[]{:S(2)}) async-start(bf16[32,2,3584]{2,1,0:T(2,128)(2,1)} %shard_map.133), calls=%async_computation.1 | async-start | bytes 917504 | tf_op jit(solution)/shard_map/all_to_all | solution.py:243
  45.7 16.7 %collective-permute-start.3 = (bf16[80,512]{1,0:T(8,128)(2,1)S(1)}, bf16[80,512]{1,0:T(8,128)(2,1)S(1)}, u32[]{:S(2)}, u32[]{:S(2)}) collective-permute-start(bf16[80,512]{1,0:T(8,128)(2,1)S(1)} %copy-done.9), channel_id=1, source_target_pairs={{0,448},{64,128},{128,64},{192,256},{256,192},{320,384},{384,320},... | collective-permute-start | bytes 245768 | tf_op jit(solution)/shard_map/ppermute | solution.py:187
  51.0 11.4 %collective-permute-start.4 = (bf16[80,512]{1,0:T(8,128)(2,1)S(1)}, bf16[80,512]{1,0:T(8,128)(2,1)S(1)}, u32[]{:S(2)}, u32[]{:S(2)}) collective-permute-start(bf16[80,512]{1,0:T(8,128)(2,1)S(1)} %copy-done.7), channel_id=1, source_target_pairs={{0,64},{64,0},{128,192},{192,128},{256,320},{320,256},{384,448},{4... | collective-permute-start | bytes 245768 | tf_op jit(solution)/shard_map/ppermute | solution.py:187
  62.8 4.7 %collective-permute-start.5 = (bf16[1,3584]{1,0:T(2,128)(2,1)S(1)}, bf16[1,3584]{1,0:T(2,128)(2,1)S(1)}, u32[]{:S(2)}, u32[]{:S(2)}) collective-permute-start(bf16[1,3584]{1,0:T(2,128)(2,1)S(1)} %get-tuple-element.36), channel_id=1, source_target_pairs={{0,64},{64,0},{128,192},{192,128},{256,320},{320,256},{384,448},{4... | collective-permute-start | bytes 21512 | tf_op jit(solution)/shard_map/ppermute | solution.py:187
  64.7 6.6 %collective-permute-start.6 = (bf16[1,3584]{1,0:T(2,128)(2,1)S(1)}, bf16[1,3584]{1,0:T(2,128)(2,1)S(1)}, u32[]{:S(2)}, u32[]{:S(2)}) collective-permute-start(bf16[1,3584]{1,0:T(2,128)(2,1)S(1)} %get-tuple-element.37), channel_id=1, source_target_pairs={{0,448},{64,128},{128,64},{192,256},{256,192},{320,384},{384,320},... | collective-permute-start | bytes 21512 | tf_op jit(solution)/shard_map/ppermute | solution.py:187

commit v9 on v8

--- a/solution.py
+++ b/solution.py
@@ -30,8 +30,9 @@
 
 
 def attend_kernel(
-    table, lens, moves, odd, ids, gates, pool, query, outer, inner, stay, mix
+    table, lens, moves, ids, gates, pool, query, outer, inner, stay, mix
 ):
+    odd = lax.rem(lax.axis_index("grp"), 2)
     requests, heads = query.shape[0], query.shape[1]
     results = []
     for j in range(requests):
@@ -51,7 +52,7 @@
     for k in range(ids.shape[1]):
         total = total + jnp.where(ids[:, k : k + 1] == lane, gates[:, k : k + 1], 0.0)
     mix[:rows] = total
-    flags = [moves[j] for j in range(requests)] + [odd[0]]
+    flags = [moves[j] for j in range(requests)] + [odd]
     place = lax.broadcasted_iota(jnp.int32, (mix.shape[0] - rows, mix.shape[1]), 0)
     kept = jnp.zeros(place.shape, jnp.int32)
     for j, flag in enumerate(flags):
@@ -65,7 +66,7 @@
     behind = outer.shape[0] - heads
     row_forward = jnp.broadcast_to(pieces[requests + 1 : requests + 2], (behind, pieces.shape[1]))
     row_backward = jnp.broadcast_to(pieces[requests : requests + 1], (behind, pieces.shape[1]))
-    is_odd = odd[0] == 1
+    is_odd = odd == 1
     outer[:heads] = jnp.where(is_odd, forward, backward).astype(jnp.bfloat16)
     outer[heads:] = jnp.where(is_odd, row_forward, row_backward).astype(jnp.bfloat16)
     inner[:heads] = jnp.where(is_odd, backward, forward).astype(jnp.bfloat16)
@@ -179,7 +180,6 @@
     devices = lax.axis_size("ep")
 
     groups = lax.axis_size("grp")
-    group_odd = (lax.axis_index("grp") % 2).astype(jnp.int32).reshape(1)
     outer_pairs = [(i, (i + 1) % groups if i % 2 else (i - 1) % groups) for i in range(groups)]
     inner_pairs = [(i, i ^ 1) for i in range(groups)]
 
@@ -187,7 +187,7 @@
         return lax.ppermute(outer, "grp", outer_pairs), lax.ppermute(inner, "grp", inner_pairs)
 
     def served(stay, got_outer, got_inner):
-        odd = group_odd[0] == 1
+        odd = mix[-2, 0] == 1.0
         from_prev = jnp.where(odd, got_inner, got_outer)
         from_next = jnp.where(odd, got_outer, got_inner)
         return jnp.concatenate([stay, from_prev, from_next], axis=0)[None, None]
@@ -202,12 +202,12 @@
             jax.ShapeDtypeStruct((requests, heads, VDIM), jnp.bfloat16),
             jax.ShapeDtypeStruct((expert_ids.shape[2] + requests + 2, 128), jnp.float32),
         ),
-        in_specs=in_smem(4) + in_vmem(4),
+        in_specs=in_smem(3) + in_vmem(4),
         out_specs=tuple(in_vmem(4)),
         compiler_params=SMALL,
         cost_estimate=pl.CostEstimate(flops=40_000_000_000, bytes_accessed=400_000_000, transcendentals=100_000_000),
     )(
-        table, lengths[0, 0], moves, group_odd, expert_ids[0, 0], expert_gates[0, 0], pool, query[0, 0]
+        table, lengths[0, 0], moves, expert_ids[0, 0], expert_gates[0, 0], pool, query[0, 0]
     )
 
     cores = 2

time: 72.7 us -> 72.6 us (level)
  waiting for transfers between devices: 13.3 us -> 12.1 us
    ppermute x2, waiting for transfers between devices: 13.2 us -> 12 us  [exchanged(): lax.ppermute(outer, 'grp', outer_pairs)]
  transfers between devices with their start and end apart: 9 -> 9, of which waited for: 3 -> 3; matrix products, arithmetic and copies ran while one was open for 1% -> 2% of each run, Pallas kernels for 2% -> 2%
where the time goes in v9:
time: 72.6 us; the launch traced here: 72 us
  starting transfers between devices  47.2 us (65%)
  waiting for transfers between devices  12.1 us (17%)
  Pallas kernels  5.47 us (8%)
  local copies, waits for them, and re-layouts  4.22 us (6%)
  between operations  1.55 us (2%)
  other arithmetic  1.45 us (2%)
    all_to_all x1, starting transfers between devices, body(): lax.all_to_all(outgoing, 'ep', split_axis=0, concat_axis=0, axis_index_gr...  16.8 us
    ppermute x2, waiting for transfers between devices, exchanged(): lax.ppermute(outer, 'grp', outer_pairs)  12 us
    all_to_all x1, starting transfers between devices, body(): lax.all_to_all(pair, 'ep', split_axis=0, concat_axis=0, axis_index_groups...  11.7 us
    ppermute x3, starting transfers between devices, body(): traded = tuple((lax.ppermute(weight, 'ep', swap) for weight in weights))  7.48 us
    ppermute x2, starting transfers between devices, exchanged(): lax.ppermute(outer, 'grp', outer_pairs)  7.34 us
    ppermute x2, starting transfers between devices, exchanged(): lax.ppermute(inner, 'grp', inner_pairs)  3.84 us
    unnamed x32, local copies, waits for them, and re-layouts  3.69 us
    pallas_call x1, Pallas kernels, body(): pl.pallas_call(experts_kernel, out_shape=jax.ShapeDtypeStruct((chips, req...  2.81 us
  transfers between devices with their start and end apart: 9, of which 3 were waited for; matrix products, arithmetic and copies ran while one was open for 2% of the time, Pallas kernels for 2%

profile of v9, /device:TPU:1, one launch (start us, length us, event | category | flops | bytes accessed | tf_op | source)
XLA Modules:
  0.0 72.0 jit_solution(13667542058159154678)
XLA Ops:
  0.6 0.8 %copy-done.3 = bf16[1,1,2,3584]{3,2,1,0:T(2,128)(2,1)S(1)} copy-done((bf16[1,1,2,3584]{3,2,1,0:T(2,128)(2,1)S(1)}, bf16[1,1,2,3584]{3,2,1,0:T(2,128)(2,1)}, u32[]{:S(2)}) %copy-start.3) | copy-done | bytes 14360
  1.4 0.8 %shard_map.131 = bf16[32,2,3584]{2,1,0:T(2,128)(2,1)} custom-call(bf16[2,3584]{1,0:T(2,128)(2,1)S(1)} %bitcast.26), custom_call_target="tpu_custom_call" | custom-call | tf_op jit(solution)/shard_map/pallas_call | solution.py:217
  2.2 16.8 %all-to-all-start = ((bf16[32,2,3584]{2,1,0:T(2,128)(2,1)}), bf16[32,2,3584]{2,1,0:T(2,128)(2,1)S(1)}, u32[]{:S(2)}, u32[]{:S(2)}) async-start(bf16[32,2,3584]{2,1,0:T(2,128)(2,1)} %shard_map.131), calls=%async_computation | async-start | bytes 917504 | tf_op jit(solution)/shard_map/all_to_all | solution.py:224
  19.0 0.0 copy-start.11
  19.0 3.1 %collective-permute-start = (bf16[3584,128]{1,0:T(8,128)(2,1)S(1)}, bf16[3584,128]{1,0:T(8,128)(2,1)}, u32[]{:S(2)}, u32[]{:S(2)}) collective-permute-start(bf16[3584,128]{1,0:T(8,128)(2,1)S(1)} %bitcast.20), channel_id=1, source_target_pairs={{0,1},{1,0},{2,3},{3,2},{4,5},{5,4},{6,7},{7,6},{8,9},{9,8},{10,11... | collective-permute-start | bytes 2752520 | tf_op jit(solution)/shard_map/ppermute | solution.py:229
  22.2 0.0 copy-start.14
  22.2 1.9 %collective-permute-start.1 = (bf16[3584,128]{1,0:T(8,128)(2,1)}, bf16[3584,128]{1,0:T(8,128)(2,1)}, u32[]{:S(2)}, u32[]{:S(2)}) collective-permute-start(bf16[3584,128]{1,0:T(8,128)(2,1)} %bitcast.22), channel_id=1, source_target_pairs={{0,1},{1,0},{2,3},{3,2},{4,5},{5,4},{6,7},{7,6},{8,9},{9,8},{10,11... | collective-permute-start | bytes 2752520 | tf_op jit(solution)/shard_map/ppermute | solution.py:229
  24.1 2.4 %collective-permute-start.2 = (bf16[128,3584]{1,0:T(8,128)(2,1)}, bf16[128,3584]{1,0:T(8,128)(2,1)}, u32[]{:S(2)}, u32[]{:S(2)}) collective-permute-start(bf16[128,3584]{1,0:T(8,128)(2,1)} %bitcast.24), channel_id=1, source_target_pairs={{0,1},{1,0},{2,3},{3,2},{4,5},{5,4},{6,7},{7,6},{8,9},{9,8},{10,11... | collective-permute-start | bytes 2752520 | tf_op jit(solution)/shard_map/ppermute | solution.py:229
  26.6 0.0 copy-start.10
  26.6 0.0 copy-start.12
  26.6 0.0 copy-start.13
  26.6 0.6 copy-done.10
  27.2 0.0 copy-done.12
  27.3 1.0 %copy-done.4 = bf16[1,1,4,64,576]{4,3,2,1,0:T(8,128)(2,1)S(1)} copy-done((bf16[1,1,4,64,576]{4,3,2,1,0:T(8,128)(2,1)S(1)}, bf16[1,1,4,64,576]{4,3,2,1,0:T(8,128)(2,1)}, u32[]{:S(2)}) %copy-start.4) | copy-done | bytes 294936
  28.2 1.4 %shard_map.132 = (bf16[80,512]{1,0:T(8,128)(2,1)S(1)}, bf16[80,512]{1,0:T(8,128)(2,1)S(1)}, bf16[2,64,512]{2,1,0:T(8,128)(2,1)S(1)}, f32[8,128]{1,0:T(8,128)S(1)}) custom-call(s32[2,2]{1,0:T(2,128)S(1)} %bitcast.31, s32[2]{0:T(128)S(1)} %bitcast.32, s32[2]{0:T(128)S(1)} %bitcast.33, s32[4,6]{1,0:T(4,128)S(1)} %bitcast.29, f32[4,6]{1,0:T(4,128)S(1)} %bitcast.30, ...), custom_call_target="tpu_custom_call" | custom-call | flops 40000000000 | bytes 400000000 | tf_op jit(solution)/shard_map/pallas_call | solution.py:197
  29.7 0.6 copy-done.6
  30.3 0.6 copy-done.8
  31.0 0.1 all-to-all-done.x
  31.0 0.0 collective-permute-done.gate_there
  31.1 2.8 %shard_map.133 = bf16[32,2,3584]{2,1,0:T(2,128)(2,1)} custom-call(bf16[32,2,3584]{2,1,0:T(2,128)(2,1)S(1)} %all-to-all-done.x, f32[1,3584]{1,0:T(1,128)S(1)} %broadcast_in_dim.11.gain, bf16[3584,128]{1,0:T(8,128)(2,1)S(1)} %bitcast.21, bf16[3584,128]{1,0:T(8,128)(2,1)S(1)} %bitcast.23, bf16[128,3584]{1,0:T(8,128)(2,1)S(1)} %bitcast.25, ...), custom_call_target="tpu_custom_call" | custom-call | tf_op jit(solution)/shard_map/pallas_call | solution.py:233
  33.9 0.0 copy-start.9
  33.9 11.7 %all-to-all-start.1 = ((bf16[32,2,3584]{2,1,0:T(2,128)(2,1)}), bf16[32,2,3584]{2,1,0:T(2,128)(2,1)S(1)}, u32[]{:S(2)}, u32[]{:S(2)}) async-start(bf16[32,2,3584]{2,1,0:T(2,128)(2,1)} %shard_map.133), calls=%async_computation.1 | async-start | bytes 917504 | tf_op jit(solution)/shard_map/all_to_all | solution.py:243
  45.7 5.3 %collective-permute-start.3 = (bf16[80,512]{1,0:T(8,128)(2,1)S(1)}, bf16[80,512]{1,0:T(8,128)(2,1)S(1)}, u32[]{:S(2)}, u32[]{:S(2)}) collective-permute-start(bf16[80,512]{1,0:T(8,128)(2,1)S(1)} %copy-done.9), channel_id=1, source_target_pairs={{0,448},{64,128},{128,64},{192,256},{256,192},{320,384},{384,320},... | collective-permute-start | bytes 245768 | tf_op jit(solution)/shard_map/ppermute | solution.py:187
  51.0 1.9 %collective-permute-start.4 = (bf16[80,512]{1,0:T(8,128)(2,1)S(1)}, bf16[80,512]{1,0:T(8,128)(2,1)S(1)}, u32[]{:S(2)}, u32[]{:S(2)}) collective-permute-start(bf16[80,512]{1,0:T(8,128)(2,1)S(1)} %copy-done.7), channel_id=1, source_target_pairs={{0,64},{64,0},{128,192},{192,128},{256,320},{320,256},{384,448},{4... | collective-permute-start | bytes 245768 | tf_op jit(solution)/shard_map/ppermute | solution.py:187
  52.9 0.5 slice.10
  54.1 8.3 %collective-permute-done.3.got_outer = bf16[80,512]{1,0:T(8,128)(2,1)S(1)} collective-permute-done((bf16[80,512]{1,0:T(8,128)(2,1)S(1)}, bf16[80,512]{1,0:T(8,128)(2,1)S(1)}, u32[]{:S(2)}, u32[]{:S(2)}) %collective-permute-start.3) | collective-permute-done | bytes 81952 | tf_op jit(solution)/shard_map/ppermute | solution.py:187
  62.3 0.4 shard_map.134
  62.8 1.9 %collective-permute-start.5 = (bf16[1,3584]{1,0:T(2,128)(2,1)S(1)}, bf16[1,3584]{1,0:T(2,128)(2,1)S(1)}, u32[]{:S(2)}, u32[]{:S(2)}) collective-permute-start(bf16[1,3584]{1,0:T(2,128)(2,1)S(1)} %get-tuple-element.36), channel_id=1, source_target_pairs={{0,64},{64,0},{128,192},{192,128},{256,320},{320,256},{384,448},{4... | collective-permute-start | bytes 21512 | tf_op jit(solution)/shard_map/ppermute | solution.py:187
  64.7 2.0 %collective-permute-start.6 = (bf16[1,3584]{1,0:T(2,128)(2,1)S(1)}, bf16[1,3584]{1,0:T(2,128)(2,1)S(1)}, u32[]{:S(2)}, u32[]{:S(2)}) collective-permute-start(bf16[1,3584]{1,0:T(2,128)(2,1)S(1)} %get-tuple-element.37), channel_id=1, source_target_pairs={{0,448},{64,128},{128,64},{192,256},{256,192},{320,384},{384,320},... | collective-permute-start | bytes 21512 | tf_op jit(solution)/shard_map/ppermute | solution.py:187
  66.8 0.7 %maximum_bitcast_fusion = bf16[1,1,4,64,512]{4,3,2,1,0:T(8,128)(2,1)} fusion(bf16[1,64,512]{2,1,0:T(8,128)(2,1)S(1)} %get-tuple-element.39, bf16[1,64,512]{2,1,0:T(8,128)(2,1)S(1)} %get-tuple-element.38, bf16[2,64,512]{2,1,0:T(8,128)(2,1)S(1)} %get-tuple-element.28), kind=kLoop, calls=%fused_computation | loop fusion | flops 262144 | bytes 524288 | tf_op jit(solution)/shard_map/broadcast_in_dim | solution.py:193
  67.5 3.8 %collective-permute-done.6 = bf16[1,3584]{1,0:T(2,128)(2,1)S(1)} collective-permute-done((bf16[1,3584]{1,0:T(2,128)(2,1)S(1)}, bf16[1,3584]{1,0:T(2,128)(2,1)S(1)}, u32[]{:S(2)}, u32[]{:S(2)}) %collective-permute-start.6) | collective-permute-done | bytes 7200 | tf_op jit(solution)/shard_map/ppermute | solution.py:187
  71.3 0.7 maximum_bitcast_fusion.1
  (28 shorter events, 0.1 us)
Async XLA Ops:
  0.6 18.4 %copy-start = (bf16[1,3584,128]{2,1,0:T(8,128)(2,1)S(1)}, bf16[1,3584,128]{2,1,0:T(8,128)(2,1)}, u32[]{:S(2)}) copy-start(bf16[1,3584,128]{2,1,0:T(8,128)(2,1)} %param.21) | copy-start | bytes 2752516
  0.6 0.8 %copy-start.3 = (bf16[1,1,2,3584]{3,2,1,0:T(2,128)(2,1)S(1)}, bf16[1,1,2,3584]{3,2,1,0:T(2,128)(2,1)}, u32[]{:S(2)}) copy-start(bf16[1,1,2,3584]{3,2,1,0:T(2,128)(2,1)} %param.17) | copy-start | bytes 43012
  2.2 24.4 %copy-start.5 = (bf16[1,1,2,64,576]{4,3,2,1,0:T(8,128)(2,1)S(1)}, bf16[1,1,2,64,576]{4,3,2,1,0:T(8,128)(2,1)}, u32[]{:S(2)}) copy-start(bf16[1,1,2,64,576]{4,3,2,1,0:T(8,128)(2,1)} %param.16) | copy-start | bytes 442372
  2.2 28.8 %all-to-all-start = ((bf16[32,2,3584]{2,1,0:T(2,128)(2,1)}), bf16[32,2,3584]{2,1,0:T(2,128)(2,1)S(1)}, u32[]{:S(2)}, u32[]{:S(2)}) async-start(bf16[32,2,3584]{2,1,0:T(2,128)(2,1)} %shard_map.131), calls=%async_computation | async-start | bytes 917504 | tf_op jit(solution)/shard_map/all_to_all | solution.py:224
  19.0 7.6 %copy-start.11 = (f32[1,1,4,6]{3,2,1,0:T(4,128)S(1)}, f32[1,1,4,6]{3,2,1,0:T(4,128)}, u32[]{:S(2)}) copy-start(f32[1,1,4,6]{3,2,1,0:T(4,128)} %param.20) | copy-start | bytes 292
  19.0 12.0 %collective-permute-start = (bf16[3584,128]{1,0:T(8,128)(2,1)S(1)}, bf16[3584,128]{1,0:T(8,128)(2,1)}, u32[]{:S(2)}, u32[]{:S(2)}) collective-permute-start(bf16[3584,128]{1,0:T(8,128)(2,1)S(1)} %bitcast.20), channel_id=1, source_target_pairs={{0,1},{1,0},{2,3},{3,2},{4,5},{5,4},{6,7},{7,6},{8,9},{9,8},{10,11... | collective-permute-start | bytes 2752520 | tf_op jit(solution)/shard_map/ppermute | solution.py:229
  22.2 4.4 %copy-start.14 = (s32[1,1,2]{2,1,0:T(1,128)S(1)}, s32[1,1,2]{2,1,0:T(1,128)}, u32[]{:S(2)}) copy-start(s32[1,1,2]{2,1,0:T(1,128)} %param.15) | copy-start | bytes 28
  22.2 8.8 %collective-permute-start.1 = (bf16[3584,128]{1,0:T(8,128)(2,1)}, bf16[3584,128]{1,0:T(8,128)(2,1)}, u32[]{:S(2)}, u32[]{:S(2)}) collective-permute-start(bf16[3584,128]{1,0:T(8,128)(2,1)} %bitcast.22), channel_id=1, source_target_pairs={{0,1},{1,0},{2,3},{3,2},{4,5},{5,4},{6,7},{7,6},{8,9},{9,8},{10,11... | collective-permute-start | bytes 2752520 | tf_op jit(solution)/shard_map/ppermute | solution.py:229
  24.1 6.9 %collective-permute-start.2 = (bf16[128,3584]{1,0:T(8,128)(2,1)}, bf16[128,3584]{1,0:T(8,128)(2,1)}, u32[]{:S(2)}, u32[]{:S(2)}) collective-permute-start(bf16[128,3584]{1,0:T(8,128)(2,1)} %bitcast.24), channel_id=1, source_target_pairs={{0,1},{1,0},{2,3},{3,2},{4,5},{5,4},{6,7},{7,6},{8,9},{9,8},{10,11... | collective-permute-start | bytes 2752520 | tf_op jit(solution)/shard_map/ppermute | solution.py:229
  26.6 0.7 copy-start.10
  26.6 0.7 copy-start.12
  26.6 0.7 copy-start.13
  27.3 1.0 %copy-start.4 = (bf16[1,1,4,64,576]{4,3,2,1,0:T(8,128)(2,1)S(1)}, bf16[1,1,4,64,576]{4,3,2,1,0:T(8,128)(2,1)}, u32[]{:S(2)}) copy-start(bf16[1,1,4,64,576]{4,3,2,1,0:T(8,128)(2,1)} %param.12) | copy-start | bytes 884740
  28.2 2.7 %copy-start.15 = (f32[3584]{0:T(1024)S(1)}, f32[3584]{0:T(1024)}, u32[]{:S(2)}) copy-start(f32[3584]{0:T(1024)} %param.18) | copy-start | bytes 43012
  28.2 2.8 %copy-start.1 = (bf16[1,3584,128]{2,1,0:T(8,128)(2,1)S(1)}, bf16[1,3584,128]{2,1,0:T(8,128)(2,1)}, u32[]{:S(2)}) copy-start(bf16[1,3584,128]{2,1,0:T(8,128)(2,1)} %param.22) | copy-start | bytes 2752516
  28.2 2.8 %copy-start.2 = (bf16[1,128,3584]{2,1,0:T(8,128)(2,1)S(1)}, bf16[1,128,3584]{2,1,0:T(8,128)(2,1)}, u32[]{:S(2)}) copy-start(bf16[1,128,3584]{2,1,0:T(8,128)(2,1)} %param.23) | copy-start | bytes 2752516
  29.7 0.6 copy-start.6
  30.3 0.6 copy-start.8
  33.9 11.8 %copy-start.9 = (bf16[80,512]{1,0:T(8,128)(2,1)S(1)}, bf16[80,512]{1,0:T(8,128)(2,1)}, u32[]{:S(2)}) copy-start(bf16[80,512]{1,0:T(8,128)(2,1)} %copy-done.8) | copy-start | bytes 245764
  33.9 17.1 %copy-start.7 = (bf16[80,512]{1,0:T(8,128)(2,1)S(1)}, bf16[80,512]{1,0:T(8,128)(2,1)}, u32[]{:S(2)}) copy-start(bf16[80,512]{1,0:T(8,128)(2,1)} %copy-done.6) | copy-start | bytes 245764
  33.9 28.4 %all-to-all-start.1 = ((bf16[32,2,3584]{2,1,0:T(2,128)(2,1)}), bf16[32,2,3584]{2,1,0:T(2,128)(2,1)S(1)}, u32[]{:S(2)}, u32[]{:S(2)}) async-start(bf16[32,2,3584]{2,1,0:T(2,128)(2,1)} %shard_map.133), calls=%async_computation.1 | async-start | bytes 917504 | tf_op jit(solution)/shard_map/all_to_all | solution.py:243
  45.7 16.7 %collective-permute-start.3 = (bf16[80,512]{1,0:T(8,128)(2,1)S(1)}, bf16[80,512]{1,0:T(8,128)(2,1)S(1)}, u32[]{:S(2)}, u32[]{:S(2)}) collective-permute-start(bf16[80,512]{1,0:T(8,128)(2,1)S(1)} %copy-done.9), channel_id=1, source_target_pairs={{0,448},{64,128},{128,64},{192,256},{256,192},{320,384},{384,320},... | collective-permute-start | bytes 245768 | tf_op jit(solution)/shard_map/ppermute | solution.py:187
  51.0 11.4 %collective-permute-start.4 = (bf16[80,512]{1,0:T(8,128)(2,1)S(1)}, bf16[80,512]{1,0:T(8,128)(2,1)S(1)}, u32[]{:S(2)}, u32[]{:S(2)}) collective-permute-start(bf16[80,512]{1,0:T(8,128)(2,1)S(1)} %copy-done.7), channel_id=1, source_target_pairs={{0,64},{64,0},{128,192},{192,128},{256,320},{320,256},{384,448},{4... | collective-permute-start | bytes 245768 | tf_op jit(solution)/shard_map/ppermute | solution.py:187
  62.8 4.7 %collective-permute-start.5 = (bf16[1,3584]{1,0:T(2,128)(2,1)S(1)}, bf16[1,3584]{1,0:T(2,128)(2,1)S(1)}, u32[]{:S(2)}, u32[]{:S(2)}) collective-permute-start(bf16[1,3584]{1,0:T(2,128)(2,1)S(1)} %get-tuple-element.36), channel_id=1, source_target_pairs={{0,64},{64,0},{128,192},{192,128},{256,320},{320,256},{384,448},{4... | collective-permute-start | bytes 21512 | tf_op jit(solution)/shard_map/ppermute | solution.py:187
  64.7 6.6 %collective-permute-start.6 = (bf16[1,3584]{1,0:T(2,128)(2,1)S(1)}, bf16[1,3584]{1,0:T(2,128)(2,1)S(1)}, u32[]{:S(2)}, u32[]{:S(2)}) collective-permute-start(bf16[1,3584]{1,0:T(2,128)(2,1)S(1)} %get-tuple-element.37), channel_id=1, source_target_pairs={{0,448},{64,128},{128,64},{192,256},{256,192},{320,384},{384,320},... | collective-permute-start | bytes 21512 | tf_op jit(solution)/shard_map/ppermute | solution.py:187

commit v10 on v9

--- a/solution.py
+++ b/solution.py
@@ -11,7 +11,7 @@
 QK_DIM = 192
 SLICES = 8
 BEHIND = 16
-PIECES = 2
+LAST = 1024
 
 
 def dot(left, right):
@@ -74,7 +74,7 @@
 
 
 def experts_kernel(
-    x, gain, gate_a, up_a, down_a, gate_there, up_there, down_there, out, gate_b, up_b, down_b, pieces, sems, out_sems
+    x, gain, gate_a, up_a, down_a, gate_there, up_there, down_there, out, gate_b, up_b, down_b, large, small, sems, out_sems
 ):
     pairs = ((gate_there, gate_b), (up_there, up_b), (down_there, down_b))
     copies = [pltpu.make_async_copy(*pair, sems.at[i]) for i, pair in enumerate(pairs)]
@@ -91,12 +91,11 @@
     act = (jax.nn.silu(gate) * dot(normed, up_b[...])).astype(jnp.bfloat16)
     copies[2].wait()
     leaving = []
-    for i in range(PIECES):
-        size = out.shape[2] // PIECES
-        columns = slice(i * size, (i + 1) * size)
-        piece = total[:, columns] + dot(act, down_b[:, columns])
-        pieces[i] = piece.astype(jnp.bfloat16).reshape(pieces.shape[1:])
-        leaving.append(pltpu.make_async_copy(pieces.at[i], out.at[:, :, columns], out_sems.at[i]))
+    for i, (first, piece) in enumerate(((0, large), (large.shape[2], small))):
+        columns = slice(first, first + piece.shape[2])
+        values = total[:, columns] + dot(act, down_b[:, columns])
+        piece[...] = values.astype(jnp.bfloat16).reshape(piece.shape)
+        leaving.append(pltpu.make_async_copy(piece, out.at[:, :, columns], out_sems.at[i]))
         leaving[i].start()
     for copy in leaving:
         copy.wait()
@@ -236,8 +235,8 @@
         in_specs=in_vmem(5) + [pl.BlockSpec(memory_space=pl.ANY) for _ in traded],
         out_specs=pl.BlockSpec(memory_space=pl.ANY),
         scratch_shapes=[pltpu.VMEM(weight.shape, weight.dtype) for weight in traded]
-        + [pltpu.VMEM((PIECES, chips, requests, width // PIECES), jnp.bfloat16)]
-        + [pltpu.SemaphoreType.DMA((len(traded),)), pltpu.SemaphoreType.DMA((PIECES,))],
+        + [pltpu.VMEM((chips, requests, part), jnp.bfloat16) for part in (width - LAST, LAST)]
+        + [pltpu.SemaphoreType.DMA((len(traded),)), pltpu.SemaphoreType.DMA((2,))],
         compiler_params=LIMIT,
     )(received, norm_gain[None, :], *weights, *traded)
     returned = lax.all_to_all(

time: 72.6 us -> 72.6 us (level)
  no operation moved by 1% of the time
where the time goes in v10:
time: 72.6 us; the launch traced here: 72 us
  starting transfers between devices  47.2 us (65%)
  waiting for transfers between devices  12.1 us (17%)
  Pallas kernels  5.47 us (8%)
  local copies, waits for them, and re-layouts  4.22 us (6%)
  between operations  1.55 us (2%)
  other arithmetic  1.45 us (2%)
    all_to_all x1, starting transfers between devices, body(): lax.all_to_all(outgoing, 'ep', split_axis=0, concat_axis=0, axis_index_gr...  16.8 us
    ppermute x2, waiting for transfers between devices, exchanged(): lax.ppermute(outer, 'grp', outer_pairs)  12 us
    all_to_all x1, starting transfers between devices, body(): lax.all_to_all(pair, 'ep', split_axis=0, concat_axis=0, axis_index_groups...  11.7 us
    ppermute x3, starting transfers between devices, body(): traded = tuple((lax.ppermute(weight, 'ep', swap) for weight in weights))  7.48 us
    ppermute x2, starting transfers between devices, exchanged(): lax.ppermute(outer, 'grp', outer_pairs)  7.34 us
    ppermute x2, starting transfers between devices, exchanged(): lax.ppermute(inner, 'grp', inner_pairs)  3.84 us
    unnamed x32, local copies, waits for them, and re-layouts  3.69 us
    pallas_call x1, Pallas kernels, body(): pl.pallas_call(experts_kernel, out_shape=jax.ShapeDtypeStruct((chips, req...  2.82 us
  transfers between devices with their start and end apart: 9, of which 3 were waited for; matrix products, arithmetic and copies ran while one was open for 2% of the time, Pallas kernels for 2%

profile of v10, /device:TPU:1, one launch (start us, length us, event | category | flops | bytes accessed | tf_op | source)
XLA Modules:
  0.0 72.0 jit_solution(5195542942437943554)
XLA Ops:
  0.6 0.8 %copy-done.3 = bf16[1,1,2,3584]{3,2,1,0:T(2,128)(2,1)S(1)} copy-done((bf16[1,1,2,3584]{3,2,1,0:T(2,128)(2,1)S(1)}, bf16[1,1,2,3584]{3,2,1,0:T(2,128)(2,1)}, u32[]{:S(2)}) %copy-start.3) | copy-done | bytes 14360
  1.4 0.8 %shard_map.131 = bf16[32,2,3584]{2,1,0:T(2,128)(2,1)} custom-call(bf16[2,3584]{1,0:T(2,128)(2,1)S(1)} %bitcast.26), custom_call_target="tpu_custom_call" | custom-call | tf_op jit(solution)/shard_map/pallas_call | solution.py:216
  2.2 16.8 %all-to-all-start = ((bf16[32,2,3584]{2,1,0:T(2,128)(2,1)}), bf16[32,2,3584]{2,1,0:T(2,128)(2,1)S(1)}, u32[]{:S(2)}, u32[]{:S(2)}) async-start(bf16[32,2,3584]{2,1,0:T(2,128)(2,1)} %shard_map.131), calls=%async_computation | async-start | bytes 917504 | tf_op jit(solution)/shard_map/all_to_all | solution.py:223
  19.0 0.0 copy-start.11
  19.0 3.1 %collective-permute-start = (bf16[3584,128]{1,0:T(8,128)(2,1)S(1)}, bf16[3584,128]{1,0:T(8,128)(2,1)}, u32[]{:S(2)}, u32[]{:S(2)}) collective-permute-start(bf16[3584,128]{1,0:T(8,128)(2,1)S(1)} %bitcast.20), channel_id=1, source_target_pairs={{0,1},{1,0},{2,3},{3,2},{4,5},{5,4},{6,7},{7,6},{8,9},{9,8},{10,11... | collective-permute-start | bytes 2752520 | tf_op jit(solution)/shard_map/ppermute | solution.py:228
  22.2 0.0 copy-start.14
  22.2 1.9 %collective-permute-start.1 = (bf16[3584,128]{1,0:T(8,128)(2,1)}, bf16[3584,128]{1,0:T(8,128)(2,1)}, u32[]{:S(2)}, u32[]{:S(2)}) collective-permute-start(bf16[3584,128]{1,0:T(8,128)(2,1)} %bitcast.22), channel_id=1, source_target_pairs={{0,1},{1,0},{2,3},{3,2},{4,5},{5,4},{6,7},{7,6},{8,9},{9,8},{10,11... | collective-permute-start | bytes 2752520 | tf_op jit(solution)/shard_map/ppermute | solution.py:228
  24.1 2.4 %collective-permute-start.2 = (bf16[128,3584]{1,0:T(8,128)(2,1)}, bf16[128,3584]{1,0:T(8,128)(2,1)}, u32[]{:S(2)}, u32[]{:S(2)}) collective-permute-start(bf16[128,3584]{1,0:T(8,128)(2,1)} %bitcast.24), channel_id=1, source_target_pairs={{0,1},{1,0},{2,3},{3,2},{4,5},{5,4},{6,7},{7,6},{8,9},{9,8},{10,11... | collective-permute-start | bytes 2752520 | tf_op jit(solution)/shard_map/ppermute | solution.py:228
  26.6 0.0 copy-start.10
  26.6 0.0 copy-start.12
  26.6 0.0 copy-start.13
  26.6 0.6 copy-done.10
  27.2 0.0 copy-done.12
  27.3 1.0 %copy-done.4 = bf16[1,1,4,64,576]{4,3,2,1,0:T(8,128)(2,1)S(1)} copy-done((bf16[1,1,4,64,576]{4,3,2,1,0:T(8,128)(2,1)S(1)}, bf16[1,1,4,64,576]{4,3,2,1,0:T(8,128)(2,1)}, u32[]{:S(2)}) %copy-start.4) | copy-done | bytes 294936
  28.2 1.4 %shard_map.132 = (bf16[80,512]{1,0:T(8,128)(2,1)S(1)}, bf16[80,512]{1,0:T(8,128)(2,1)S(1)}, bf16[2,64,512]{2,1,0:T(8,128)(2,1)S(1)}, f32[8,128]{1,0:T(8,128)S(1)}) custom-call(s32[2,2]{1,0:T(2,128)S(1)} %bitcast.31, s32[2]{0:T(128)S(1)} %bitcast.32, s32[2]{0:T(128)S(1)} %bitcast.33, s32[4,6]{1,0:T(4,128)S(1)} %bitcast.29, f32[4,6]{1,0:T(4,128)S(1)} %bitcast.30, ...), custom_call_target="tpu_custom_call" | custom-call | flops 40000000000 | bytes 400000000 | tf_op jit(solution)/shard_map/pallas_call | solution.py:196
  29.7 0.6 copy-done.6
  30.3 0.6 copy-done.8
  31.0 0.1 all-to-all-done.x
  31.0 0.0 collective-permute-done.gate_there
  31.1 2.8 %shard_map.133 = bf16[32,2,3584]{2,1,0:T(2,128)(2,1)} custom-call(bf16[32,2,3584]{2,1,0:T(2,128)(2,1)S(1)} %all-to-all-done.x, f32[1,3584]{1,0:T(1,128)S(1)} %broadcast_in_dim.11.gain, bf16[3584,128]{1,0:T(8,128)(2,1)S(1)} %bitcast.21, bf16[3584,128]{1,0:T(8,128)(2,1)S(1)} %bitcast.23, bf16[128,3584]{1,0:T(8,128)(2,1)S(1)} %bitcast.25, ...), custom_call_target="tpu_custom_call" | custom-call | tf_op jit(solution)/shard_map/pallas_call | solution.py:232
  33.9 0.0 copy-start.9
  33.9 11.7 %all-to-all-start.1 = ((bf16[32,2,3584]{2,1,0:T(2,128)(2,1)}), bf16[32,2,3584]{2,1,0:T(2,128)(2,1)S(1)}, u32[]{:S(2)}, u32[]{:S(2)}) async-start(bf16[32,2,3584]{2,1,0:T(2,128)(2,1)} %shard_map.133), calls=%async_computation.1 | async-start | bytes 917504 | tf_op jit(solution)/shard_map/all_to_all | solution.py:242
  45.7 5.3 %collective-permute-start.3 = (bf16[80,512]{1,0:T(8,128)(2,1)S(1)}, bf16[80,512]{1,0:T(8,128)(2,1)S(1)}, u32[]{:S(2)}, u32[]{:S(2)}) collective-permute-start(bf16[80,512]{1,0:T(8,128)(2,1)S(1)} %copy-done.9), channel_id=1, source_target_pairs={{0,448},{64,128},{128,64},{192,256},{256,192},{320,384},{384,320},... | collective-permute-start | bytes 245768 | tf_op jit(solution)/shard_map/ppermute | solution.py:186
  51.0 1.9 %collective-permute-start.4 = (bf16[80,512]{1,0:T(8,128)(2,1)S(1)}, bf16[80,512]{1,0:T(8,128)(2,1)S(1)}, u32[]{:S(2)}, u32[]{:S(2)}) collective-permute-start(bf16[80,512]{1,0:T(8,128)(2,1)S(1)} %copy-done.7), channel_id=1, source_target_pairs={{0,64},{64,0},{128,192},{192,128},{256,320},{320,256},{384,448},{4... | collective-permute-start | bytes 245768 | tf_op jit(solution)/shard_map/ppermute | solution.py:186
  52.9 0.5 slice.10
  54.1 8.3 %collective-permute-done.3.got_outer = bf16[80,512]{1,0:T(8,128)(2,1)S(1)} collective-permute-done((bf16[80,512]{1,0:T(8,128)(2,1)S(1)}, bf16[80,512]{1,0:T(8,128)(2,1)S(1)}, u32[]{:S(2)}, u32[]{:S(2)}) %collective-permute-start.3) | collective-permute-done | bytes 81952 | tf_op jit(solution)/shard_map/ppermute | solution.py:186
  62.4 0.4 shard_map.134
  62.8 1.9 %collective-permute-start.5 = (bf16[1,3584]{1,0:T(2,128)(2,1)S(1)}, bf16[1,3584]{1,0:T(2,128)(2,1)S(1)}, u32[]{:S(2)}, u32[]{:S(2)}) collective-permute-start(bf16[1,3584]{1,0:T(2,128)(2,1)S(1)} %get-tuple-element.36), channel_id=1, source_target_pairs={{0,64},{64,0},{128,192},{192,128},{256,320},{320,256},{384,448},{4... | collective-permute-start | bytes 21512 | tf_op jit(solution)/shard_map/ppermute | solution.py:186
  64.7 2.0 %collective-permute-start.6 = (bf16[1,3584]{1,0:T(2,128)(2,1)S(1)}, bf16[1,3584]{1,0:T(2,128)(2,1)S(1)}, u32[]{:S(2)}, u32[]{:S(2)}) collective-permute-start(bf16[1,3584]{1,0:T(2,128)(2,1)S(1)} %get-tuple-element.37), channel_id=1, source_target_pairs={{0,448},{64,128},{128,64},{192,256},{256,192},{320,384},{384,320},... | collective-permute-start | bytes 21512 | tf_op jit(solution)/shard_map/ppermute | solution.py:186
  66.8 0.7 %maximum_bitcast_fusion = bf16[1,1,4,64,512]{4,3,2,1,0:T(8,128)(2,1)} fusion(bf16[1,64,512]{2,1,0:T(8,128)(2,1)S(1)} %get-tuple-element.39, bf16[1,64,512]{2,1,0:T(8,128)(2,1)S(1)} %get-tuple-element.38, bf16[2,64,512]{2,1,0:T(8,128)(2,1)S(1)} %get-tuple-element.28), kind=kLoop, calls=%fused_computation | loop fusion | flops 262144 | bytes 524288 | tf_op jit(solution)/shard_map/broadcast_in_dim | solution.py:192
  67.5 3.8 %collective-permute-done.6 = bf16[1,3584]{1,0:T(2,128)(2,1)S(1)} collective-permute-done((bf16[1,3584]{1,0:T(2,128)(2,1)S(1)}, bf16[1,3584]{1,0:T(2,128)(2,1)S(1)}, u32[]{:S(2)}, u32[]{:S(2)}) %collective-permute-start.6) | collective-permute-done | bytes 7200 | tf_op jit(solution)/shard_map/ppermute | solution.py:186
  71.3 0.7 maximum_bitcast_fusion.1
  (28 shorter events, 0.1 us)
Async XLA Ops:
  0.6 18.4 %copy-start = (bf16[1,3584,128]{2,1,0:T(8,128)(2,1)S(1)}, bf16[1,3584,128]{2,1,0:T(8,128)(2,1)}, u32[]{:S(2)}) copy-start(bf16[1,3584,128]{2,1,0:T(8,128)(2,1)} %param.21) | copy-start | bytes 2752516
  0.6 0.8 %copy-start.3 = (bf16[1,1,2,3584]{3,2,1,0:T(2,128)(2,1)S(1)}, bf16[1,1,2,3584]{3,2,1,0:T(2,128)(2,1)}, u32[]{:S(2)}) copy-start(bf16[1,1,2,3584]{3,2,1,0:T(2,128)(2,1)} %param.17) | copy-start | bytes 43012
  2.2 24.4 %copy-start.5 = (bf16[1,1,2,64,576]{4,3,2,1,0:T(8,128)(2,1)S(1)}, bf16[1,1,2,64,576]{4,3,2,1,0:T(8,128)(2,1)}, u32[]{:S(2)}) copy-start(bf16[1,1,2,64,576]{4,3,2,1,0:T(8,128)(2,1)} %param.16) | copy-start | bytes 442372
  2.2 28.8 %all-to-all-start = ((bf16[32,2,3584]{2,1,0:T(2,128)(2,1)}), bf16[32,2,3584]{2,1,0:T(2,128)(2,1)S(1)}, u32[]{:S(2)}, u32[]{:S(2)}) async-start(bf16[32,2,3584]{2,1,0:T(2,128)(2,1)} %shard_map.131), calls=%async_computation | async-start | bytes 917504 | tf_op jit(solution)/shard_map/all_to_all | solution.py:223
  19.0 7.6 %copy-start.11 = (f32[1,1,4,6]{3,2,1,0:T(4,128)S(1)}, f32[1,1,4,6]{3,2,1,0:T(4,128)}, u32[]{:S(2)}) copy-start(f32[1,1,4,6]{3,2,1,0:T(4,128)} %param.20) | copy-start | bytes 292
  19.0 12.0 %collective-permute-start = (bf16[3584,128]{1,0:T(8,128)(2,1)S(1)}, bf16[3584,128]{1,0:T(8,128)(2,1)}, u32[]{:S(2)}, u32[]{:S(2)}) collective-permute-start(bf16[3584,128]{1,0:T(8,128)(2,1)S(1)} %bitcast.20), channel_id=1, source_target_pairs={{0,1},{1,0},{2,3},{3,2},{4,5},{5,4},{6,7},{7,6},{8,9},{9,8},{10,11... | collective-permute-start | bytes 2752520 | tf_op jit(solution)/shard_map/ppermute | solution.py:228
  22.2 4.4 %copy-start.14 = (s32[1,1,2]{2,1,0:T(1,128)S(1)}, s32[1,1,2]{2,1,0:T(1,128)}, u32[]{:S(2)}) copy-start(s32[1,1,2]{2,1,0:T(1,128)} %param.15) | copy-start | bytes 28
  22.2 8.8 %collective-permute-start.1 = (bf16[3584,128]{1,0:T(8,128)(2,1)}, bf16[3584,128]{1,0:T(8,128)(2,1)}, u32[]{:S(2)}, u32[]{:S(2)}) collective-permute-start(bf16[3584,128]{1,0:T(8,128)(2,1)} %bitcast.22), channel_id=1, source_target_pairs={{0,1},{1,0},{2,3},{3,2},{4,5},{5,4},{6,7},{7,6},{8,9},{9,8},{10,11... | collective-permute-start | bytes 2752520 | tf_op jit(solution)/shard_map/ppermute | solution.py:228
  24.1 6.9 %collective-permute-start.2 = (bf16[128,3584]{1,0:T(8,128)(2,1)}, bf16[128,3584]{1,0:T(8,128)(2,1)}, u32[]{:S(2)}, u32[]{:S(2)}) collective-permute-start(bf16[128,3584]{1,0:T(8,128)(2,1)} %bitcast.24), channel_id=1, source_target_pairs={{0,1},{1,0},{2,3},{3,2},{4,5},{5,4},{6,7},{7,6},{8,9},{9,8},{10,11... | collective-permute-start | bytes 2752520 | tf_op jit(solution)/shard_map/ppermute | solution.py:228
  26.6 0.7 copy-start.10
  26.6 0.7 copy-start.12
  26.6 0.7 copy-start.13
  27.3 1.0 %copy-start.4 = (bf16[1,1,4,64,576]{4,3,2,1,0:T(8,128)(2,1)S(1)}, bf16[1,1,4,64,576]{4,3,2,1,0:T(8,128)(2,1)}, u32[]{:S(2)}) copy-start(bf16[1,1,4,64,576]{4,3,2,1,0:T(8,128)(2,1)} %param.12) | copy-start | bytes 884740
  28.2 2.7 %copy-start.15 = (f32[3584]{0:T(1024)S(1)}, f32[3584]{0:T(1024)}, u32[]{:S(2)}) copy-start(f32[3584]{0:T(1024)} %param.18) | copy-start | bytes 43012
  28.2 2.8 %copy-start.1 = (bf16[1,3584,128]{2,1,0:T(8,128)(2,1)S(1)}, bf16[1,3584,128]{2,1,0:T(8,128)(2,1)}, u32[]{:S(2)}) copy-start(bf16[1,3584,128]{2,1,0:T(8,128)(2,1)} %param.22) | copy-start | bytes 2752516
  28.2 2.8 %copy-start.2 = (bf16[1,128,3584]{2,1,0:T(8,128)(2,1)S(1)}, bf16[1,128,3584]{2,1,0:T(8,128)(2,1)}, u32[]{:S(2)}) copy-start(bf16[1,128,3584]{2,1,0:T(8,128)(2,1)} %param.23) | copy-start | bytes 2752516
  29.7 0.6 copy-start.6
  30.3 0.6 copy-start.8
  33.9 11.8 %copy-start.9 = (bf16[80,512]{1,0:T(8,128)(2,1)S(1)}, bf16[80,512]{1,0:T(8,128)(2,1)}, u32[]{:S(2)}) copy-start(bf16[80,512]{1,0:T(8,128)(2,1)} %copy-done.8) | copy-start | bytes 245764
  33.9 17.1 %copy-start.7 = (bf16[80,512]{1,0:T(8,128)(2,1)S(1)}, bf16[80,512]{1,0:T(8,128)(2,1)}, u32[]{:S(2)}) copy-start(bf16[80,512]{1,0:T(8,128)(2,1)} %copy-done.6) | copy-start | bytes 245764
  33.9 28.4 %all-to-all-start.1 = ((bf16[32,2,3584]{2,1,0:T(2,128)(2,1)}), bf16[32,2,3584]{2,1,0:T(2,128)(2,1)S(1)}, u32[]{:S(2)}, u32[]{:S(2)}) async-start(bf16[32,2,3584]{2,1,0:T(2,128)(2,1)} %shard_map.133), calls=%async_computation.1 | async-start | bytes 917504 | tf_op jit(solution)/shard_map/all_to_all | solution.py:242
  45.7 16.7 %collective-permute-start.3 = (bf16[80,512]{1,0:T(8,128)(2,1)S(1)}, bf16[80,512]{1,0:T(8,128)(2,1)S(1)}, u32[]{:S(2)}, u32[]{:S(2)}) collective-permute-start(bf16[80,512]{1,0:T(8,128)(2,1)S(1)} %copy-done.9), channel_id=1, source_target_pairs={{0,448},{64,128},{128,64},{192,256},{256,192},{320,384},{384,320},... | collective-permute-start | bytes 245768 | tf_op jit(solution)/shard_map/ppermute | solution.py:186
  51.0 11.4 %collective-permute-start.4 = (bf16[80,512]{1,0:T(8,128)(2,1)S(1)}, bf16[80,512]{1,0:T(8,128)(2,1)S(1)}, u32[]{:S(2)}, u32[]{:S(2)}) collective-permute-start(bf16[80,512]{1,0:T(8,128)(2,1)S(1)} %copy-done.7), channel_id=1, source_target_pairs={{0,64},{64,0},{128,192},{192,128},{256,320},{320,256},{384,448},{4... | collective-permute-start | bytes 245768 | tf_op jit(solution)/shard_map/ppermute | solution.py:186
  62.8 4.7 %collective-permute-start.5 = (bf16[1,3584]{1,0:T(2,128)(2,1)S(1)}, bf16[1,3584]{1,0:T(2,128)(2,1)S(1)}, u32[]{:S(2)}, u32[]{:S(2)}) collective-permute-start(bf16[1,3584]{1,0:T(2,128)(2,1)S(1)} %get-tuple-element.36), channel_id=1, source_target_pairs={{0,64},{64,0},{128,192},{192,128},{256,320},{320,256},{384,448},{4... | collective-permute-start | bytes 21512 | tf_op jit(solution)/shard_map/ppermute | solution.py:186
  64.7 6.6 %collective-permute-start.6 = (bf16[1,3584]{1,0:T(2,128)(2,1)S(1)}, bf16[1,3584]{1,0:T(2,128)(2,1)S(1)}, u32[]{:S(2)}, u32[]{:S(2)}) collective-permute-start(bf16[1,3584]{1,0:T(2,128)(2,1)S(1)} %get-tuple-element.37), channel_id=1, source_target_pairs={{0,448},{64,128},{128,64},{192,256},{256,192},{320,384},{384,320},... | collective-permute-start | bytes 21512 | tf_op jit(solution)/shard_map/ppermute | solution.py:186
